TPU v7x, 512 devices: a whole 4x8x8 slice. The times are simulated.
512 devices in a mesh: ctx: 64 (over z, x, core), head: 8 (over y).
Axes of the slice: x: 4, y: 8, z: 8, core: 2. Of those that a mesh axis runs over, the one named last changes fastest.
Arguments:
- hidden: bfloat16 [65536, 2048], P('ctx'), may hold values from -16 to 16
- qkv_weight: bfloat16 [2048, 3072], P('ctx', 'head'), may hold values from -0.125 to 0.125
- out_grad: float32 [65536, 1024], P('ctx', 'head'), may hold values from -6 to 6
Outputs:
- attended: float32 [65536, 1024], P('ctx', 'head')
- weight_grad: float32 [2048, 3072], P('ctx', 'head')
All inputs are finite; a program needn't handle non-finite values.
Results may differ from a plain program's by a relative error of at most 0.0018.
Values may be sent and summed in bfloat16 or wider, within the bound.
No kernel may reach another device: no remote copies, remote signals or barrier semaphores. Data moves between devices by JAX's collectives and lax.ppermute only.
A program may use at most 64 MiB of HBM per device.

v0:
```python
import jax
import jax.numpy as jnp
from jax import lax
from jax.sharding import PartitionSpec as P

HD = 128
BLOCK = 128


HIGH = lax.Precision.HIGHEST


def prefix_2(part, axis, combine, identity, reverse):
    count = lax.axis_size(axis)
    place = lax.axis_index(axis)
    ahead = count - 1 - place if reverse else place
    gathered = lax.all_gather(part, axis)
    state = jnp.zeros_like(part) + jnp.asarray(identity, part.dtype)

    def one(step, state):
        source = count - 1 - step if reverse else step
        return combine(state, lax.dynamic_index_in_dim(gathered, source, 0, False))

    return lax.fori_loop(0, ahead, one, state)


def local(hidden, qkv_weight, out_grad):
    tokens = hidden.shape[0]
    columns = qkv_weight.shape[1]
    heads = columns // (3 * HD)
    total_tokens = tokens * lax.axis_size("ctx")
    scale = float(HD * total_tokens) ** (-0.5)
    grad_scale = float(total_tokens) ** (-0.5)
    inputs = hidden
    proj = jnp.dot(
        inputs,
        lax.all_gather(qkv_weight, "ctx", axis=0, tiled=True),
        preferred_element_type=jnp.float32,
    )
    count = tokens // BLOCK
    proj = proj.reshape(count, BLOCK, heads, 3, HD)
    query = proj[:, :, :, 0]
    keys = proj[:, :, :, 1]
    values = proj[:, :, :, 2]
    cotangent = out_grad.reshape(count, BLOCK, heads, HD)
    kv_block = jnp.einsum("nshd,nshe->nhde", keys, values, precision=HIGH)
    qg_block = jnp.einsum("nthd,nthe->nhde", query, cotangent, precision=HIGH)
    kv_total = jnp.sum(kv_block, axis=0)
    qg_total = jnp.sum(qg_block, axis=0)
    zeros_state = jnp.zeros_like(kv_total)
    before = prefix_2(kv_total, "ctx", lambda a, b: a + b, zeros_state, False)
    after = prefix_2(qg_total, "ctx", lambda a, b: a + b, zeros_state, True)
    prefix = before[None] + jnp.cumsum(kv_block, axis=0) - kv_block
    suffix = after[None] + qg_total[None] - jnp.cumsum(qg_block, axis=0)
    rows = jnp.arange(BLOCK)
    mask = (rows[:, None] >= rows[None, :]).astype(jnp.float32)
    scores = jnp.einsum("nthd,nshd->nhts", query, keys, precision=HIGH) * mask
    inner = jnp.einsum("nhts,nshe->nthe", scores, values, precision=HIGH)
    carried = jnp.einsum("nthd,nhde->nthe", query, prefix, precision=HIGH)
    attended = (scale * (inner + carried)).reshape(tokens, heads * HD)
    dmat = jnp.einsum("nthe,nshe->nhts", cotangent, values, precision=HIGH) * mask
    dquery = scale * (
        jnp.einsum("nhts,nshd->nthd", dmat, keys, precision=HIGH)
        + jnp.einsum("nthe,nhde->nthd", cotangent, prefix, precision=HIGH)
    )
    dkeys = scale * (
        jnp.einsum("nhts,nthd->nshd", dmat, query, precision=HIGH)
        + jnp.einsum("nshe,nhde->nshd", values, suffix, precision=HIGH)
    )
    dvalues = scale * (
        jnp.einsum("nhts,nthe->nshe", scores, cotangent, precision=HIGH)
        + jnp.einsum("nshd,nhde->nshe", keys, suffix, precision=HIGH)
    )
    dproj = (
        jnp.stack([dquery, dkeys, dvalues], axis=3).reshape(tokens, columns).astype(jnp.bfloat16)
    )
    inputs = hidden
    product = lax.dot_general(
        inputs, dproj, (((0,), (0,)), ((), ())), preferred_element_type=jnp.float32
    )
    weight_grad = lax.psum_scatter(product * grad_scale, "ctx", scatter_dimension=0, tiled=True)
    return (attended, weight_grad)


def solution(mesh):
    return jax.shard_map(
        local,
        mesh=mesh,
        in_specs=(P("ctx", None), P("ctx", "head"), P("ctx", "head")),
        out_specs=(P("ctx", "head"), P("ctx", "head")),
        check_vma=False,
    )
```

profile of v0, /device:TPU:1, one launch (start us, length us, event | category | flops | bytes accessed | tf_op | source)
XLA Modules:
  0.0 494.8 jit_solution(4324925228339906326)
XLA Ops:
  8.0 92.4 %all-gather.6.cloned.1.call-done = bf16[2048,384]{1,0:T(8,128)(2,1)} async-done(((bf16[32,384]{1,0:T(8,128)(2,1)}), bf16[2048,384]{1,0:T(8,128)(2,1)}) %all-gather.6.cloned.1.call-update) | async-done | bytes 1572880 | tf_op jit(solution)/shard_map/all_gather | solution.py:37
  100.3 4.5 convolution_bitcast_fusion
  105.8 1.6 fusion.33
  107.7 2.5 fusion.34
  110.3 1.2 fusion.5
  111.5 1.8 fusion.22
  113.4 1.4 fusion.15
  114.8 1.2 convolution_multiply_fusion
  116.0 1.8 convolution_bitcast_fusion.1
  117.8 72.2 %all-gather.8.cloned.1.call-done = f32[8192,128]{1,0:T(8,128)} async-done(((f32[128,128]{1,0:T(8,128)}), f32[8192,128]{1,0:T(8,128)}) %all-gather.8.cloned.1.call-update) | async-done | bytes 4194320 | tf_op jit(solution)/shard_map/all_gather | solution.py:17
  190.9 84.5 %all-gather.10.cloned.1.call-done = f32[8192,128]{1,0:T(8,128)} async-done(((f32[128,128]{1,0:T(8,128)}), f32[8192,128]{1,0:T(8,128)}) %all-gather.10.cloned.1.call-update) | async-done | bytes 4194320 | tf_op jit(solution)/shard_map/all_gather | solution.py:17
  275.3 54.7 %while.23 = (s32[]{:T(128)}, f32[1,128,128]{2,1,0:T(8,128)S(1)}, s32[]{:T(128)}, f32[64,1,128,128]{3,2,1,0:T(8,128)}, s32[]{:T(128)}, /*index=5*/s32[]{:T(128)}, s32[]{:T(128)}, s32[]{:T(128)}) while((s32[]{:T(128)}, f32[1,128,128]{2,1,0:T(8,128)S(1)}, s32[]{:T(128)}, f32[64,1,128,128]{3,2,1,0:T(8,128)}, s32[]{:T(128)}, /*index=5*/s32[]{:T(128)}, ...), condition=%wide.region_6.7_spmd, body=%wide.region_5.6_spmd.sunk | while | flops 16390 | bytes 196751 | solution.py:24
  276.2 0.9 bitcast_add_fusion.6
  277.1 0.9 bitcast_add_fusion.6
  278.0 0.9 bitcast_add_fusion.6
  278.8 0.9 bitcast_add_fusion.6
  287.6 0.9 bitcast_add_fusion.6
  290.3 0.9 bitcast_add_fusion.6
  304.3 0.9 bitcast_add_fusion.6
  307.0 0.9 bitcast_add_fusion.6
  321.1 0.9 bitcast_add_fusion.6
  323.7 0.9 bitcast_add_fusion.6
  330.1 1.2 reduce-window_subtract_fusion
  331.2 1.7 fusion.9
  332.9 1.2 fusion.10
  334.2 1.2 fusion.11
  335.4 1.0 pad_maximum_fusion
  336.4 2.4 copy.58
  338.8 5.9 %multiply_bitcast_fusion = f32[2048,384]{0,1:T(8,128)} fusion(bf16[1024,2048]{1,0:T(8,128)(2,1)} %param.7, bf16[48,8,8,128]{3,2,1,0:T(8,128)(2,1)} %bitcast.117), kind=kOutput, calls=%fused_computation.2 | convolution fusion | flops 1611399168 | bytes 8126464 | tf_op jit(solution)/shard_map/dot_general | solution.py:78
  344.7 3.6 copy.73
  348.9 1.4 fusion.4
  350.3 138.0 %reduce-scatter.4.cloned.1.call-done = f32[32,384]{1,0:T(8,128)} async-done(((f32[2048,384]{1,0:T(8,128)}), f32[32,384]{1,0:T(8,128)}) %reduce-scatter.4.cloned.1.call-update) | async-done | bytes 49168
  (81 shorter events, 49.0 us)
Async XLA Ops:
  7.2 100.6 %copy-start = (f32[1024,128]{1,0:T(8,128)S(1)}, f32[1024,128]{1,0:T(8,128)}, u32[]{:S(2)}) copy-start(f32[1024,128]{1,0:T(8,128)} %param.9) | copy-start | bytes 1572868
  7.2 93.2 %all-gather.6.cloned.1.call-start = ((), (), s32[]{:S(2)}) async-start(), calls=%async_computation.1 | async-start | bytes 1597440 | tf_op jit(solution)/shard_map/all_gather | solution.py:37
  7.9 182.1 %all-gather.8.cloned.1.call-start = ((), (), s32[]{:S(2)}) async-start(), calls=%async_computation.2 | async-start | bytes 4259840 | tf_op jit(solution)/shard_map/all_gather | solution.py:17
  107.4 167.9 %all-gather.10.cloned.1.call-start = ((), (), s32[]{:S(2)}) async-start(), calls=%async_computation.3 | async-start | bytes 4259840 | tf_op jit(solution)/shard_map/all_gather | solution.py:17
  110.2 378.0 %reduce-scatter.4.cloned.1.call-start = ((), (), s32[]{:S(2)}) async-start(), calls=%async_computation.4 | async-start | bytes 3194880
  114.8 215.3 %copy-start.3 = (f32[128,128]{1,0:T(8,128)S(1)}, f32[128,128]{1,0:T(8,128)}, u32[]{:S(2)}) copy-start(f32[128,128]{1,0:T(8,128)} %get-tuple-element.122) | copy-start | bytes 196612
  330.0 2.9 copy-start.2
  330.1 4.1 copy-start.1
Sparse Core Ops, SparseCore 0:
  11.4 88.9 all-gather.5
  107.6 82.3 all-gather.7
  193.3 81.9 all-gather.9
  348.4 139.8 reduce-scatter.3
where the time goes:
time: 502 us; the launch traced here: 495 us
  waiting for transfers between devices  388 us (77%)
  other arithmetic  56.2 us (11%)
  matrix products  28.1 us (6%)
  between operations  13.9 us (3%)
  local copies, waits for them, and re-layouts  7.09 us (1%)
    all_gather x2, waiting for transfers between devices, prefix_2(): gathered = lax.all_gather(part, axis)  157 us
    unnamed x5, waiting for transfers between devices  139 us
    all_gather x1, waiting for transfers between devices, local(): lax.all_gather(qkv_weight, 'ctx', axis=0, tiled=True)  92.4 us
    add x62, other arithmetic, local(): after = prefix_2(qg_total, 'ctx', lambda a, b: a + b, zeros_state, True)  53.1 us
  transfers between devices with their start and end apart: 4, of which 4 were waited for; matrix products, arithmetic and copies ran while one was open for 3% of the time, Pallas kernels for 0%

commit v1 on v0

v1 whole, which is shorter than its diff:
```python
import jax
import jax.numpy as jnp
from jax import lax
from jax.sharding import Mesh, PartitionSpec as P

HD = 128
BLOCK = 128
CORES = 2

HIGH = lax.Precision.HIGH
HIGHEST = lax.Precision.HIGHEST
SWAP = [(0, 1), (1, 0)]
CTX = ("chip", "core")


def gathered_weight(weight):
    chips = lax.axis_size("chip")
    core = lax.axis_index("core")
    spread = jnp.broadcast_to(weight[None], (chips,) + weight.shape)
    mine = lax.all_to_all(spread, "chip", 0, 0, tiled=True)
    other = lax.ppermute(mine, "core", SWAP)
    first = jnp.where(core == 0, mine, other)
    second = jnp.where(core == 0, other, mine)
    whole = jnp.stack([first, second], axis=1)
    return whole.reshape(-1, weight.shape[1])


def exchanged_states(kv_total, qg_total):
    chips = lax.axis_size("chip")
    devices = chips * CORES
    core = lax.axis_index("core")
    rows = HD // chips
    parts = jnp.stack(
        [kv_total.reshape(chips, rows, HD), qg_total.reshape(chips, rows, HD)], axis=1
    ).reshape(devices, rows, HD)
    pieces = lax.all_to_all(parts, CTX, 0, 0, tiled=True)
    place = jnp.arange(devices)
    earlier = place[:, None] > place[None, :]
    chosen = jnp.where(core == 0, earlier, earlier.T).astype(jnp.float32)
    sums = jnp.dot(chosen, pieces.reshape(devices, rows * HD), precision=HIGHEST)
    back = lax.all_to_all(sums.reshape(devices, rows, HD), CTX, 0, 0, tiled=True)
    back = back.reshape(chips, CORES, rows, HD)
    return back[:, 0].reshape(HD, HD), back[:, 1].reshape(HD, HD)


def summed_gradient(product):
    chips = lax.axis_size("chip")
    core = lax.axis_index("core")
    rows = product.shape[0] // (chips * CORES)
    halves = product.reshape(chips, CORES, rows, product.shape[1])
    keep = jnp.where(core == 0, halves[:, 0], halves[:, 1])
    give = jnp.where(core == 0, halves[:, 1], halves[:, 0])
    total = keep + lax.ppermute(give, "core", SWAP)
    landed = lax.all_to_all(total.astype(jnp.bfloat16), "chip", 0, 0, tiled=True)
    return jnp.sum(landed.astype(jnp.float32), axis=0)


def local(hidden, qkv_weight, out_grad):
    tokens = hidden.shape[0]
    columns = qkv_weight.shape[1]
    total_tokens = tokens * lax.axis_size("chip") * CORES
    scale = float(HD * total_tokens) ** (-0.5)
    grad_scale = float(total_tokens) ** (-0.5)
    proj = jnp.dot(hidden, gathered_weight(qkv_weight), preferred_element_type=jnp.float32)
    count = tokens // BLOCK
    blocks = proj.reshape(count, BLOCK, 3, HD)
    query, keys, values = blocks[:, :, 0], blocks[:, :, 1], blocks[:, :, 2]
    cotangent = out_grad.reshape(count, BLOCK, HD)
    kv_block = jnp.einsum("nsd,nse->nde", keys, values, precision=HIGH)
    qg_block = jnp.einsum("ntd,nte->nde", query, cotangent, precision=HIGH)
    kv_total = jnp.sum(kv_block, axis=0)
    qg_total = jnp.sum(qg_block, axis=0)
    before, after = exchanged_states(kv_total, qg_total)
    prefix = before[None] + jnp.cumsum(kv_block, axis=0) - kv_block
    suffix = after[None] + qg_total[None] - jnp.cumsum(qg_block, axis=0)
    rows = jnp.arange(BLOCK)
    mask = (rows[:, None] >= rows[None, :]).astype(jnp.float32)
    scores = jnp.einsum("ntd,nsd->nts", query, keys, precision=HIGH) * mask
    inner = jnp.einsum("nts,nse->nte", scores, values, precision=HIGH)
    carried = jnp.einsum("ntd,nde->nte", query, prefix, precision=HIGH)
    attended = (scale * (inner + carried)).reshape(tokens, HD)
    dmat = jnp.einsum("nte,nse->nts", cotangent, values, precision=HIGH) * mask
    dquery = scale * (
        jnp.einsum("nts,nsd->ntd", dmat, keys, precision=HIGH)
        + jnp.einsum("nte,nde->ntd", cotangent, prefix, precision=HIGH)
    )
    dkeys = scale * (
        jnp.einsum("nts,ntd->nsd", dmat, query, precision=HIGH)
        + jnp.einsum("nse,nde->nsd", values, suffix, precision=HIGH)
    )
    dvalues = scale * (
        jnp.einsum("nts,nte->nse", scores, cotangent, precision=HIGH)
        + jnp.einsum("nsd,nde->nse", keys, suffix, precision=HIGH)
    )
    dproj = jnp.concatenate([dquery, dkeys, dvalues], axis=2).reshape(tokens, columns)
    product = lax.dot_general(
        hidden,
        dproj.astype(jnp.bfloat16),
        (((0,), (0,)), ((), ())),
        preferred_element_type=jnp.float32,
    )
    return attended, summed_gradient(product) * grad_scale


def solution(mesh):
    chips, heads = mesh.shape["ctx"] // CORES, mesh.shape["head"]
    fine = Mesh(mesh.devices.reshape(chips, CORES, heads), ("chip", "core", "head"))
    return jax.shard_map(
        local,
        mesh=fine,
        in_specs=(P(CTX, None), P(CTX, "head"), P(CTX, "head")),
        out_specs=(P(CTX, "head"), P(CTX, "head")),
        check_vma=False,
    )
```

time: 502 us -> 137 us (0.27); the launches traced: 495 us -> 135 us
  waiting for transfers between devices: 388 us -> 44.6 us
  other arithmetic: 56.2 us -> 6.03 us
  blocking collectives: 0 us -> 34.6 us
  starting transfers between devices: 0.16 us -> 21.1 us
  between operations: 13.9 us -> 0.95 us
  matrix products: 28.1 us -> 16 us
    all_gather x3 -> x0, waiting for transfers between devices: 249 us -> none  [the longest x2 157 us: prefix_2(): gathered = lax.all_gather(part, axis)]
    unnamed x5 -> x0, waiting for transfers between devices: 139 us -> none
    add x63 -> x0, other arithmetic: 54 us -> none  [the longest x62 53.1 us: local(): after = prefix_2(qg_total, 'ctx', lambda a, b: a + b, zeros_state, True)]
    all_to_all x0 -> x3, waiting for transfers between devices: none -> 39.7 us  [the longest x1 20 us: summed_gradient(): lax.all_to_all(total.astype(jnp.bfloat16), 'chip', 0, 0, tiled=True)]
    all_to_all x0 -> x1, blocking collectives: none -> 34.6 us  [gathered_weight(): mine = lax.all_to_all(spread, 'chip', 0, 0, tiled=True)]
    all_to_all x0 -> x3, starting transfers between devices: none -> 14.1 us  [the longest x1 5.62 us: exchanged_states(): pieces = lax.all_to_all(parts, CTX, 0, 0, tiled=True)]
    dot_general x14 -> x15, matrix products: 28.1 us -> 16 us  [the longest x1 3.51 us: local(): lax.dot_general(hidden, dproj.astype(jnp.bfloat16), (((0,), (0,)), ((), (...]
    ppermute x0 -> x2, starting transfers between devices: none -> 7.02 us  [the longest x1 4.72 us: gathered_weight(): other = lax.ppermute(mine, 'core', SWAP)]
  transfers between devices with their start and end apart: 4 -> 5, of which waited for: 4 -> 5; matrix products, arithmetic and copies ran while one was open for 3% -> 3% of each run, Pallas kernels for 0% -> 0%
where the time goes in v1:
time: 137 us; the launch traced here: 135 us
  waiting for transfers between devices  44.6 us (33%)
  blocking collectives  34.6 us (25%)
  starting transfers between devices  21.1 us (15%)
  matrix products  16 us (12%)
  local copies, waits for them, and re-layouts  12 us (9%)
  other arithmetic  6.03 us (4%)
    all_to_all x1, blocking collectives, gathered_weight(): mine = lax.all_to_all(spread, 'chip', 0, 0, tiled=True)  34.6 us
    all_to_all x1, waiting for transfers between devices, summed_gradient(): lax.all_to_all(total.astype(jnp.bfloat16), 'chip', 0, 0, tiled=True)  20 us
    all_to_all x1, waiting for transfers between devices, exchanged_states(): lax.all_to_all(sums.reshape(devices, rows, HD), CTX, 0, 0, tiled=True)  9.93 us
    all_to_all x1, waiting for transfers between devices, exchanged_states(): pieces = lax.all_to_all(parts, CTX, 0, 0, tiled=True)  9.73 us
    all_to_all x1, starting transfers between devices, exchanged_states(): pieces = lax.all_to_all(parts, CTX, 0, 0, tiled=True)  5.62 us
    unnamed x22, local copies, waits for them, and re-layouts  5.11 us
    ppermute x1, starting transfers between devices, gathered_weight(): other = lax.ppermute(mine, 'core', SWAP)  4.72 us
    all_to_all x1, starting transfers between devices, exchanged_states(): lax.all_to_all(sums.reshape(devices, rows, HD), CTX, 0, 0, tiled=True)  4.44 us
  transfers between devices with their start and end apart: 5, of which 5 were waited for; matrix products, arithmetic and copies ran while one was open for 3% of the time, Pallas kernels for 0%

profile of v1, /device:TPU:1, one launch (start us, length us, event | category | flops | bytes accessed | tf_op | source)
XLA Modules:
  0.0 135.3 jit_solution(14593105799894132449)
XLA Ops:
  0.6 0.9 broadcast_in_dim.2
  1.5 34.6 %all_to_all.20 = bf16[32,32,384]{2,1,0:T(8,128)(2,1)S(1)} all-to-all(bf16[32,32,384]{2,1,0:T(8,128)(2,1)S(1)} %broadcast_in_dim.2), channel_id=1, replica_groups=mesh['chip'=32,'core'=2,'head'=8] {'chip'}, dimensions={0} | all-to-all | bytes 1572864 | tf_op jit(solution)/shard_map/all_to_all | solution.py:20
  36.1 4.7 %collective-permute-start = (bf16[32,32,384]{2,1,0:T(8,128)(2,1)S(1)}, bf16[32,32,384]{2,1,0:T(8,128)(2,1)S(1)}, u32[]{:S(2)}, u32[]{:S(2)}) collective-permute-start(bf16[32,32,384]{2,1,0:T(8,128)(2,1)S(1)} %all_to_all.20), channel_id=1, source_target_pairs={{0,8},{8,0},{1,9},{9,1},{2,10},{10,2},{3,11},{11,3},{4,12},{12,4},... | collective-permute-start | bytes 2359304 | tf_op jit(solution)/shard_map/ppermute | solution.py:21
  40.8 1.9 %collective-permute-done = bf16[32,32,384]{2,1,0:T(8,128)(2,1)S(1)} collective-permute-done((bf16[32,32,384]{2,1,0:T(8,128)(2,1)S(1)}, bf16[32,32,384]{2,1,0:T(8,128)(2,1)S(1)}, u32[]{:S(2)}, u32[]{:S(2)}) %collective-permute-start) | collective-permute-done | bytes 786464 | tf_op jit(solution)/shard_map/ppermute | solution.py:21
  43.0 1.9 %copy-done.2 = bf16[1024,2048]{1,0:T(8,128)(2,1)S(1)} copy-done((bf16[1024,2048]{1,0:T(8,128)(2,1)S(1)}, bf16[1024,2048]{1,0:T(8,128)(2,1)}, u32[]{:S(2)}) %copy-start.2) | copy-done | bytes 4194328
  44.9 1.8 %convolution_bitcast_fusion.1 = f32[48,8,8,128]{3,1,2,0:T(8,128)S(1)} fusion(bf16[2048,384]{1,0:T(8,128)(2,1)S(1)} %bitcast.131, bf16[1024,2048]{1,0:T(8,128)(2,1)S(1)} %copy-done.2), kind=kOutput, calls=%fused_computation.8 | convolution fusion | flops 1610612736 | bytes 7340032 | tf_op jit(solution)/shard_map/dot_general | solution.py:64
  47.1 0.9 fusion.36
  48.2 1.2 copy.120
  49.7 1.4 %fusion.38 = (f32[128,128]{1,0:T(8,128)S(1)}, f32[8,128,128]{2,1,0:T(8,128)}) fusion(f32[8,128,128]{2,1,0:T(8,128)S(1)} %bitcast.123, f32[8,128,1,128]{3,1,0,2:T(8,128)S(1)} %copy.119), kind=kOutput, calls=%fused_computation.61 | convolution fusion | flops 100777984 | bytes 1638400 | tf_op jit(solution)/shard_map/ntd,nte->nde/dot_general | solution.py:70
  51.8 0.7 fusion.8
  52.4 1.4 %fusion.39 = (f32[128,128]{1,0:T(8,128)S(1)}, f32[8,128,128]{2,1,0:T(8,128)}) fusion(f32[8,128,1,128]{3,1,0,2:T(8,128)S(1)} %copy.121, f32[8,128,1,128]{3,1,0,2:T(8,128)S(1)} %copy.120), kind=kOutput, calls=%fused_computation.62 | convolution fusion | flops 100777984 | bytes 1638400 | tf_op jit(solution)/shard_map/nsd,nse->nde/dot_general | solution.py:69
  54.0 0.7 copy.86
  54.7 5.6 %all-to-all-start.1 = ((f32[64,4,128]{2,1,0:T(4,128)}), f32[64,4,128]{2,1,0:T(4,128)S(1)}, u32[]{:S(2)}, u32[]{:S(2)}) async-start(f32[64,4,128]{2,1,0:T(4,128)} %copy.86), calls=%async_computation.1 | async-start | bytes 262144 | tf_op jit(solution)/shard_map/all_to_all | solution.py:36
  60.3 1.4 %fusion.22 = f32[8,128,128]{2,1,0:T(8,128)} fusion(f32[8,128,128]{2,1,0:T(8,128)S(1)} %fusion.8, f32[8,128,1,128]{3,1,0,2:T(8,128)S(1)} %copy.119), kind=kOutput, calls=%fused_computation.40 | convolution fusion | flops 100663296 | bytes 1572864 | tf_op jit(solution)/shard_map/nts,ntd->nsd/dot_general | solution.py:88
  61.7 9.7 %all-to-all-done.1 = f32[64,4,128]{2,1,0:T(4,128)S(1)} async-done(((f32[64,4,128]{2,1,0:T(4,128)}), f32[64,4,128]{2,1,0:T(4,128)S(1)}, u32[]{:S(2)}, u32[]{:S(2)}) %all-to-all-start.1) | async-done | bytes 131104 | tf_op jit(solution)/shard_map/all_to_all | solution.py:36
  71.7 0.7 copy.88
  72.4 4.4 %all-to-all-start.2 = ((f32[64,4,128]{2,1,0:T(4,128)}), f32[64,4,128]{2,1,0:T(4,128)S(1)}, u32[]{:S(2)}, u32[]{:S(2)}) async-start(f32[64,4,128]{2,1,0:T(4,128)} %copy.88), calls=%async_computation.2 | async-start | bytes 262144 | tf_op jit(solution)/shard_map/all_to_all | solution.py:41
  76.9 1.4 %fusion.40 = f32[8,128,128]{2,1,0:T(8,128)} fusion(f32[8,128,128]{2,1,0:T(8,128)S(1)} %convolution_multiply_fusion, f32[8,128,128]{2,1,0:T(8,128)S(1)} %bitcast.126), kind=kOutput, calls=%fused_computation.63 | convolution fusion | flops 100663296 | bytes 1572864 | tf_op jit(solution)/shard_map/nts,nte->nse/dot_general | solution.py:92
  78.3 9.9 %all-to-all-done.2 = f32[64,4,128]{2,1,0:T(4,128)S(1)} async-done(((f32[64,4,128]{2,1,0:T(4,128)}), f32[64,4,128]{2,1,0:T(4,128)S(1)}, u32[]{:S(2)}, u32[]{:S(2)}) %all-to-all-start.2) | async-done | bytes 131104 | tf_op jit(solution)/shard_map/all_to_all | solution.py:41
  88.2 1.2 reduce-window_subtract_fusion
  89.4 0.7 fusion.10
  90.6 0.7 convolution_bitcast_fusion.2
  91.8 1.2 copy-done.3
  93.0 3.5 %convolution_bitcast_fusion = f32[2048,384]{0,1:T(8,128)} fusion(bf16[1024,384]{1,0:T(8,128)(2,1)S(1)} %bitcast.130, bf16[1024,2048]{1,0:T(8,128)(2,1)S(1)} %copy-done.3), kind=kOutput, calls=%fused_computation | convolution fusion | flops 1610612736 | bytes 8126464 | tf_op jit(solution)/shard_map/dot_general | solution.py:96
  96.5 3.6 %copy.101 = f32[2048,384]{1,0:T(8,128)} copy(f32[2048,384]{0,1:T(8,128)} %convolution_bitcast_fusion) | data formatting | bytes 6291456 | tf_op jit(solution)/shard_map/dot_general | solution.py:96
  100.0 2.3 %select_bitcast_fusion = f32[32,32,384]{2,1,0:T(8,128)S(1)} fusion(f32[32,2,32,384]{3,2,1,0:T(8,128)} %bitcast.127, pred[]{:T(512)S(6)} %eq.2), kind=kLoop, calls=%fused_computation.7 | loop fusion | flops 393216 | bytes 4718593 | tf_op jit(solution)/shard_map/jit(_where)/select_n | solution.py:52
  102.3 2.3 %collective-permute-start.1 = (f32[32,32,384]{2,1,0:T(8,128)S(1)}, f32[32,32,384]{2,1,0:T(8,128)S(1)}, u32[]{:S(2)}, u32[]{:S(2)}) collective-permute-start(f32[32,32,384]{2,1,0:T(8,128)S(1)} %select_bitcast_fusion), channel_id=1, source_target_pairs={{0,8},{8,0},{1,9},{9,1},{2,10},{10,2},{3,11},{11,3},{4,12},{12,4},... | collective-permute-start | bytes 4718600 | tf_op jit(solution)/shard_map/ppermute | solution.py:53
  104.6 3.0 %collective-permute-done.1 = f32[32,32,384]{2,1,0:T(8,128)S(1)} collective-permute-done((f32[32,32,384]{2,1,0:T(8,128)S(1)}, f32[32,32,384]{2,1,0:T(8,128)S(1)}, u32[]{:S(2)}, u32[]{:S(2)}) %collective-permute-start.1) | collective-permute-done | bytes 1572896 | tf_op jit(solution)/shard_map/ppermute | solution.py:53
  107.6 1.3 fusion.2
  109.0 4.0 %all-to-all-start.3 = ((bf16[32,32,384]{2,1,0:T(8,128)(2,1)}), bf16[32,32,384]{2,1,0:T(8,128)(2,1)S(1)}, u32[]{:S(2)}, u32[]{:S(2)}) async-start(bf16[32,32,384]{2,1,0:T(8,128)(2,1)} %fusion.2), calls=%async_computation.3 | async-start | bytes 1572864 | tf_op jit(solution)/shard_map/all_to_all | solution.py:54
  113.4 1.2 fusion.7
  114.6 20.0 %all-to-all-done.3 = bf16[32,32,384]{2,1,0:T(8,128)(2,1)S(1)} async-done(((bf16[32,32,384]{2,1,0:T(8,128)(2,1)}), bf16[32,32,384]{2,1,0:T(8,128)(2,1)S(1)}, u32[]{:S(2)}, u32[]{:S(2)}) %all-to-all-start.3) | async-done | bytes 786464 | tf_op jit(solution)/shard_map/all_to_all | solution.py:54
  (35 shorter events, 4.2 us)
Async XLA Ops:
  0.6 49.1 %copy-start = (f32[1024,128]{1,0:T(8,128)S(1)}, f32[1024,128]{1,0:T(8,128)}, u32[]{:S(2)}) copy-start(f32[1024,128]{1,0:T(8,128)} %param.5) | copy-start | bytes 1572868
  36.1 6.6 %collective-permute-start = (bf16[32,32,384]{2,1,0:T(8,128)(2,1)S(1)}, bf16[32,32,384]{2,1,0:T(8,128)(2,1)S(1)}, u32[]{:S(2)}, u32[]{:S(2)}) collective-permute-start(bf16[32,32,384]{2,1,0:T(8,128)(2,1)S(1)} %all_to_all.20), channel_id=1, source_target_pairs={{0,8},{8,0},{1,9},{9,1},{2,10},{10,2},{3,11},{11,3},{4,12},{12,4},... | collective-permute-start | bytes 2359304 | tf_op jit(solution)/shard_map/ppermute | solution.py:21
  42.7 2.2 %copy-start.2 = (bf16[1024,2048]{1,0:T(8,128)(2,1)S(1)}, bf16[1024,2048]{1,0:T(8,128)(2,1)}, u32[]{:S(2)}) copy-start(bf16[1024,2048]{1,0:T(8,128)(2,1)} %param.3) | copy-start | bytes 12582916
  54.7 16.7 %all-to-all-start.1 = ((f32[64,4,128]{2,1,0:T(4,128)}), f32[64,4,128]{2,1,0:T(4,128)S(1)}, u32[]{:S(2)}, u32[]{:S(2)}) async-start(f32[64,4,128]{2,1,0:T(4,128)} %copy.86), calls=%async_computation.1 | async-start | bytes 262144 | tf_op jit(solution)/shard_map/all_to_all | solution.py:36
  72.4 15.8 %all-to-all-start.2 = ((f32[64,4,128]{2,1,0:T(4,128)}), f32[64,4,128]{2,1,0:T(4,128)S(1)}, u32[]{:S(2)}, u32[]{:S(2)}) async-start(f32[64,4,128]{2,1,0:T(4,128)} %copy.88), calls=%async_computation.2 | async-start | bytes 262144 | tf_op jit(solution)/shard_map/all_to_all | solution.py:41
  88.2 1.2 copy-start.7
  88.2 1.9 %copy-start.8 = (f32[8,128,128]{2,1,0:T(8,128)S(1)}, f32[8,128,128]{2,1,0:T(8,128)}, u32[]{:S(2)}) copy-start(f32[8,128,128]{2,1,0:T(8,128)} %fusion.40) | copy-start | bytes 1572868
  89.4 1.1 copy-start.4
  90.6 1.1 copy-start.5
  90.6 2.4 %copy-start.3 = (bf16[1024,2048]{1,0:T(8,128)(2,1)S(1)}, bf16[1024,2048]{1,0:T(8,128)(2,1)}, u32[]{:S(2)}) copy-start(bf16[1024,2048]{1,0:T(8,128)(2,1)} %param.3) | copy-start | bytes 12582916
  100.0 7.6 %copy-start.1 = (f32[2048,384]{1,0:T(8,128)S(1)}, f32[2048,384]{1,0:T(8,128)}, u32[]{:S(2)}) copy-start(f32[2048,384]{1,0:T(8,128)} %copy.101) | copy-start | bytes 9437188
  102.3 5.3 %collective-permute-start.1 = (f32[32,32,384]{2,1,0:T(8,128)S(1)}, f32[32,32,384]{2,1,0:T(8,128)S(1)}, u32[]{:S(2)}, u32[]{:S(2)}) collective-permute-start(f32[32,32,384]{2,1,0:T(8,128)S(1)} %select_bitcast_fusion), channel_id=1, source_target_pairs={{0,8},{8,0},{1,9},{9,1},{2,10},{10,2},{3,11},{11,3},{4,12},{12,4},... | collective-permute-start | bytes 4718600 | tf_op jit(solution)/shard_map/ppermute | solution.py:53
  109.0 4.4 %copy-start.6 = (f32[8,128,128]{2,1,0:T(8,128)S(1)}, f32[8,128,128]{2,1,0:T(8,128)}, u32[]{:S(2)}) copy-start(f32[8,128,128]{2,1,0:T(8,128)} %copy-done.5) | copy-start | bytes 1572868
  109.0 25.6 %all-to-all-start.3 = ((bf16[32,32,384]{2,1,0:T(8,128)(2,1)}), bf16[32,32,384]{2,1,0:T(8,128)(2,1)S(1)}, u32[]{:S(2)}, u32[]{:S(2)}) async-start(bf16[32,32,384]{2,1,0:T(8,128)(2,1)} %fusion.2), calls=%async_computation.3 | async-start | bytes 1572864 | tf_op jit(solution)/shard_map/all_to_all | solution.py:54

commit v2 on v0

v2 whole, which is shorter than its diff:
```python
import functools

import jax
import jax.numpy as jnp
from jax import lax
from jax.experimental import pallas as pl
from jax.experimental.pallas import tpu as pltpu
from jax.sharding import Mesh, PartitionSpec as P

HD = 128
BLOCK = 256
CORES = 2
MIB = 1 << 20

SWAP = [(0, 1), (1, 0)]
CTX = ("chip", "core")
F32 = jnp.float32
BF16 = jnp.bfloat16

PLAIN = (((1,), (0,)), ((), ()))
ROWS = (((1,), (1,)), ((), ()))
COLS = (((0,), (0,)), ((), ()))


def mxu(a, b, dims=PLAIN):
    return lax.dot_general(a, b, dims, preferred_element_type=F32)


def split(x):
    high = x.astype(BF16)
    return high, (x - high.astype(F32)).astype(BF16)


def mxu3(a, b, dims=PLAIN):
    return mxu(a[0], b[0], dims) + (mxu(a[0], b[1], dims) + mxu(a[1], b[0], dims))


def call(body, outs, args, flops, vmem, scratch=(), scalars=0):
    specs = [pl.BlockSpec(memory_space=pltpu.SMEM)] * scalars + [
        pl.BlockSpec(memory_space=pltpu.VMEM)
    ] * (len(args) - scalars)
    size = sum(a.size * a.dtype.itemsize for a in (*args, *outs))
    return pl.pallas_call(
        body,
        out_shape=list(outs),
        in_specs=specs,
        out_specs=[pl.BlockSpec(memory_space=pltpu.VMEM)] * len(outs),
        scratch_shapes=list(scratch),
        cost_estimate=pl.CostEstimate(flops=flops, bytes_accessed=size, transcendentals=0),
        compiler_params=pltpu.CompilerParams(vmem_limit_bytes=vmem * MIB),
    )(*args)


def turn_kernel(core, hidden, keep, give):
    first = core[0] == 0
    group = keep.shape[1]
    for column in range(hidden.shape[1] // HD):
        turned = hidden[:, column * HD : (column + 1) * HD].T
        for pair in range(HD // (CORES * group)):
            at = pair * CORES * group
            even = turned[at : at + group]
            odd = turned[at + group : at + CORES * group]
            chip = column * (HD // (CORES * group)) + pair
            keep[chip] = jnp.where(first, even, odd)
            give[chip] = jnp.where(first, odd, even)


def project_kernel(core, hidden, mine, other, cotangent, proj, parts, weight):
    place = core[0]
    chips, group, columns = mine.shape
    for chip in range(chips):
        weight[2 * chip + place] = mine[chip]
        weight[2 * chip + 1 - place] = other[chip]
    whole = weight[...].reshape(chips * CORES * group, columns)
    kv = jnp.zeros((HD, HD), F32)
    qg = jnp.zeros((HD, HD), F32)
    for start in range(0, hidden.shape[0], BLOCK):
        rows = slice(start, start + BLOCK)
        part = mxu(hidden[rows, :], whole)
        proj[rows, :] = part
        query, keys, values = (split(part[:, j * HD : (j + 1) * HD]) for j in range(3))
        kv += mxu3(keys, values, COLS)
        qg += mxu3(query, split(cotangent[rows, :]), COLS)
    piece = HD // chips
    for chip in range(chips):
        parts[2 * chip] = kv[chip * piece : (chip + 1) * piece]
        parts[2 * chip + 1] = qg[chip * piece : (chip + 1) * piece]


def causal():
    at = lax.broadcasted_iota(jnp.int32, (BLOCK, BLOCK), 0)
    return at >= lax.broadcasted_iota(jnp.int32, (BLOCK, BLOCK), 1)


def local_kernel(proj, cotangent, dlocal):
    tokens = proj.shape[0]
    mask = causal()
    state = jnp.zeros((HD, HD), F32)
    for start in range(0, tokens, BLOCK):
        rows = slice(start, start + BLOCK)
        query, keys, values = (split(proj[rows, j * HD : (j + 1) * HD]) for j in range(3))
        cot = split(cotangent[rows, :])
        scores = split(jnp.where(mask, mxu3(query, keys, ROWS), 0.0))
        dmat = split(jnp.where(mask, mxu3(cot, values, ROWS), 0.0))
        dquery = mxu3(dmat, keys)
        if start:
            dquery += mxu3(cot, split(state), ROWS)
        dlocal[rows, 0:HD] = dquery
        dlocal[rows, HD : 2 * HD] = mxu3(dmat, query, COLS)
        dlocal[rows, 2 * HD : 3 * HD] = mxu3(scores, cot, COLS)
        if start + BLOCK < tokens:
            state += mxu3(keys, values, COLS)
    state = jnp.zeros((HD, HD), F32)
    for start in range(tokens - 2 * BLOCK, -1, -BLOCK):
        later = slice(start + BLOCK, start + 2 * BLOCK)
        rows = slice(start, start + BLOCK)
        state += mxu3(split(proj[later, 0:HD]), split(cotangent[later, :]), COLS)
        suffix = split(state)
        keys, values = split(proj[rows, HD : 2 * HD]), split(proj[rows, 2 * HD : 3 * HD])
        dlocal[rows, HD : 2 * HD] += mxu3(values, suffix, ROWS)
        dlocal[rows, 2 * HD : 3 * HD] += mxu3(keys, suffix)


def scan_kernel(core, pieces, sums):
    devices = pieces.shape[0]
    flip = core[0] == 1
    total = jnp.zeros(pieces.shape[1:], F32)
    for step in range(devices):
        source = jnp.where(flip, devices - 1 - step, step)
        sums[source] = total
        total += pieces[source]


def joined(back, states, which):
    chips, piece = back.shape[0] // CORES, back.shape[1]
    for chip in range(chips):
        states[which, chip * piece : (chip + 1) * piece, :] = back[CORES * chip + which]


def dproj_kernel(scale, back, proj, cotangent, dlocal, dproj, states):
    joined(back, states, 0)
    joined(back, states, 1)
    prefix, suffix = split(states[0]), split(states[1])
    for start in range(0, proj.shape[0], BLOCK):
        rows = slice(start, start + BLOCK)
        keys, values = split(proj[rows, HD : 2 * HD]), split(proj[rows, 2 * HD : 3 * HD])
        cot = split(cotangent[rows, :])
        for j, term in enumerate(
            (
                mxu3(cot, prefix, ROWS),
                mxu3(values, suffix, ROWS),
                mxu3(keys, suffix),
            )
        ):
            columns = slice(j * HD, (j + 1) * HD)
            dproj[rows, columns] = (scale * (dlocal[rows, columns] + term)).astype(BF16)


def attended_kernel(scale, back, proj, attended, states):
    joined(back, states, 0)
    state = states[0]
    mask = causal()
    for start in range(0, proj.shape[0], BLOCK):
        rows = slice(start, start + BLOCK)
        query, keys, values = (split(proj[rows, j * HD : (j + 1) * HD]) for j in range(3))
        scores = split(jnp.where(mask, mxu3(query, keys, ROWS), 0.0))
        attended[rows, :] = scale * (mxu3(scores, values) + mxu3(query, split(state)))
        state += mxu3(keys, values, COLS)


def own_kernel(turned, dproj, product):
    for start in range(0, turned.shape[0], BLOCK):
        rows = slice(start, start + BLOCK)
        product[rows, :] = mxu(turned[rows, :], dproj[...])


def total_kernel(turned, dproj, product, total):
    for start in range(0, turned.shape[0], BLOCK):
        rows = slice(start, start + BLOCK)
        total[rows, :] = (product[rows, :] + mxu(turned[rows, :], dproj[...])).astype(BF16)


def shape(dims, dtype=F32):
    return jax.ShapeDtypeStruct(dims, dtype)


def local(hidden, qkv_weight, out_grad):
    tokens, width = hidden.shape
    group, columns = qkv_weight.shape
    chips = lax.axis_size("chip")
    devices = chips * CORES
    piece = HD // chips
    total_tokens = tokens * devices
    scale = float(HD * total_tokens) ** (-0.5)
    grad_scale = float(total_tokens) ** (-0.5)
    core = lax.axis_index("core").astype(jnp.int32).reshape(1)
    half = width // CORES

    spread = jnp.broadcast_to(qkv_weight[None], (chips, group, columns))
    mine = lax.all_to_all(spread, "chip", 0, 0, tiled=True)
    keep, give = call(
        turn_kernel,
        [shape((chips, group, tokens), BF16)] * 2,
        [core, hidden],
        tokens * width * 1024,
        24,
        scalars=1,
    )
    mine, keep, give = lax.optimization_barrier((mine, keep, give))
    keep, give = keep.reshape(half, tokens), give.reshape(half, tokens)
    taken = lax.ppermute(give, "core", SWAP)
    other = lax.ppermute(mine, "core", SWAP)

    proj, parts = call(
        project_kernel,
        [shape((tokens, columns)), shape((devices, piece, HD))],
        [core, hidden, mine, other, out_grad],
        2 * tokens * width * columns + 12 * tokens * HD * HD,
        32,
        [pltpu.VMEM((devices, group, columns), BF16)],
        scalars=1,
    )
    pieces = lax.all_to_all(parts, CTX, 0, 0, tiled=True)
    (dlocal,) = call(
        local_kernel,
        [shape((tokens, columns))],
        [proj, out_grad],
        15 * 6 * tokens * HD * HD,
        24,
    )
    pieces, dlocal = lax.optimization_barrier((pieces, dlocal))
    (sums,) = call(
        scan_kernel, [shape(parts.shape)], [core, pieces], devices * HD * HD, 8, scalars=1
    )
    back = lax.all_to_all(sums, CTX, 0, 0, tiled=True)

    states = [pltpu.VMEM((2, HD, HD), F32)]
    (dproj,) = call(
        functools.partial(dproj_kernel, scale),
        [shape((tokens, columns), BF16)],
        [back, proj, out_grad, dlocal],
        18 * tokens * HD * HD,
        24,
        states,
    )
    theirs = lax.ppermute(dproj, "core", SWAP)
    (product,) = call(
        own_kernel,
        [shape((half, columns))],
        [keep, dproj],
        2 * half * tokens * columns,
        24,
    )
    (total,) = call(
        total_kernel,
        [shape((half, columns), BF16)],
        [taken, theirs, product],
        2 * half * tokens * columns,
        24,
    )
    landed = lax.all_to_all(total.reshape(chips, group, columns), "chip", 0, 0, tiled=True)
    (attended,) = call(
        functools.partial(attended_kernel, scale),
        [shape((tokens, HD))],
        [back, proj],
        6 * 6 * tokens * HD * HD,
        24,
        states,
    )
    return attended, jnp.sum(landed.astype(F32), axis=0) * grad_scale


def solution(mesh):
    chips, heads = mesh.shape["ctx"] // CORES, mesh.shape["head"]
    fine = Mesh(mesh.devices.reshape(chips, CORES, heads), ("chip", "core", "head"))
    return jax.shard_map(
        local,
        mesh=fine,
        in_specs=(P(CTX, None), P(CTX, "head"), P(CTX, "head")),
        out_specs=(P(CTX, "head"), P(CTX, "head")),
        check_vma=False,
    )
```

time: 502 us -> 124 us (0.25); the launches traced: 495 us -> 123 us
  waiting for transfers between devices: 388 us -> 40.4 us
  other arithmetic: 56.2 us -> 0.74 us
  starting transfers between devices: 0.16 us -> 32.5 us
  matrix products: 28.1 us -> 0 us
  Pallas kernels: 0 us -> 17.9 us
  blocking collectives: 0 us -> 16.4 us
  between operations: 13.9 us -> 0.8 us
  local copies, waits for them, and re-layouts: 7.09 us -> 14 us
    all_gather x3 -> x0, waiting for transfers between devices: 249 us -> none  [the longest x2 157 us: prefix_2(): gathered = lax.all_gather(part, axis)]
    unnamed x5 -> x0, waiting for transfers between devices: 139 us -> none
    add x64 -> x0, other arithmetic: 54 us -> none  [the longest x62 53.1 us: local(): after = prefix_2(qg_total, 'ctx', lambda a, b: a + b, zeros_state, True)]
    all_to_all x0 -> x3, waiting for transfers between devices: none -> 39.9 us  [the longest x1 18.8 us: local(): lax.all_to_all(total.reshape(chips, group, columns), 'chip', 0, 0, tiled=...]
    dot_general x14 -> x0, matrix products: 28.1 us -> none  [the longest x1 5.88 us: local(): lax.dot_general(inputs, dproj, (((0,), (0,)), ((), ())), preferred_elemen...]
    all_to_all x0 -> x3, starting transfers between devices: none -> 23.4 us  [the longest x1 13.7 us: local(): mine = lax.all_to_all(spread, 'chip', 0, 0, tiled=True)]
    pallas_call x0 -> x8, Pallas kernels: none -> 17.9 us  [call(): pl.pallas_call(body, out_shape=list(outs), in_specs=specs, out_specs=[pl....]
    all_to_all x0 -> x1, blocking collectives: none -> 16.4 us  [local(): back = lax.all_to_all(sums, CTX, 0, 0, tiled=True)]
  transfers between devices with their start and end apart: 4 -> 6, of which waited for: 4 -> 4; matrix products, arithmetic and copies ran while one was open for 3% -> 0% of each run, Pallas kernels for 0% -> 12%
where the time goes in v2:
time: 124 us; the launch traced here: 123 us
  waiting for transfers between devices  40.4 us (33%)
  starting transfers between devices  32.5 us (26%)
  Pallas kernels  17.9 us (14%)
  blocking collectives  16.4 us (13%)
  local copies, waits for them, and re-layouts  14 us (11%)
    all_to_all x1, waiting for transfers between devices, local(): lax.all_to_all(total.reshape(chips, group, columns), 'chip', 0, 0, tiled=...  18.8 us
    pallas_call x8, Pallas kernels, call(): pl.pallas_call(body, out_shape=list(outs), in_specs=specs, out_specs=[pl....  17.9 us
    all_to_all x1, blocking collectives, local(): back = lax.all_to_all(sums, CTX, 0, 0, tiled=True)  16.4 us
    all_to_all x1, waiting for transfers between devices, local(): mine = lax.all_to_all(spread, 'chip', 0, 0, tiled=True)  16.4 us
    all_to_all x1, starting transfers between devices, local(): mine = lax.all_to_all(spread, 'chip', 0, 0, tiled=True)  13.7 us
    unnamed x20, local copies, waits for them, and re-layouts  12.3 us
    all_to_all x1, starting transfers between devices, local(): pieces = lax.all_to_all(parts, CTX, 0, 0, tiled=True)  5.73 us
    all_to_all x1, waiting for transfers between devices, local(): pieces = lax.all_to_all(parts, CTX, 0, 0, tiled=True)  4.78 us
  transfers between devices with their start and end apart: 6, of which 4 were waited for; matrix products, arithmetic and copies ran while one was open for 0% of the time, Pallas kernels for 12%

profile of v2, /device:TPU:1, one launch (start us, length us, event | category | flops | bytes accessed | tf_op | source)
XLA Modules:
  0.0 122.7 jit_solution(10625015164017706224)
XLA Ops:
  0.6 1.7 %broadcast_in_dim.2 = bf16[32,32,384]{2,1,0:T(8,128)(2,1)} broadcast(bf16[32,384]{1,0:T(8,128)(2,1)} %param.4), dimensions={1,2} | broadcast | bytes 811008 | tf_op jit(solution)/shard_map/broadcast_in_dim | solution.py:199
  2.3 13.7 %all-to-all-start = ((bf16[32,32,384]{2,1,0:T(8,128)(2,1)}), bf16[32,32,384]{2,1,0:T(8,128)(2,1)S(1)}, u32[]{:S(2)}, u32[]{:S(2)}) async-start(bf16[32,32,384]{2,1,0:T(8,128)(2,1)} %broadcast_in_dim.2), calls=%async_computation | async-start | bytes 1572864 | tf_op jit(solution)/shard_map/all_to_all | solution.py:200
  16.1 0.0 copy-start.7
  16.1 2.2 %copy-done.7 = bf16[1024,2048]{1,0:T(8,128)(2,1)S(1)} copy-done((bf16[1024,2048]{1,0:T(8,128)(2,1)S(1)}, bf16[1024,2048]{1,0:T(8,128)(2,1)}, u32[]{:S(2)}) %copy-start.7) | copy-done | bytes 4194328
  18.2 1.2 shard_map.50
  19.4 1.3 %copy-done.9 = bf16[32,32,1024]{2,1,0:T(8,128)(2,1)} copy-done((bf16[32,32,1024]{2,1,0:T(8,128)(2,1)}, bf16[32,32,1024]{2,1,0:T(8,128)(2,1)S(1)}, u32[]{:S(2)}) %copy-start.9) | copy-done | bytes 2097176
  20.8 16.4 %all-to-all-done.mine = bf16[32,32,384]{2,1,0:T(8,128)(2,1)S(1)} async-done(((bf16[32,32,384]{2,1,0:T(8,128)(2,1)}), bf16[32,32,384]{2,1,0:T(8,128)(2,1)S(1)}, u32[]{:S(2)}, u32[]{:S(2)}) %all-to-all-start) | async-done | bytes 786464 | tf_op jit(solution)/shard_map/all_to_all | solution.py:200
  37.1 4.7 %collective-permute-start = (bf16[32,32,384]{2,1,0:T(8,128)(2,1)S(1)}, bf16[32,32,384]{2,1,0:T(8,128)(2,1)S(1)}, u32[]{:S(2)}, u32[]{:S(2)}) collective-permute-start(bf16[32,32,384]{2,1,0:T(8,128)(2,1)S(1)} %all-to-all-done.mine), channel_id=1, source_target_pairs={{0,8},{8,0},{1,9},{9,1},{2,10},{10,2},{3,11},{11,3},{4,12},{12,4},... | collective-permute-start | bytes 2359304 | tf_op jit(solution)/shard_map/ppermute | solution.py:212
  41.8 1.9 %collective-permute-start.1 = (bf16[1024,1024]{1,0:T(8,128)(2,1)}, bf16[1024,1024]{1,0:T(8,128)(2,1)}, u32[]{:S(2)}, u32[]{:S(2)}) collective-permute-start(bf16[1024,1024]{1,0:T(8,128)(2,1)} %bitcast.5), channel_id=1, source_target_pairs={{0,8},{8,0},{1,9},{9,1},{2,10},{10,2},{3,11},{11,3},{4,12},{12,4},... | collective-permute-start | bytes 6291464 | tf_op jit(solution)/shard_map/ppermute | solution.py:211
  43.8 0.0 copy-start.8
  43.8 2.2 %copy-done.8 = bf16[1024,2048]{1,0:T(8,128)(2,1)S(1)} copy-done((bf16[1024,2048]{1,0:T(8,128)(2,1)S(1)}, bf16[1024,2048]{1,0:T(8,128)(2,1)}, u32[]{:S(2)}) %copy-start.8) | copy-done | bytes 4194328
  46.0 4.3 %shard_map.51 = (f32[1024,384]{1,0:T(8,128)S(1)}, f32[64,4,128]{2,1,0:T(4,128)}) custom-call(s32[1]{0:T(128)} %bitcast.core, bf16[1024,2048]{1,0:T(8,128)(2,1)S(1)} %copy-done.8, bf16[32,32,384]{2,1,0:T(8,128)(2,1)S(1)} %all-to-all-done.mine, bf16[32,32,384]{2,1,0:T(8,128)(2,1)S(1)} %collective-permute-done.other, f32[1024,128]{1,0:T(8,128)S(1)} %copy-done.6), custom_call_target="tpu_custom_call" | custom-call | flops 1811939328 | bytes 7995396 | tf_op jit(solution)/shard_map/pallas_call | solution.py:43
  50.3 1.2 copy-done
  51.5 5.7 %all-to-all-start.1 = ((f32[64,4,128]{2,1,0:T(4,128)}), f32[64,4,128]{2,1,0:T(4,128)S(1)}, u32[]{:S(2)}, u32[]{:S(2)}) async-start(f32[64,4,128]{2,1,0:T(4,128)} %get-tuple-element.14), calls=%async_computation.1 | async-start | bytes 262144 | tf_op jit(solution)/shard_map/all_to_all | solution.py:223
  57.2 1.4 %copy-done.1 = f32[1024,384]{1,0:T(8,128)S(1)} copy-done((f32[1024,384]{1,0:T(8,128)S(1)}, f32[1024,384]{1,0:T(8,128)}, u32[]{:S(2)}) %copy-start.1) | copy-done | bytes 1572888
  58.6 3.7 %shard_map.52.dlocal = f32[1024,384]{1,0:T(8,128)S(1)} custom-call(f32[1024,384]{1,0:T(8,128)S(1)} %copy-done.1, f32[1024,128]{1,0:T(8,128)S(1)} %copy-done.6), custom_call_target="tpu_custom_call" | custom-call | flops 1509949440 | bytes 3670016 | tf_op jit(solution)/shard_map/pallas_call | solution.py:43
  62.4 1.2 copy-done.4
  63.6 4.8 %all-to-all-done.1.pieces = f32[64,4,128]{2,1,0:T(4,128)S(1)} async-done(((f32[64,4,128]{2,1,0:T(4,128)}), f32[64,4,128]{2,1,0:T(4,128)S(1)}, u32[]{:S(2)}, u32[]{:S(2)}) %all-to-all-start.1) | async-done | bytes 131104 | tf_op jit(solution)/shard_map/all_to_all | solution.py:223
  68.3 0.1 shard_map.53
  68.4 16.4 %all_to_all.20.back = f32[64,4,128]{2,1,0:T(4,128)S(1)} all-to-all(f32[64,4,128]{2,1,0:T(4,128)S(1)} %shard_map.53), channel_id=1, replica_groups=mesh['chip'=32,'core'=2,'head'=8] {'chip','core'}, dimensions={0} | all-to-all | bytes 262144 | tf_op jit(solution)/shard_map/all_to_all | solution.py:235
  84.9 1.4 %copy-done.2 = f32[1024,384]{1,0:T(8,128)S(1)} copy-done((f32[1024,384]{1,0:T(8,128)S(1)}, f32[1024,384]{1,0:T(8,128)}, u32[]{:S(2)}) %copy-start.2) | copy-done | bytes 1572888
  86.3 1.4 %copy-done.5 = f32[1024,384]{1,0:T(8,128)S(1)} copy-done((f32[1024,384]{1,0:T(8,128)S(1)}, f32[1024,384]{1,0:T(8,128)}, u32[]{:S(2)}) %copy-start.5) | copy-done | bytes 1572888
  87.7 0.8 shard_map.55.dproj
  88.5 2.5 %collective-permute-start.2 = (bf16[1024,384]{1,0:T(8,128)(2,1)S(1)}, bf16[1024,384]{1,0:T(8,128)(2,1)S(1)}, u32[]{:S(2)}, u32[]{:S(2)}) collective-permute-start(bf16[1024,384]{1,0:T(8,128)(2,1)S(1)} %shard_map.55.dproj), channel_id=1, source_target_pairs={{0,8},{8,0},{1,9},{9,1},{2,10},{10,2},{3,11},{11,3},{4,12},{12,4},... | collective-permute-start | bytes 2359304 | tf_op jit(solution)/shard_map/ppermute | solution.py:246
  91.0 1.2 %shard_map.56.product = f32[1024,384]{1,0:T(8,128)S(1)} custom-call(bf16[1024,1024]{1,0:T(8,128)(2,1)S(1)} %bitcast.4, bf16[1024,384]{1,0:T(8,128)(2,1)S(1)} %shard_map.55.dproj), custom_call_target="tpu_custom_call" | custom-call | flops 805306368 | bytes 4456448 | tf_op jit(solution)/shard_map/pallas_call | solution.py:43
  92.2 0.4 collective-permute-done.2.dproj
  92.7 3.8 %shard_map.57 = bf16[1024,384]{1,0:T(8,128)(2,1)} custom-call(bf16[1024,1024]{1,0:T(8,128)(2,1)} %collective-permute-done.1.turned, bf16[1024,384]{1,0:T(8,128)(2,1)S(1)} %collective-permute-done.2.dproj, f32[1024,384]{1,0:T(8,128)S(1)} %shard_map.56.product), custom_call_target="tpu_custom_call" | custom-call | flops 805306368 | bytes 5242880 | tf_op jit(solution)/shard_map/pallas_call | solution.py:43
  96.5 3.9 %all-to-all-start.3 = ((bf16[32,32,384]{2,1,0:T(8,128)(2,1)}), bf16[32,32,384]{2,1,0:T(8,128)(2,1)S(1)}, u32[]{:S(2)}, u32[]{:S(2)}) async-start(bf16[32,32,384]{2,1,0:T(8,128)(2,1)} %bitcast.3), calls=%async_computation.3 | async-start | bytes 1572864 | tf_op jit(solution)/shard_map/all_to_all | solution.py:261
  100.4 2.8 %shard_map.54 = f32[1024,128]{1,0:T(8,128)} custom-call(f32[64,4,128]{2,1,0:T(4,128)S(1)} %all_to_all.20.back, f32[1024,384]{1,0:T(8,128)S(1)} %copy-done.3), custom_call_target="tpu_custom_call" | custom-call | flops 603979776 | bytes 2228224 | tf_op jit(solution)/shard_map/pallas_call | solution.py:43
  103.2 18.8 %all-to-all-done.3 = bf16[32,32,384]{2,1,0:T(8,128)(2,1)S(1)} async-done(((bf16[32,32,384]{2,1,0:T(8,128)(2,1)}), bf16[32,32,384]{2,1,0:T(8,128)(2,1)S(1)}, u32[]{:S(2)}, u32[]{:S(2)}) %all-to-all-start.3) | async-done | bytes 786464 | tf_op jit(solution)/shard_map/all_to_all | solution.py:261
  122.0 0.1 convert_reduce_fusion
  122.1 0.6 broadcast_multiply_fusion
  (12 shorter events, 0.0 us)
Async XLA Ops:
  2.3 34.8 %all-to-all-start = ((bf16[32,32,384]{2,1,0:T(8,128)(2,1)}), bf16[32,32,384]{2,1,0:T(8,128)(2,1)S(1)}, u32[]{:S(2)}, u32[]{:S(2)}) async-start(bf16[32,32,384]{2,1,0:T(8,128)(2,1)} %broadcast_in_dim.2), calls=%async_computation | async-start | bytes 1572864 | tf_op jit(solution)/shard_map/all_to_all | solution.py:200
  16.1 2.2 %copy-start.7 = (bf16[1024,2048]{1,0:T(8,128)(2,1)S(1)}, bf16[1024,2048]{1,0:T(8,128)(2,1)}, u32[]{:S(2)}) copy-start(bf16[1024,2048]{1,0:T(8,128)(2,1)} %hidden.3) | copy-start | bytes 12582916
  18.2 25.5 %copy-start.6 = (f32[1024,128]{1,0:T(8,128)S(1)}, f32[1024,128]{1,0:T(8,128)}, u32[]{:S(2)}) copy-start(f32[1024,128]{1,0:T(8,128)} %cotangent.5) | copy-start | bytes 1572868
  19.4 1.3 %copy-start.9 = (bf16[32,32,1024]{2,1,0:T(8,128)(2,1)}, bf16[32,32,1024]{2,1,0:T(8,128)(2,1)S(1)}, u32[]{:S(2)}) copy-start(bf16[32,32,1024]{2,1,0:T(8,128)(2,1)S(1)} %get-tuple-element.17) | copy-start | bytes 6291460
  37.1 6.7 %collective-permute-start = (bf16[32,32,384]{2,1,0:T(8,128)(2,1)S(1)}, bf16[32,32,384]{2,1,0:T(8,128)(2,1)S(1)}, u32[]{:S(2)}, u32[]{:S(2)}) collective-permute-start(bf16[32,32,384]{2,1,0:T(8,128)(2,1)S(1)} %all-to-all-done.mine), channel_id=1, source_target_pairs={{0,8},{8,0},{1,9},{9,1},{2,10},{10,2},{3,11},{11,3},{4,12},{12,4},... | collective-permute-start | bytes 2359304 | tf_op jit(solution)/shard_map/ppermute | solution.py:212
  41.8 50.8 %collective-permute-start.1 = (bf16[1024,1024]{1,0:T(8,128)(2,1)}, bf16[1024,1024]{1,0:T(8,128)(2,1)}, u32[]{:S(2)}, u32[]{:S(2)}) collective-permute-start(bf16[1024,1024]{1,0:T(8,128)(2,1)} %bitcast.5), channel_id=1, source_target_pairs={{0,8},{8,0},{1,9},{9,1},{2,10},{10,2},{3,11},{11,3},{4,12},{12,4},... | collective-permute-start | bytes 6291464 | tf_op jit(solution)/shard_map/ppermute | solution.py:211
  43.8 2.2 %copy-start.8 = (bf16[1024,2048]{1,0:T(8,128)(2,1)S(1)}, bf16[1024,2048]{1,0:T(8,128)(2,1)}, u32[]{:S(2)}) copy-start(bf16[1024,2048]{1,0:T(8,128)(2,1)} %hidden.3) | copy-start | bytes 12582916
  50.3 1.2 copy-start
  51.5 16.9 %all-to-all-start.1 = ((f32[64,4,128]{2,1,0:T(4,128)}), f32[64,4,128]{2,1,0:T(4,128)S(1)}, u32[]{:S(2)}, u32[]{:S(2)}) async-start(f32[64,4,128]{2,1,0:T(4,128)} %get-tuple-element.14), calls=%async_computation.1 | async-start | bytes 262144 | tf_op jit(solution)/shard_map/all_to_all | solution.py:223
  57.2 1.4 %copy-start.1 = (f32[1024,384]{1,0:T(8,128)S(1)}, f32[1024,384]{1,0:T(8,128)}, u32[]{:S(2)}) copy-start(f32[1024,384]{1,0:T(8,128)} %copy-done) | copy-start | bytes 4718596
  62.4 1.2 copy-start.4
  84.9 1.4 %copy-start.2 = (f32[1024,384]{1,0:T(8,128)S(1)}, f32[1024,384]{1,0:T(8,128)}, u32[]{:S(2)}) copy-start(f32[1024,384]{1,0:T(8,128)} %copy-done) | copy-start | bytes 4718596
  86.3 1.4 %copy-start.5 = (f32[1024,384]{1,0:T(8,128)S(1)}, f32[1024,384]{1,0:T(8,128)}, u32[]{:S(2)}) copy-start(f32[1024,384]{1,0:T(8,128)} %copy-done.4) | copy-start | bytes 4718596
  88.5 4.2 %collective-permute-start.2 = (bf16[1024,384]{1,0:T(8,128)(2,1)S(1)}, bf16[1024,384]{1,0:T(8,128)(2,1)S(1)}, u32[]{:S(2)}, u32[]{:S(2)}) collective-permute-start(bf16[1024,384]{1,0:T(8,128)(2,1)S(1)} %shard_map.55.dproj), channel_id=1, source_target_pairs={{0,8},{8,0},{1,9},{9,1},{2,10},{10,2},{3,11},{11,3},{4,12},{12,4},... | collective-permute-start | bytes 2359304 | tf_op jit(solution)/shard_map/ppermute | solution.py:246
  92.2 8.1 %copy-start.3 = (f32[1024,384]{1,0:T(8,128)S(1)}, f32[1024,384]{1,0:T(8,128)}, u32[]{:S(2)}) copy-start(f32[1024,384]{1,0:T(8,128)} %copy-done) | copy-start | bytes 4718596
  96.5 25.5 %all-to-all-start.3 = ((bf16[32,32,384]{2,1,0:T(8,128)(2,1)}), bf16[32,32,384]{2,1,0:T(8,128)(2,1)S(1)}, u32[]{:S(2)}, u32[]{:S(2)}) async-start(bf16[32,32,384]{2,1,0:T(8,128)(2,1)} %bitcast.3), calls=%async_computation.3 | async-start | bytes 1572864 | tf_op jit(solution)/shard_map/all_to_all | solution.py:261

commit v3 on v2

v3 whole, which is shorter than its diff:
```python
import functools

import jax
import jax.numpy as jnp
from jax import lax
from jax.experimental import pallas as pl
from jax.experimental.pallas import tpu as pltpu
from jax.sharding import Mesh, PartitionSpec as P

HD = 128
BLOCK = 256
CORES = 2
MIB = 1 << 20

SWAP = [(0, 1), (1, 0)]
CTX = ("chip", "core")
F32 = jnp.float32
BF16 = jnp.bfloat16

PLAIN = (((1,), (0,)), ((), ()))
ROWS = (((1,), (1,)), ((), ()))
COLS = (((0,), (0,)), ((), ()))


def mxu(a, b, dims=PLAIN):
    return lax.dot_general(a, b, dims, preferred_element_type=F32)


def split(x):
    high = x.astype(BF16)
    return high, (x - high.astype(F32)).astype(BF16)


def mxu3(a, b, dims=PLAIN):
    return mxu(a[0], b[0], dims) + (mxu(a[0], b[1], dims) + mxu(a[1], b[0], dims))


HBM = pl.BlockSpec(memory_space=pltpu.HBM)
VMEM = pl.BlockSpec(memory_space=pltpu.VMEM)
SMEM = pl.BlockSpec(memory_space=pltpu.SMEM)


def call(body, outs, args, flops, vmem, specs, scratch=(), kind=jax.ShapeDtypeStruct):
    size = sum(a.size * a.dtype.itemsize for a in args)
    args = [
        pltpu.with_memory_space_constraint(a, pltpu.HBM) if spec is HBM else a
        for a, spec in zip(args, specs)
    ]
    return pl.pallas_call(
        body,
        out_shape=[kind(dims, dtype) for dims, dtype in outs],
        in_specs=specs,
        out_specs=[VMEM] * len(outs),
        scratch_shapes=list(scratch),
        cost_estimate=pl.CostEstimate(flops=flops, bytes_accessed=size, transcendentals=0),
        compiler_params=pltpu.CompilerParams(vmem_limit_bytes=vmem * MIB),
    )(*args)


def causal():
    at = lax.broadcasted_iota(jnp.int32, (BLOCK, BLOCK), 0)
    return at >= lax.broadcasted_iota(jnp.int32, (BLOCK, BLOCK), 1)


def blocks(tokens):
    return [
        (slab, slice(start, start + BLOCK))
        for slab in range(CORES)
        for start in range(0, tokens, BLOCK)
    ]


def pieces_of(ref, slab, rows):
    return tuple(split(ref[slab, rows, j * HD : (j + 1) * HD]) for j in range(3))


def spread_kernel(weight, copies):
    for chip in range(copies.shape[0]):
        copies[chip] = weight[...]


def prepare_kernel(group, core, hidden, partner, cot, cot_partner, near, far, turned, cots):
    cots[core[0]] = cot[...]
    cots[1 - core[0]] = cot_partner[...]
    wide = 2 * HD
    at = lax.broadcasted_iota(jnp.int32, (wide, wide), 0)
    to = lax.broadcasted_iota(jnp.int32, (wide, wide), 1)
    parity = jnp.where(to < HD, core[0], 1 - core[0])
    slot = lax.rem(to, HD)
    source = (lax.div(slot, group) * CORES + parity) * group + lax.rem(slot, group)
    order = jnp.where(at == source, 1.0, 0.0).astype(BF16)
    for which, rows in ((core[0], hidden), (1 - core[0], partner)):
        for step in range(hidden.shape[1] // wide):
            columns = mxu(rows[:, step * wide : (step + 1) * wide], order).astype(BF16)
            span = slice(step * HD, (step + 1) * HD)
            near[which, :, span] = columns[:, :HD]
            far[which, :, span] = columns[:, HD:]
            turned[which, span, :] = columns[:, :HD].T


def half_kernel(near, mine, partial):
    chips, group, columns = mine.shape
    weight = mine[...].reshape(chips * group, columns)
    for slab, rows in blocks(near.shape[1]):
        partial[slab, rows, :] = mxu(near[slab, rows, :], weight)


def project_kernel(core, far, theirs, partial, cots, proj, parts):
    chips, group, columns = theirs.shape
    weight = theirs[...].reshape(chips * group, columns)
    first = core[0] == 0
    state = jnp.zeros((HD, HD), F32)
    for slab, rows in blocks(far.shape[1]):
        part = partial[slab, rows, :] + mxu(far[slab, rows, :], weight)
        proj[slab, rows, :] = part
        cotangent = cots[slab, rows, :]
        left = jnp.where(first, part[:, HD : 2 * HD], part[:, :HD])
        right = jnp.where(first, part[:, 2 * HD :], cotangent)
        state += mxu3(split(left), split(right), COLS)
    piece = HD // chips
    for chip in range(chips):
        parts[chip] = state[chip * piece : (chip + 1) * piece]


def local_kernel(proj, cots, dlocal, states):
    mask = causal()
    state = jnp.zeros((HD, HD), F32)
    for slab, rows in blocks(proj.shape[1]):
        if slab and rows.start == 0:
            states[...] = state
        query, keys, values = pieces_of(proj, slab, rows)
        cot = split(cots[slab, rows, :])
        scores = split(jnp.where(mask, mxu3(query, keys, ROWS), 0.0))
        dmat = split(jnp.where(mask, mxu3(cot, values, ROWS), 0.0))
        dlocal[slab, rows, 0:HD] = mxu3(dmat, keys) + mxu3(cot, split(state), ROWS)
        dlocal[slab, rows, HD : 2 * HD] = mxu3(dmat, query, COLS)
        dlocal[slab, rows, 2 * HD :] = mxu3(scores, cot, COLS)
        state += mxu3(keys, values, COLS)


def later_kernel(proj, cots, dlocal, out):
    state = jnp.zeros((HD, HD), F32)
    for slab, rows in reversed(blocks(proj.shape[1])):
        query, keys, values = pieces_of(proj, slab, rows)
        suffix = split(state)
        out[slab, rows, 0:HD] = dlocal[slab, rows, 0:HD]
        out[slab, rows, HD : 2 * HD] = dlocal[slab, rows, HD : 2 * HD] + mxu3(
            values, suffix, ROWS
        )
        out[slab, rows, 2 * HD :] = dlocal[slab, rows, 2 * HD :] + mxu3(keys, suffix)
        state += mxu3(query, split(cots[slab, rows, :]), COLS)


def scan_kernel(core, pieces, sums):
    chips = pieces.shape[0]
    flip = core[0] == 1
    total = jnp.zeros(pieces.shape[1:], F32)
    for step in range(chips):
        chip = jnp.where(flip, chips - 1 - step, step)
        for member in range(CORES):
            sums[CORES * chip + member] = total
        total += pieces[chip]


def joined(back, which, states):
    chips, piece = back.shape[0] // CORES, back.shape[1]
    for chip in range(chips):
        states[which, chip * piece : (chip + 1) * piece, :] = back[CORES * chip + which]
    return states[which]


def finish_kernel(scale, back, proj, cots, dlocal, turned, total,
                  kv, cot, part, rows_turned, dproj, states, sems):
    tokens = cots.shape[1]
    loads = []
    for index, (slab, rows) in enumerate(blocks(tokens)):
        loads.append(
            [
                pltpu.make_async_copy(source, target, sems.at[index, which])
                for which, (source, target) in enumerate(
                    (
                        (proj.at[slab, rows, pl.ds(HD, 2 * HD)], kv.at[slab, rows, :]),
                        (cots.at[slab, rows, :], cot.at[slab, rows, :]),
                        (dlocal.at[slab, rows, :], part.at[slab, rows, :]),
                    )
                )
            ]
        )
    last = len(loads)
    loads.append(
        [
            pltpu.make_async_copy(turned.at[slab], rows_turned.at[slab], sems.at[last, slab])
            for slab in range(CORES)
        ]
    )
    for group in loads:
        for load in group:
            load.start()
    before, after = joined(back, 0, states), joined(back, 1, states)
    prefix, suffix, suffix_turned = split(before.T), split(after), split(after.T)
    for index, (slab, rows) in enumerate(blocks(tokens)):
        for load in loads[index]:
            load.wait()
        keys, values = split(kv[slab, rows, :HD]), split(kv[slab, rows, HD:])
        for j, term in enumerate(
            (
                mxu3(split(cot[slab, rows, :]), prefix),
                mxu3(values, suffix_turned),
                mxu3(keys, suffix),
            )
        ):
            columns = slice(j * HD, (j + 1) * HD)
            dproj[slab, rows, columns] = (scale * (part[slab, rows, columns] + term)).astype(BF16)
    for load in loads[last]:
        load.wait()
    for start in range(0, turned.shape[1], BLOCK):
        rows = slice(start, start + BLOCK)
        total[rows, :] = (
            mxu(rows_turned[0, rows, :], dproj[0]) + mxu(rows_turned[1, rows, :], dproj[1])
        ).astype(BF16)


def attended_kernel(scale, core, back, early, proj, attended, states):
    tokens = proj.shape[1]
    before = joined(back, 0, states)
    state = jnp.where(core[0] == 0, before, before + early[...])
    mask = causal()
    for start in range(0, tokens, BLOCK):
        rows = slice(start, start + BLOCK)
        query, keys, values = pieces_of(proj, core[0], rows)
        scores = split(jnp.where(mask, mxu3(query, keys, ROWS), 0.0))
        attended[rows, :] = scale * (mxu3(scores, values) + mxu3(query, split(state)))
        state += mxu3(keys, values, COLS)


def local(hidden, qkv_weight, out_grad):
    tokens, width = hidden.shape
    group, columns = qkv_weight.shape
    chips = lax.axis_size("chip")
    devices = chips * CORES
    piece = HD // chips
    half = width // CORES
    total_tokens = tokens * devices
    scale = float(HD * total_tokens) ** (-0.5)
    grad_scale = float(total_tokens) ** (-0.5)
    core = lax.axis_index("core").astype(jnp.int32).reshape(1)
    square = CORES * tokens * HD * HD
    product = 2 * CORES * tokens * half * columns

    (copies,) = call(spread_kernel, [((chips, group, columns), BF16)], [qkv_weight], 1024, 8, [VMEM])
    mine = lax.all_to_all(copies, "chip", 0, 0, tiled=True)
    partner = lax.ppermute(hidden, "core", SWAP)
    cot_partner = lax.ppermute(out_grad, "core", SWAP)
    near, far, turned, cots = call(
        functools.partial(prepare_kernel, group),
        [((CORES, tokens, half), BF16)] * 2 + [
            ((CORES, half, tokens), BF16),
            ((CORES, tokens, HD), F32),
        ],
        [core, hidden, partner, out_grad, cot_partner],
        2 * tokens * width * 1024,
        40,
        [SMEM] + [VMEM] * 4,
    )
    mine, near, far, turned, cots = lax.optimization_barrier((mine, near, far, turned, cots))
    theirs = lax.ppermute(mine, "core", SWAP)
    (partial,) = call(
        half_kernel, [((CORES, tokens, columns), F32)], [near, mine], product, 24, [VMEM, VMEM]
    )
    proj, parts = call(
        project_kernel,
        [((CORES, tokens, columns), F32), ((chips, piece, HD), F32)],
        [core, far, theirs, partial, cots],
        product + 6 * square,
        32,
        [SMEM] + [VMEM] * 4,
    )
    pieces = lax.all_to_all(parts, "chip", 0, 0, tiled=True)
    dlocal, early = call(
        local_kernel,
        [((CORES, tokens, columns), F32), ((HD, HD), F32)],
        [proj, cots],
        12 * 6 * square,
        32,
        [VMEM, VMEM],
    )
    pieces, dlocal = lax.optimization_barrier((pieces, dlocal))
    (sums,) = call(
        scan_kernel, [((devices, piece, HD), F32)], [core, pieces], 4 * HD * HD, 8, [SMEM, VMEM]
    )
    back = lax.all_to_all(sums, CTX, 0, 0, tiled=True)
    (dlocal,) = call(
        later_kernel,
        [((CORES, tokens, columns), F32)],
        [proj, cots, dlocal],
        3 * 6 * square,
        32,
        [VMEM] * 3,
    )
    (total,) = call(
        functools.partial(finish_kernel, scale),
        [((half, columns), BF16)],
        [back, proj, cots, dlocal, turned],
        18 * square + product,
        32,
        [VMEM] + [HBM] * 4,
        [
            pltpu.VMEM((CORES, tokens, 2 * HD), F32),
            pltpu.VMEM((CORES, tokens, HD), F32),
            pltpu.VMEM((CORES, tokens, columns), F32),
            pltpu.VMEM((CORES, half, tokens), BF16),
            pltpu.VMEM((CORES, tokens, columns), BF16),
            pltpu.VMEM((2, HD, HD), F32),
            pltpu.SemaphoreType.DMA((CORES * tokens // BLOCK + 1, 3)),
        ],
        pltpu.HBM,
    )
    landed = lax.all_to_all(total.reshape(chips, group, columns), "chip", 0, 0, tiled=True)
    (attended,) = call(
        functools.partial(attended_kernel, scale),
        [((tokens, HD), F32)],
        [core, back, early, proj],
        6 * 6 * square,
        24,
        [SMEM] + [VMEM] * 3,
        [pltpu.VMEM((2, HD, HD), F32)],
    )
    return attended, jnp.sum(landed.astype(F32), axis=0) * grad_scale


def solution(mesh):
    chips, heads = mesh.shape["ctx"] // CORES, mesh.shape["head"]
    fine = Mesh(mesh.devices.reshape(chips, CORES, heads), ("chip", "core", "head"))
    return jax.shard_map(
        local,
        mesh=fine,
        in_specs=(P(CTX, None), P(CTX, "head"), P(CTX, "head")),
        out_specs=(P(CTX, "head"), P(CTX, "head")),
        check_vma=False,
    )
```

time: 124 us -> 129 us (1.040)
  Pallas kernels: 17.9 us -> 35.2 us
  blocking collectives: 16.4 us -> 0 us
  waiting for transfers between devices: 40.4 us -> 28.2 us
  starting transfers between devices: 32.5 us -> 43.6 us
  local copies, waits for them, and re-layouts: 14 us -> 16.8 us
    pallas_call x8 -> x9, Pallas kernels: 17.9 us -> 35.2 us  [call(): pl.pallas_call(body, out_shape=[kind(dims, dtype) for dims, dtype in outs...]
    all_to_all x1 -> x0, blocking collectives: 16.4 us -> none  [local(): back = lax.all_to_all(sums, CTX, 0, 0, tiled=True)]
    all_to_all x2 -> x3, waiting for transfers between devices: 21.1 us -> 7.88 us  [the longest x1 4.11 us: local(): mine = lax.all_to_all(copies, 'chip', 0, 0, tiled=True)]
    ppermute x3, starting transfers between devices: 9.12 us -> 14.5 us  [the longest x1 8.79 us: local(): partner = lax.ppermute(hidden, 'core', SWAP)]
    unnamed x20 -> x30, local copies, waits for them, and re-layouts: 12.3 us -> 16.8 us
    all_to_all x2 -> x3, starting transfers between devices: 19.4 us -> 23.1 us  [the longest x1 10.2 us: local(): back = lax.all_to_all(sums, CTX, 0, 0, tiled=True)]
    all_to_all x1, starting transfers between devices: 3.91 us -> 5.97 us  [local(): lax.all_to_all(total.reshape(chips, group, columns), 'chip', 0, 0, tiled=...]
    broadcast_in_dim x1 -> x0, local copies, waits for them, and re-layouts: 1.7 us -> none  [local(): spread = jnp.broadcast_to(qkv_weight[None], (chips, group, columns))]
  transfers between devices with their start and end apart: 6 -> 7, of which waited for: 4 -> 4; matrix products, arithmetic and copies ran while one was open for 0% -> 0% of each run, Pallas kernels for 12% -> 17%
where the time goes in v3:
time: 129 us; the launch traced here: 127 us
  starting transfers between devices  43.6 us (34%)
  Pallas kernels  35.2 us (27%)
  waiting for transfers between devices  28.2 us (22%)
  local copies, waits for them, and re-layouts  16.8 us (13%)
  other arithmetic  1.88 us (1%)
    pallas_call x9, Pallas kernels, call(): pl.pallas_call(body, out_shape=[kind(dims, dtype) for dims, dtype in outs...  35.2 us
    all_to_all x1, waiting for transfers between devices, local(): lax.all_to_all(total.reshape(chips, group, columns), 'chip', 0, 0, tiled=...  18.5 us
    unnamed x30, local copies, waits for them, and re-layouts  16.8 us
    all_to_all x1, starting transfers between devices, local(): back = lax.all_to_all(sums, CTX, 0, 0, tiled=True)  10.2 us
    ppermute x1, starting transfers between devices, local(): partner = lax.ppermute(hidden, 'core', SWAP)  8.79 us
    all_to_all x1, starting transfers between devices, local(): mine = lax.all_to_all(copies, 'chip', 0, 0, tiled=True)  7.51 us
    all_to_all x1, starting transfers between devices, local(): lax.all_to_all(total.reshape(chips, group, columns), 'chip', 0, 0, tiled=...  5.97 us
    all_to_all x1, starting transfers between devices, local(): pieces = lax.all_to_all(parts, 'chip', 0, 0, tiled=True)  5.4 us
  transfers between devices with their start and end apart: 7, of which 4 were waited for; matrix products, arithmetic and copies ran while one was open for 0% of the time, Pallas kernels for 17%

profile of v3, /device:TPU:1, one launch (start us, length us, event | category | flops | bytes accessed | tf_op | source)
XLA Modules:
  0.0 126.5 jit_solution(2256262429680091171)
XLA Ops:
  0.6 8.8 %collective-permute-start = (bf16[1024,2048]{1,0:T(8,128)(2,1)}, bf16[1024,2048]{1,0:T(8,128)(2,1)}, u32[]{:S(2)}, u32[]{:S(2)}) collective-permute-start(bf16[1024,2048]{1,0:T(8,128)(2,1)} %hidden.1), channel_id=1, source_target_pairs={{0,8},{8,0},{1,9},{9,1},{2,10},{10,2},{3,11},{11,3},{4,12},{12,4},... | collective-permute-start | bytes 12582920 | tf_op jit(solution)/shard_map/ppermute | solution.py:252
  9.4 0.7 copy-done.13
  10.2 1.0 shard_map.50
  11.1 7.5 %all-to-all-start = ((bf16[32,32,384]{2,1,0:T(8,128)(2,1)}), bf16[32,32,384]{2,1,0:T(8,128)(2,1)S(1)}, u32[]{:S(2)}, u32[]{:S(2)}) async-start(bf16[32,32,384]{2,1,0:T(8,128)(2,1)} %shard_map.50), calls=%async_computation | async-start | bytes 1572864 | tf_op jit(solution)/shard_map/all_to_all | solution.py:251
  18.6 2.2 %collective-permute-start.1 = (f32[1024,128]{1,0:T(8,128)}, f32[1024,128]{1,0:T(8,128)S(1)}, u32[]{:S(2)}, u32[]{:S(2)}) collective-permute-start(f32[1024,128]{1,0:T(8,128)} %cot.1), channel_id=1, source_target_pairs={{0,8},{8,0},{1,9},{9,1},{2,10},{10,2},{3,11},{11,3},{4,12},{12,4},... | collective-permute-start | bytes 1572872 | tf_op jit(solution)/shard_map/ppermute | solution.py:253
  20.9 1.8 %collective-permute-done.1.cot_partner = f32[1024,128]{1,0:T(8,128)S(1)} collective-permute-done((f32[1024,128]{1,0:T(8,128)}, f32[1024,128]{1,0:T(8,128)S(1)}, u32[]{:S(2)}, u32[]{:S(2)}) %collective-permute-start.1) | collective-permute-done | bytes 524320 | tf_op jit(solution)/shard_map/ppermute | solution.py:253
  22.7 1.0 copy-done.14
  23.7 7.9 %shard_map.51 = (bf16[2,1024,1024]{2,1,0:T(8,128)(2,1)S(1)}, bf16[2,1024,1024]{2,1,0:T(8,128)(2,1)S(1)}, bf16[2,1024,1024]{2,1,0:T(8,128)(2,1)}, f32[2,1024,128]{2,1,0:T(8,128)S(1)}) custom-call(s32[1]{0:T(128)} %bitcast.core, bf16[1024,2048]{1,0:T(8,128)(2,1)} %hidden.1, bf16[1024,2048]{1,0:T(8,128)(2,1)} %collective-permute-done.partner, ...), custom_call_target="tpu_custom_call" | custom-call | flops 4294967296 | bytes 9437188 | tf_op jit(solution)/shard_map/pallas_call | solution.py:49
  31.6 1.0 copy-done.3
  32.6 2.0 %copy-done.7 = bf16[2,1024,1024]{2,1,0:T(8,128)(2,1)} copy-done((bf16[2,1024,1024]{2,1,0:T(8,128)(2,1)}, bf16[2,1024,1024]{2,1,0:T(8,128)(2,1)S(1)}, u32[]{:S(2)}) %copy-start.7) | copy-done | bytes 4194328
  34.7 2.0 %copy-done.9 = bf16[2,1024,1024]{2,1,0:T(8,128)(2,1)} copy-done((bf16[2,1024,1024]{2,1,0:T(8,128)(2,1)}, bf16[2,1024,1024]{2,1,0:T(8,128)(2,1)S(1)}, u32[]{:S(2)}) %copy-start.9) | copy-done | bytes 4194328
  36.6 4.1 %all-to-all-done.mine = bf16[32,32,384]{2,1,0:T(8,128)(2,1)S(1)} async-done(((bf16[32,32,384]{2,1,0:T(8,128)(2,1)}), bf16[32,32,384]{2,1,0:T(8,128)(2,1)S(1)}, u32[]{:S(2)}, u32[]{:S(2)}) %all-to-all-start) | async-done | bytes 786464 | tf_op jit(solution)/shard_map/all_to_all | solution.py:251
  40.8 3.5 %collective-permute-start.2 = (bf16[32,32,384]{2,1,0:T(8,128)(2,1)S(1)}, bf16[32,32,384]{2,1,0:T(8,128)(2,1)S(1)}, u32[]{:S(2)}, u32[]{:S(2)}) collective-permute-start(bf16[32,32,384]{2,1,0:T(8,128)(2,1)S(1)} %all-to-all-done.mine), channel_id=1, source_target_pairs={{0,8},{8,0},{1,9},{9,1},{2,10},{10,2},{3,11},{11,3},{4,12},{12,4},... | collective-permute-start | bytes 2359304 | tf_op jit(solution)/shard_map/ppermute | solution.py:266
  44.3 2.2 %copy-done.10 = bf16[2,1024,1024]{2,1,0:T(8,128)(2,1)S(1)} copy-done((bf16[2,1024,1024]{2,1,0:T(8,128)(2,1)S(1)}, bf16[2,1024,1024]{2,1,0:T(8,128)(2,1)}, u32[]{:S(2)}) %copy-start.10) | copy-done | bytes 4194328
  46.5 2.3 %shard_map.52.partial = f32[2,1024,384]{2,1,0:T(8,128)S(1)} custom-call(bf16[2,1024,1024]{2,1,0:T(8,128)(2,1)S(1)} %copy-done.10, bf16[32,32,384]{2,1,0:T(8,128)(2,1)S(1)} %all-to-all-done.mine), custom_call_target="tpu_custom_call" | custom-call | flops 1610612736 | bytes 4980736 | tf_op jit(solution)/shard_map/pallas_call | solution.py:49
  48.8 4.8 %shard_map.53 = (f32[2,1024,384]{2,1,0:T(8,128)S(1)}, f32[32,4,128]{2,1,0:T(4,128)}) custom-call(s32[1]{0:T(128)} %bitcast.core, bf16[2,1024,1024]{2,1,0:T(8,128)(2,1)S(1)} %copy-done.8, bf16[32,32,384]{2,1,0:T(8,128)(2,1)S(1)} %collective-permute-done.2.theirs, f32[2,1024,384]{2,1,0:T(8,128)S(1)} %shard_map.52.partial, f32[2,1024,128]{2,1,0:T(8,128)S(1)} %copy-done.4), custom_call_target="tpu_custom_call" | custom-call | flops 1811939328 | bytes 9175044 | tf_op jit(solution)/shard_map/pallas_call | solution.py:49
  53.6 5.4 %all-to-all-start.1 = ((f32[32,4,128]{2,1,0:T(4,128)}), f32[32,4,128]{2,1,0:T(4,128)S(1)}, u32[]{:S(2)}, u32[]{:S(2)}) async-start(f32[32,4,128]{2,1,0:T(4,128)} %get-tuple-element.25), calls=%async_computation.1 | async-start | bytes 131072 | tf_op jit(solution)/shard_map/all_to_all | solution.py:278
  59.1 1.2 copy-done.5
  60.3 5.7 %shard_map.54 = (f32[2,1024,384]{2,1,0:T(8,128)S(1)}, f32[128,128]{1,0:T(8,128)S(1)}) custom-call(f32[2,1024,384]{2,1,0:T(8,128)S(1)} %get-tuple-element.26.proj, f32[2,1024,128]{2,1,0:T(8,128)S(1)} %copy-done.5), custom_call_target="tpu_custom_call" | custom-call | flops 2415919104 | bytes 4194304 | tf_op jit(solution)/shard_map/pallas_call | solution.py:49
  66.0 1.7 %copy-done.11 = f32[2,1024,384]{2,1,0:T(8,128)} copy-done((f32[2,1024,384]{2,1,0:T(8,128)}, f32[2,1024,384]{2,1,0:T(8,128)S(1)}, u32[]{:S(2)}) %copy-start.11) | copy-done | bytes 3145752
  67.7 0.7 shard_map.55
  68.4 10.2 %all-to-all-start.2 = ((f32[64,4,128]{2,1,0:T(4,128)}), f32[64,4,128]{2,1,0:T(4,128)S(1)}, u32[]{:S(2)}, u32[]{:S(2)}) async-start(f32[64,4,128]{2,1,0:T(4,128)} %shard_map.55), calls=%async_computation.2 | async-start | bytes 262144 | tf_op jit(solution)/shard_map/all_to_all | solution.py:291
  78.7 1.2 copy-done.6
  79.9 1.9 %copy-done.12 = f32[2,1024,384]{2,1,0:T(8,128)S(1)} copy-done((f32[2,1024,384]{2,1,0:T(8,128)S(1)}, f32[2,1024,384]{2,1,0:T(8,128)}, u32[]{:S(2)}) %copy-start.12) | copy-done | bytes 3145752
  81.8 2.5 %shard_map.57.dlocal = f32[2,1024,384]{2,1,0:T(8,128)S(1)} custom-call(f32[2,1024,384]{2,1,0:T(8,128)S(1)} %get-tuple-element.26.proj, f32[2,1024,128]{2,1,0:T(8,128)S(1)} %copy-done.6, f32[2,1024,384]{2,1,0:T(8,128)S(1)} %copy-done.12), custom_call_target="tpu_custom_call" | custom-call | flops 603979776 | bytes 7340032 | tf_op jit(solution)/shard_map/pallas_call | solution.py:49
  84.2 1.7 %copy-done.2 = f32[2,1024,384]{2,1,0:T(8,128)} copy-done((f32[2,1024,384]{2,1,0:T(8,128)}, f32[2,1024,384]{2,1,0:T(8,128)S(1)}, u32[]{:S(2)}) %copy-start.2) | copy-done | bytes 3145752
  86.0 3.8 %all-to-all-done.2.back = f32[64,4,128]{2,1,0:T(4,128)S(1)} async-done(((f32[64,4,128]{2,1,0:T(4,128)}), f32[64,4,128]{2,1,0:T(4,128)S(1)}, u32[]{:S(2)}, u32[]{:S(2)}) %all-to-all-start.2) | async-done | bytes 131104 | tf_op jit(solution)/shard_map/all_to_all | solution.py:291
  89.7 7.6 %shard_map.58 = bf16[1024,384]{1,0:T(8,128)(2,1)} custom-call(f32[64,4,128]{2,1,0:T(4,128)S(1)} %all-to-all-done.2.back, f32[2,1024,384]{2,1,0:T(8,128)} %copy-done, f32[2,1024,128]{2,1,0:T(8,128)} %copy-done.3, f32[2,1024,384]{2,1,0:T(8,128)} %copy-done.2, bf16[2,1024,1024]{2,1,0:T(8,128)(2,1)} %get-tuple-element.31.turned), custom_call_target="tpu_custom_call" | custom-call | flops 2214592512 | bytes 11665408 | tf_op jit(solution)/shard_map/pallas_call | solution.py:49
  97.4 6.0 %all-to-all-start.3 = ((bf16[32,32,384]{2,1,0:T(8,128)(2,1)}), bf16[32,32,384]{2,1,0:T(8,128)(2,1)}, u32[]{:S(2)}, u32[]{:S(2)}) async-start(bf16[32,32,384]{2,1,0:T(8,128)(2,1)} %bitcast.2), calls=%async_computation.3 | async-start | bytes 1572864 | tf_op jit(solution)/shard_map/all_to_all | solution.py:318
  103.4 2.8 %shard_map.56 = f32[1024,128]{1,0:T(8,128)} custom-call(s32[1]{0:T(128)} %bitcast.core, f32[64,4,128]{2,1,0:T(4,128)S(1)} %all-to-all-done.2.back, f32[128,128]{1,0:T(8,128)S(1)} %get-tuple-element.29.early, f32[2,1024,384]{2,1,0:T(8,128)S(1)} %copy-done.1), custom_call_target="tpu_custom_call" | custom-call | flops 1207959552 | bytes 3342340 | tf_op jit(solution)/shard_map/pallas_call | solution.py:49
  106.2 18.5 %all-to-all-done.3 = bf16[32,32,384]{2,1,0:T(8,128)(2,1)} async-done(((bf16[32,32,384]{2,1,0:T(8,128)(2,1)}), bf16[32,32,384]{2,1,0:T(8,128)(2,1)}, u32[]{:S(2)}, u32[]{:S(2)}) %all-to-all-start.3) | async-done | bytes 786464 | tf_op jit(solution)/shard_map/all_to_all | solution.py:318
  124.6 1.3 convert_reduce_fusion
  (23 shorter events, 0.7 us)
Async XLA Ops:
  0.6 22.0 %collective-permute-start = (bf16[1024,2048]{1,0:T(8,128)(2,1)}, bf16[1024,2048]{1,0:T(8,128)(2,1)}, u32[]{:S(2)}, u32[]{:S(2)}) collective-permute-start(bf16[1024,2048]{1,0:T(8,128)(2,1)} %hidden.1), channel_id=1, source_target_pairs={{0,8},{8,0},{1,9},{9,1},{2,10},{10,2},{3,11},{11,3},{4,12},{12,4},... | collective-permute-start | bytes 12582920 | tf_op jit(solution)/shard_map/ppermute | solution.py:252
  9.4 0.7 copy-start.13
  11.1 29.6 %all-to-all-start = ((bf16[32,32,384]{2,1,0:T(8,128)(2,1)}), bf16[32,32,384]{2,1,0:T(8,128)(2,1)S(1)}, u32[]{:S(2)}, u32[]{:S(2)}) async-start(bf16[32,32,384]{2,1,0:T(8,128)(2,1)} %shard_map.50), calls=%async_computation | async-start | bytes 1572864 | tf_op jit(solution)/shard_map/all_to_all | solution.py:251
  18.6 4.0 %collective-permute-start.1 = (f32[1024,128]{1,0:T(8,128)}, f32[1024,128]{1,0:T(8,128)S(1)}, u32[]{:S(2)}, u32[]{:S(2)}) collective-permute-start(f32[1024,128]{1,0:T(8,128)} %cot.1), channel_id=1, source_target_pairs={{0,8},{8,0},{1,9},{9,1},{2,10},{10,2},{3,11},{11,3},{4,12},{12,4},... | collective-permute-start | bytes 1572872 | tf_op jit(solution)/shard_map/ppermute | solution.py:253
  22.7 1.0 copy-start.14
  31.6 1.0 copy-start.3
  32.6 2.0 %copy-start.7 = (bf16[2,1024,1024]{2,1,0:T(8,128)(2,1)}, bf16[2,1024,1024]{2,1,0:T(8,128)(2,1)S(1)}, u32[]{:S(2)}) copy-start(bf16[2,1024,1024]{2,1,0:T(8,128)(2,1)S(1)} %get-tuple-element.21.far) | copy-start | bytes 12582916
  34.7 2.0 %copy-start.9 = (bf16[2,1024,1024]{2,1,0:T(8,128)(2,1)}, bf16[2,1024,1024]{2,1,0:T(8,128)(2,1)S(1)}, u32[]{:S(2)}) copy-start(bf16[2,1024,1024]{2,1,0:T(8,128)(2,1)S(1)} %get-tuple-element.23.near) | copy-start | bytes 12582916
  40.8 8.1 %copy-start.4 = (f32[2,1024,128]{2,1,0:T(8,128)S(1)}, f32[2,1024,128]{2,1,0:T(8,128)}, u32[]{:S(2)}) copy-start(f32[2,1024,128]{2,1,0:T(8,128)} %copy-done.3) | copy-start | bytes 3145732
  40.8 8.1 %copy-start.8 = (bf16[2,1024,1024]{2,1,0:T(8,128)(2,1)S(1)}, bf16[2,1024,1024]{2,1,0:T(8,128)(2,1)}, u32[]{:S(2)}) copy-start(bf16[2,1024,1024]{2,1,0:T(8,128)(2,1)} %copy-done.7) | copy-start | bytes 12582916
  40.8 8.1 %collective-permute-start.2 = (bf16[32,32,384]{2,1,0:T(8,128)(2,1)S(1)}, bf16[32,32,384]{2,1,0:T(8,128)(2,1)S(1)}, u32[]{:S(2)}, u32[]{:S(2)}) collective-permute-start(bf16[32,32,384]{2,1,0:T(8,128)(2,1)S(1)} %all-to-all-done.mine), channel_id=1, source_target_pairs={{0,8},{8,0},{1,9},{9,1},{2,10},{10,2},{3,11},{11,3},{4,12},{12,4},... | collective-permute-start | bytes 2359304 | tf_op jit(solution)/shard_map/ppermute | solution.py:266
  44.3 2.2 %copy-start.10 = (bf16[2,1024,1024]{2,1,0:T(8,128)(2,1)S(1)}, bf16[2,1024,1024]{2,1,0:T(8,128)(2,1)}, u32[]{:S(2)}) copy-start(bf16[2,1024,1024]{2,1,0:T(8,128)(2,1)} %copy-done.9) | copy-start | bytes 12582916
  53.6 25.0 %copy-start = (f32[2,1024,384]{2,1,0:T(8,128)}, f32[2,1024,384]{2,1,0:T(8,128)S(1)}, u32[]{:S(2)}) copy-start(f32[2,1024,384]{2,1,0:T(8,128)S(1)} %get-tuple-element.26.proj) | copy-start | bytes 9437188
  53.6 14.1 %all-to-all-start.1 = ((f32[32,4,128]{2,1,0:T(4,128)}), f32[32,4,128]{2,1,0:T(4,128)S(1)}, u32[]{:S(2)}, u32[]{:S(2)}) async-start(f32[32,4,128]{2,1,0:T(4,128)} %get-tuple-element.25), calls=%async_computation.1 | async-start | bytes 131072 | tf_op jit(solution)/shard_map/all_to_all | solution.py:278
  59.0 1.2 copy-start.5
  66.0 1.8 %copy-start.11 = (f32[2,1024,384]{2,1,0:T(8,128)}, f32[2,1024,384]{2,1,0:T(8,128)S(1)}, u32[]{:S(2)}) copy-start(f32[2,1024,384]{2,1,0:T(8,128)S(1)} %get-tuple-element.30.dlocal) | copy-start | bytes 9437188
  68.4 21.3 %all-to-all-start.2 = ((f32[64,4,128]{2,1,0:T(4,128)}), f32[64,4,128]{2,1,0:T(4,128)S(1)}, u32[]{:S(2)}, u32[]{:S(2)}) async-start(f32[64,4,128]{2,1,0:T(4,128)} %shard_map.55), calls=%async_computation.2 | async-start | bytes 262144 | tf_op jit(solution)/shard_map/all_to_all | solution.py:291
  78.6 1.2 copy-start.6
  79.9 1.9 %copy-start.12 = (f32[2,1024,384]{2,1,0:T(8,128)S(1)}, f32[2,1024,384]{2,1,0:T(8,128)}, u32[]{:S(2)}) copy-start(f32[2,1024,384]{2,1,0:T(8,128)} %copy-done.11) | copy-start | bytes 9437188
  84.2 1.8 %copy-start.2 = (f32[2,1024,384]{2,1,0:T(8,128)}, f32[2,1024,384]{2,1,0:T(8,128)S(1)}, u32[]{:S(2)}) copy-start(f32[2,1024,384]{2,1,0:T(8,128)S(1)} %shard_map.57.dlocal) | copy-start | bytes 9437188
  86.0 17.4 %copy-start.1 = (f32[2,1024,384]{2,1,0:T(8,128)S(1)}, f32[2,1024,384]{2,1,0:T(8,128)}, u32[]{:S(2)}) copy-start(f32[2,1024,384]{2,1,0:T(8,128)} %copy-done) | copy-start | bytes 9437188
  97.4 27.3 %all-to-all-start.3 = ((bf16[32,32,384]{2,1,0:T(8,128)(2,1)}), bf16[32,32,384]{2,1,0:T(8,128)(2,1)}, u32[]{:S(2)}, u32[]{:S(2)}) async-start(bf16[32,32,384]{2,1,0:T(8,128)(2,1)} %bitcast.2), calls=%async_computation.3 | async-start | bytes 1572864 | tf_op jit(solution)/shard_map/all_to_all | solution.py:318

commit v4 on v2

v4 whole, which is shorter than its diff:
```python
import functools

import jax
import jax.numpy as jnp
from jax import lax
from jax.experimental import pallas as pl
from jax.experimental.pallas import tpu as pltpu
from jax.sharding import Mesh, PartitionSpec as P

HD = 128
BLOCK = 256
CORES = 2
MIB = 1 << 20

SWAP = [(0, 1), (1, 0)]
CTX = ("chip", "core")
F32 = jnp.float32
BF16 = jnp.bfloat16

PLAIN = (((1,), (0,)), ((), ()))
ROWS = (((1,), (1,)), ((), ()))
COLS = (((0,), (0,)), ((), ()))


def mxu(a, b, dims=PLAIN):
    return lax.dot_general(a, b, dims, preferred_element_type=F32)


def split(x):
    high = x.astype(BF16)
    return high, (x - high.astype(F32)).astype(BF16)


def beside(x):
    return jnp.concatenate(split(x), axis=1)


def doubled(x):
    both = beside(x)
    return jnp.concatenate([both, both], axis=0)


def folded(out):
    width = out.shape[1] // 2
    return out[:, :width] + out[:, width:]


def times(left, right):
    return folded(mxu(left, right))


def gram(left, right):
    out = folded(mxu(left, right, COLS))
    height = out.shape[0] // 2
    return out[:height] + out[height:]


def cross(left, right):
    high, low = split(right)
    return mxu(left, jnp.concatenate([high, high], axis=1), ROWS) + mxu(
        left, jnp.concatenate([low, low], axis=1), ROWS
    )


HBM = pl.BlockSpec(memory_space=pltpu.HBM)
VMEM = pl.BlockSpec(memory_space=pltpu.VMEM)
SMEM = pl.BlockSpec(memory_space=pltpu.SMEM)


def vmem(dims, dtype=F32):
    return jax.ShapeDtypeStruct(dims, dtype), VMEM


def hbm(dims, dtype=F32):
    return pltpu.HBM(dims, dtype), VMEM


def direct(dims, dtype=F32):
    return pltpu.HBM(dims, dtype), HBM


def call(body, outs, args, flops, limit, specs, scratch=()):
    size = sum(a.size * a.dtype.itemsize for a in args)
    args = [
        pltpu.with_memory_space_constraint(a, pltpu.HBM) if spec is HBM else a
        for a, spec in zip(args, specs)
    ]
    return pl.pallas_call(
        body,
        out_shape=[kind for kind, _ in outs],
        in_specs=specs,
        out_specs=[spec for _, spec in outs],
        scratch_shapes=list(scratch),
        cost_estimate=pl.CostEstimate(flops=flops, bytes_accessed=size, transcendentals=0),
        compiler_params=pltpu.CompilerParams(vmem_limit_bytes=limit * MIB),
    )(*args)


def chunks(total):
    return [slice(start, start + BLOCK) for start in range(0, total, BLOCK)]


def fetched(source, target, sems):
    loads = [
        pltpu.make_async_copy(source.at[rows, :], target.at[rows, :], sems.at[index])
        for index, rows in enumerate(chunks(source.shape[0]))
    ]
    for load in loads:
        load.start()
    return loads


def causal():
    at = lax.broadcasted_iota(jnp.int32, (BLOCK, BLOCK), 0)
    return at >= lax.broadcasted_iota(jnp.int32, (BLOCK, BLOCK), 1)


def spread_kernel(weight, copies, sems):
    copying = [
        pltpu.make_async_copy(weight, copies.at[chip], sems.at[chip])
        for chip in range(copies.shape[0])
    ]
    for each in copying:
        each.start()
    for each in copying:
        each.wait()


def turn_kernel(core, hidden, keep, give):
    first = core[0] == 0
    group = keep.shape[1]
    for column in range(hidden.shape[1] // HD):
        turned = hidden[:, column * HD : (column + 1) * HD].T
        for pair in range(HD // (CORES * group)):
            at = pair * CORES * group
            even = turned[at : at + group]
            odd = turned[at + group : at + CORES * group]
            chip = column * (HD // (CORES * group)) + pair
            keep[chip] = jnp.where(first, even, odd)
            give[chip] = jnp.where(first, odd, even)


def project_kernel(core, hidden, mine, other, cotangent, query, kv, parts, rows_in, weight, sems):
    loads = fetched(hidden, rows_in, sems)
    place = core[0]
    chips, group, columns = mine.shape
    for chip in range(chips):
        weight[2 * chip + place] = mine[chip]
        weight[2 * chip + 1 - place] = other[chip]
    whole = weight[...].reshape(chips * CORES * group, columns)
    kv_state = jnp.zeros((HD, HD), F32)
    qg_state = jnp.zeros((HD, HD), F32)
    for load, rows in zip(loads, chunks(hidden.shape[0])):
        load.wait()
        part = mxu(rows_in[rows, :], whole)
        query[rows, :] = part[:, :HD]
        kv[rows, :] = part[:, HD:]
        kv_state += gram(beside(part[:, HD : 2 * HD]), beside(part[:, 2 * HD :]))
        qg_state += gram(beside(part[:, :HD]), beside(cotangent[rows, :]))
    piece = HD // chips
    for chip in range(chips):
        parts[2 * chip] = kv_state[chip * piece : (chip + 1) * piece]
        parts[2 * chip + 1] = qg_state[chip * piece : (chip + 1) * piece]


def local_kernel(query, kv, cotangent, dlocal):
    mask = causal()
    order = chunks(query.shape[0])
    state = jnp.zeros((HD, HD), F32)
    for rows in order:
        keys, values = kv[rows, :HD], kv[rows, HD:]
        queries, cot = beside(query[rows, :]), beside(cotangent[rows, :])
        scores = jnp.where(mask, cross(queries, keys), 0.0)
        dmat = jnp.where(mask, cross(cot, values), 0.0)
        dquery = times(beside(dmat), doubled(keys))
        if rows is not order[0]:
            dquery += times(cot, doubled(state.T))
        dlocal[rows, 0:HD] = dquery
        dlocal[rows, HD : 2 * HD] = gram(beside(dmat), queries)
        dlocal[rows, 2 * HD :] = gram(beside(scores), cot)
        if rows is not order[-1]:
            state += gram(beside(keys), beside(values))
    state = jnp.zeros((HD, HD), F32)
    for later, rows in zip(order[:0:-1], order[-2::-1]):
        state += gram(beside(query[later, :]), beside(cotangent[later, :]))
        dlocal[rows, HD : 2 * HD] += times(beside(kv[rows, HD:]), doubled(state.T))
        dlocal[rows, 2 * HD :] += times(beside(kv[rows, :HD]), doubled(state))


def scan_kernel(core, pieces, sums):
    devices = pieces.shape[0]
    flip = core[0] == 1
    total = jnp.zeros(pieces.shape[1:], F32)
    for step in range(devices):
        source = jnp.where(flip, devices - 1 - step, step)
        sums[source] = total
        total += pieces[source]


def joined(back, which, states):
    chips, piece = back.shape[0] // CORES, back.shape[1]
    for chip in range(chips):
        states[which, chip * piece : (chip + 1) * piece, :] = back[CORES * chip + which]
    return states[which]


def dproj_kernel(scale, back, kv, cotangent, dlocal, dproj, states):
    before, after = joined(back, 0, states), joined(back, 1, states)
    prefix, suffix, turned = doubled(before.T), doubled(after), doubled(after.T)
    for rows in chunks(kv.shape[0]):
        for j, term in enumerate(
            (
                times(beside(cotangent[rows, :]), prefix),
                times(beside(kv[rows, HD:]), turned),
                times(beside(kv[rows, :HD]), suffix),
            )
        ):
            columns = slice(j * HD, (j + 1) * HD)
            dproj[rows, columns] = (scale * (dlocal[rows, columns] + term)).astype(BF16)


def attended_kernel(scale, back, query, kv, attended, states):
    state = joined(back, 0, states)
    mask = causal()
    for rows in chunks(query.shape[0]):
        keys, values = kv[rows, :HD], kv[rows, HD:]
        queries = beside(query[rows, :])
        scores = jnp.where(mask, cross(queries, keys), 0.0)
        attended[rows, :] = scale * (
            times(beside(scores), doubled(values)) + times(queries, doubled(state))
        )
        state += gram(beside(keys), beside(values))


def own_kernel(turned, dproj, product):
    for rows in chunks(turned.shape[0]):
        product[rows, :] = mxu(turned[rows, :], dproj[...])


def total_kernel(turned, dproj, product, total, rows_in, sems):
    loads = fetched(turned, rows_in, sems)
    for load, rows in zip(loads, chunks(turned.shape[0])):
        load.wait()
        total[rows, :] = (product[rows, :] + mxu(rows_in[rows, :], dproj[...])).astype(BF16)


def sum_kernel(scale, landed, grad):
    total = landed[0].astype(F32)
    for chip in range(1, landed.shape[0]):
        total += landed[chip].astype(F32)
    grad[...] = scale * total


def local(hidden, qkv_weight, out_grad):
    tokens, width = hidden.shape
    group, columns = qkv_weight.shape
    chips = lax.axis_size("chip")
    devices = chips * CORES
    piece = HD // chips
    total_tokens = tokens * devices
    scale = float(HD * total_tokens) ** (-0.5)
    grad_scale = float(total_tokens) ** (-0.5)
    core = lax.axis_index("core").astype(jnp.int32).reshape(1)
    half = width // CORES
    square = tokens * HD * HD
    states = [pltpu.VMEM((2, HD, HD), F32)]

    (copies,) = call(
        spread_kernel,
        [direct((chips, group, columns), BF16)],
        [qkv_weight],
        1024,
        8,
        [HBM],
        [pltpu.SemaphoreType.DMA((chips,))],
    )
    mine = lax.all_to_all(copies, "chip", 0, 0, tiled=True)
    keep, give = call(
        turn_kernel,
        [hbm((chips, group, tokens), BF16)] * 2,
        [core, hidden],
        tokens * width * 1024,
        24,
        [SMEM, VMEM],
    )
    mine, keep, give = lax.optimization_barrier((mine, keep, give))
    keep, give = keep.reshape(half, tokens), give.reshape(half, tokens)
    taken = lax.ppermute(give, "core", SWAP)
    other = lax.ppermute(mine, "core", SWAP)

    query, kv, parts = call(
        project_kernel,
        [hbm((tokens, HD)), vmem((tokens, 2 * HD)), vmem((devices, piece, HD))],
        [core, hidden, mine, other, out_grad],
        2 * tokens * width * columns + 16 * square,
        32,
        [SMEM, HBM, VMEM, VMEM, VMEM],
        [
            pltpu.VMEM((tokens, width), BF16),
            pltpu.VMEM((devices, group, columns), BF16),
            pltpu.SemaphoreType.DMA((tokens // BLOCK,)),
        ],
    )
    pieces = lax.all_to_all(parts, CTX, 0, 0, tiled=True)
    (dlocal,) = call(
        local_kernel,
        [vmem((tokens, columns))],
        [query, kv, out_grad],
        15 * 6 * square,
        24,
        [VMEM] * 3,
    )
    pieces, dlocal = lax.optimization_barrier((pieces, dlocal))
    (sums,) = call(
        scan_kernel, [vmem(parts.shape)], [core, pieces], devices * HD * HD, 8, [SMEM, VMEM]
    )
    back = lax.all_to_all(sums, CTX, 0, 0, tiled=True)

    (dproj,) = call(
        functools.partial(dproj_kernel, scale),
        [vmem((tokens, columns), BF16)],
        [back, kv, out_grad, dlocal],
        24 * square,
        24,
        [VMEM] * 4,
        states,
    )
    theirs = lax.ppermute(dproj, "core", SWAP)
    (product,) = call(
        own_kernel,
        [vmem((half, columns))],
        [keep, dproj],
        2 * half * tokens * columns,
        24,
        [VMEM] * 2,
    )
    (total,) = call(
        total_kernel,
        [hbm((half, columns), BF16)],
        [taken, theirs, product],
        2 * half * tokens * columns,
        24,
        [HBM, VMEM, VMEM],
        [pltpu.VMEM((half, tokens), BF16), pltpu.SemaphoreType.DMA((half // BLOCK,))],
    )
    landed = lax.all_to_all(total.reshape(chips, group, columns), "chip", 0, 0, tiled=True)
    (attended,) = call(
        functools.partial(attended_kernel, scale),
        [hbm((tokens, HD))],
        [back, query, kv],
        6 * 6 * square,
        24,
        [VMEM] * 3,
        states,
    )
    (grad,) = call(
        functools.partial(sum_kernel, grad_scale),
        [hbm((group, columns))],
        [landed],
        half * columns,
        16,
        [VMEM],
    )
    return attended, grad


def solution(mesh):
    chips, heads = mesh.shape["ctx"] // CORES, mesh.shape["head"]
    fine = Mesh(mesh.devices.reshape(chips, CORES, heads), ("chip", "core", "head"))
    return jax.shard_map(
        local,
        mesh=fine,
        in_specs=(P(CTX, None), P(CTX, "head"), P(CTX, "head")),
        out_specs=(P(CTX, "head"), P(CTX, "head")),
        check_vma=False,
    )
```

time: 124 us -> 141 us (1.14)
  Pallas kernels: 17.9 us -> 46.1 us
  local copies, waits for them, and re-layouts: 14 us -> 3.23 us
  waiting for transfers between devices: 40.4 us -> 42.3 us
  blocking collectives: 16.4 us -> 14.9 us
    pallas_call x8 -> x10, Pallas kernels: 17.9 us -> 46.1 us  [call(): pl.pallas_call(body, out_shape=[kind for kind, _ in outs], in_specs=specs...]
    unnamed x20 -> x10, local copies, waits for them, and re-layouts: 12.3 us -> 3.23 us
    all_to_all x1, waiting for transfers between devices: 4.78 us -> 6.86 us  [local(): pieces = lax.all_to_all(parts, CTX, 0, 0, tiled=True)]
    broadcast_in_dim x1 -> x0, local copies, waits for them, and re-layouts: 1.7 us -> none  [local(): spread = jnp.broadcast_to(qkv_weight[None], (chips, group, columns))]
    all_to_all x1, blocking collectives: 16.4 us -> 14.9 us  [local(): back = lax.all_to_all(sums, CTX, 0, 0, tiled=True)]
where the time goes in v4:
time: 141 us; the launch traced here: 140 us
  Pallas kernels  46.1 us (33%)
  waiting for transfers between devices  42.3 us (30%)
  starting transfers between devices  32.5 us (23%)
  blocking collectives  14.9 us (11%)
  local copies, waits for them, and re-layouts  3.23 us (2%)
    pallas_call x10, Pallas kernels, call(): pl.pallas_call(body, out_shape=[kind for kind, _ in outs], in_specs=specs...  46.1 us
    all_to_all x1, waiting for transfers between devices, local(): lax.all_to_all(total.reshape(chips, group, columns), 'chip', 0, 0, tiled=...  19.2 us
    all_to_all x1, waiting for transfers between devices, local(): mine = lax.all_to_all(copies, 'chip', 0, 0, tiled=True)  15.7 us
    all_to_all x1, blocking collectives, local(): back = lax.all_to_all(sums, CTX, 0, 0, tiled=True)  14.9 us
    all_to_all x1, starting transfers between devices, local(): mine = lax.all_to_all(copies, 'chip', 0, 0, tiled=True)  13.7 us
    all_to_all x1, waiting for transfers between devices, local(): pieces = lax.all_to_all(parts, CTX, 0, 0, tiled=True)  6.86 us
    all_to_all x1, starting transfers between devices, local(): pieces = lax.all_to_all(parts, CTX, 0, 0, tiled=True)  5.76 us
    ppermute x1, starting transfers between devices, local(): other = lax.ppermute(mine, 'core', SWAP)  4.72 us
  transfers between devices with their start and end apart: 6, of which 4 were waited for; matrix products, arithmetic and copies ran while one was open for 0% of the time, Pallas kernels for 12%

profile of v4, /device:TPU:1, one launch (start us, length us, event | category | flops | bytes accessed | tf_op | source)
XLA Modules:
  0.0 139.9 jit_solution(7269156771784077358)
XLA Ops:
  0.6 25.2 %shard_map.50 = bf16[32,32,384]{2,1,0:T(8,128)(2,1)} custom-call(bf16[32,384]{1,0:T(8,128)(2,1)} %weight.1), custom_call_target="tpu_custom_call" | custom-call | flops 1024 | bytes 24576 | tf_op jit(solution)/shard_map/pallas_call | solution.py:88
  25.9 13.7 %all-to-all-start = ((bf16[32,32,384]{2,1,0:T(8,128)(2,1)}), bf16[32,32,384]{2,1,0:T(8,128)(2,1)S(1)}, u32[]{:S(2)}, u32[]{:S(2)}) async-start(bf16[32,32,384]{2,1,0:T(8,128)(2,1)} %shard_map.50), calls=%async_computation | async-start | bytes 1572864 | tf_op jit(solution)/shard_map/all_to_all | solution.py:277
  39.6 0.0 copy-start.2
  39.6 2.2 %copy-done.2 = bf16[1024,2048]{1,0:T(8,128)(2,1)S(1)} copy-done((bf16[1024,2048]{1,0:T(8,128)(2,1)S(1)}, bf16[1024,2048]{1,0:T(8,128)(2,1)}, u32[]{:S(2)}) %copy-start.2) | copy-done | bytes 4194328
  41.8 0.0 copy-start.1
  41.8 3.1 %shard_map.51 = (bf16[32,32,1024]{2,1,0:T(8,128)(2,1)}, bf16[32,32,1024]{2,1,0:T(8,128)(2,1)}) custom-call(s32[1]{0:T(128)} %bitcast.core, bf16[1024,2048]{1,0:T(8,128)(2,1)S(1)} %copy-done.2), custom_call_target="tpu_custom_call" | custom-call | flops 2147483648 | bytes 4194308 | tf_op jit(solution)/shard_map/pallas_call | solution.py:88
  44.9 15.7 %all-to-all-done.mine = bf16[32,32,384]{2,1,0:T(8,128)(2,1)S(1)} async-done(((bf16[32,32,384]{2,1,0:T(8,128)(2,1)}), bf16[32,32,384]{2,1,0:T(8,128)(2,1)S(1)}, u32[]{:S(2)}, u32[]{:S(2)}) %all-to-all-start) | async-done | bytes 786464 | tf_op jit(solution)/shard_map/all_to_all | solution.py:277
  60.7 4.7 %collective-permute-start = (bf16[32,32,384]{2,1,0:T(8,128)(2,1)S(1)}, bf16[32,32,384]{2,1,0:T(8,128)(2,1)S(1)}, u32[]{:S(2)}, u32[]{:S(2)}) collective-permute-start(bf16[32,32,384]{2,1,0:T(8,128)(2,1)S(1)} %all-to-all-done.mine), channel_id=1, source_target_pairs={{0,8},{8,0},{1,9},{9,1},{2,10},{10,2},{3,11},{11,3},{4,12},{12,4},... | collective-permute-start | bytes 2359304 | tf_op jit(solution)/shard_map/ppermute | solution.py:289
  65.4 1.9 %collective-permute-start.1 = (bf16[1024,1024]{1,0:T(8,128)(2,1)}, bf16[1024,1024]{1,0:T(8,128)(2,1)}, u32[]{:S(2)}, u32[]{:S(2)}) collective-permute-start(bf16[1024,1024]{1,0:T(8,128)(2,1)} %bitcast.6), channel_id=1, source_target_pairs={{0,8},{8,0},{1,9},{9,1},{2,10},{10,2},{3,11},{11,3},{4,12},{12,4},... | collective-permute-start | bytes 6291464 | tf_op jit(solution)/shard_map/ppermute | solution.py:288
  67.3 0.0 collective-permute-done.other
  67.3 0.0 copy-done.1
  67.3 5.8 %shard_map.52 = (f32[1024,128]{1,0:T(8,128)}, f32[1024,256]{1,0:T(8,128)S(1)}, f32[64,4,128]{2,1,0:T(4,128)}) custom-call(s32[1]{0:T(128)} %bitcast.core, bf16[1024,2048]{1,0:T(8,128)(2,1)} %hidden.3, bf16[32,32,384]{2,1,0:T(8,128)(2,1)S(1)} %all-to-all-done.mine, bf16[32,32,384]{2,1,0:T(8,128)(2,1)S(1)} %collective-permute-done.other, f32[1024,128]{1,0:T(8,128)S(1)} %copy-done.1), custom_call_target="tpu_custom_call" | custom-call | flops 1879048192 | bytes 6291460 | tf_op jit(solution)/shard_map/pallas_call | solution.py:88
  73.1 5.8 %all-to-all-start.1 = ((f32[64,4,128]{2,1,0:T(4,128)}), f32[64,4,128]{2,1,0:T(4,128)S(1)}, u32[]{:S(2)}, u32[]{:S(2)}) async-start(f32[64,4,128]{2,1,0:T(4,128)} %get-tuple-element.15), calls=%async_computation.1 | async-start | bytes 262144 | tf_op jit(solution)/shard_map/all_to_all | solution.py:304
  78.9 0.0 copy-start.3
  78.9 1.0 copy-done.3
  79.9 3.2 %shard_map.53.dlocal = f32[1024,384]{1,0:T(8,128)S(1)} custom-call(f32[1024,128]{1,0:T(8,128)S(1)} %copy-done.3, f32[1024,256]{1,0:T(8,128)S(1)} %get-tuple-element.17.kv, f32[1024,128]{1,0:T(8,128)S(1)} %copy-done.1), custom_call_target="tpu_custom_call" | custom-call | flops 1509949440 | bytes 2097152 | tf_op jit(solution)/shard_map/pallas_call | solution.py:88
  83.1 6.9 %all-to-all-done.1.pieces = f32[64,4,128]{2,1,0:T(4,128)S(1)} async-done(((f32[64,4,128]{2,1,0:T(4,128)}), f32[64,4,128]{2,1,0:T(4,128)S(1)}, u32[]{:S(2)}, u32[]{:S(2)}) %all-to-all-start.1) | async-done | bytes 131104 | tf_op jit(solution)/shard_map/all_to_all | solution.py:304
  90.0 0.1 shard_map.54
  90.1 14.9 %all_to_all.20.back = f32[64,4,128]{2,1,0:T(4,128)S(1)} all-to-all(f32[64,4,128]{2,1,0:T(4,128)S(1)} %shard_map.54), channel_id=1, replica_groups=mesh['chip'=32,'core'=2,'head'=8] {'chip','core'}, dimensions={0} | all-to-all | bytes 262144 | tf_op jit(solution)/shard_map/all_to_all | solution.py:317
  105.0 0.7 shard_map.56.dproj
  105.7 2.5 %collective-permute-start.2 = (bf16[1024,384]{1,0:T(8,128)(2,1)S(1)}, bf16[1024,384]{1,0:T(8,128)(2,1)S(1)}, u32[]{:S(2)}, u32[]{:S(2)}) collective-permute-start(bf16[1024,384]{1,0:T(8,128)(2,1)S(1)} %shard_map.56.dproj), channel_id=1, source_target_pairs={{0,8},{8,0},{1,9},{9,1},{2,10},{10,2},{3,11},{11,3},{4,12},{12,4},... | collective-permute-start | bytes 2359304 | tf_op jit(solution)/shard_map/ppermute | solution.py:328
  108.2 0.0 copy-done
  108.2 1.2 shard_map.57.product
  109.5 0.0 copy-start.4
  109.5 0.4 collective-permute-done.2.dproj
  109.9 0.0 collective-permute-done.1.turned
  109.9 3.7 %shard_map.58 = bf16[1024,384]{1,0:T(8,128)(2,1)} custom-call(bf16[1024,1024]{1,0:T(8,128)(2,1)} %collective-permute-done.1.turned, bf16[1024,384]{1,0:T(8,128)(2,1)S(1)} %collective-permute-done.2.dproj, f32[1024,384]{1,0:T(8,128)S(1)} %shard_map.57.product), custom_call_target="tpu_custom_call" | custom-call | flops 805306368 | bytes 4456448 | tf_op jit(solution)/shard_map/pallas_call | solution.py:88
  113.7 3.9 %all-to-all-start.3 = ((bf16[32,32,384]{2,1,0:T(8,128)(2,1)}), bf16[32,32,384]{2,1,0:T(8,128)(2,1)S(1)}, u32[]{:S(2)}, u32[]{:S(2)}) async-start(bf16[32,32,384]{2,1,0:T(8,128)(2,1)} %bitcast.5), calls=%async_computation.3 | async-start | bytes 1572864 | tf_op jit(solution)/shard_map/all_to_all | solution.py:346
  117.6 0.0 copy-done.4
  117.6 2.3 %shard_map.55 = f32[1024,128]{1,0:T(8,128)} custom-call(f32[64,4,128]{2,1,0:T(4,128)S(1)} %all_to_all.20.back, f32[1024,128]{1,0:T(8,128)S(1)} %copy-done.4, f32[1024,256]{1,0:T(8,128)S(1)} %get-tuple-element.17.kv), custom_call_target="tpu_custom_call" | custom-call | flops 603979776 | bytes 1703936 | tf_op jit(solution)/shard_map/pallas_call | solution.py:88
  119.9 19.2 %all-to-all-done.3.landed = bf16[32,32,384]{2,1,0:T(8,128)(2,1)S(1)} async-done(((bf16[32,32,384]{2,1,0:T(8,128)(2,1)}), bf16[32,32,384]{2,1,0:T(8,128)(2,1)S(1)}, u32[]{:S(2)}, u32[]{:S(2)}) %all-to-all-start.3) | async-done | bytes 786464 | tf_op jit(solution)/shard_map/all_to_all | solution.py:346
  139.2 0.7 shard_map.59
  (1 shorter events, 0.0 us)
Async XLA Ops:
  25.9 34.8 %all-to-all-start = ((bf16[32,32,384]{2,1,0:T(8,128)(2,1)}), bf16[32,32,384]{2,1,0:T(8,128)(2,1)S(1)}, u32[]{:S(2)}, u32[]{:S(2)}) async-start(bf16[32,32,384]{2,1,0:T(8,128)(2,1)} %shard_map.50), calls=%async_computation | async-start | bytes 1572864 | tf_op jit(solution)/shard_map/all_to_all | solution.py:277
  39.6 2.2 %copy-start.2 = (bf16[1024,2048]{1,0:T(8,128)(2,1)S(1)}, bf16[1024,2048]{1,0:T(8,128)(2,1)}, u32[]{:S(2)}) copy-start(bf16[1024,2048]{1,0:T(8,128)(2,1)} %hidden.3) | copy-start | bytes 12582916
  41.8 25.5 %copy-start.1 = (f32[1024,128]{1,0:T(8,128)S(1)}, f32[1024,128]{1,0:T(8,128)}, u32[]{:S(2)}) copy-start(f32[1024,128]{1,0:T(8,128)} %cotangent.5) | copy-start | bytes 1572868
  60.7 6.7 %collective-permute-start = (bf16[32,32,384]{2,1,0:T(8,128)(2,1)S(1)}, bf16[32,32,384]{2,1,0:T(8,128)(2,1)S(1)}, u32[]{:S(2)}, u32[]{:S(2)}) collective-permute-start(bf16[32,32,384]{2,1,0:T(8,128)(2,1)S(1)} %all-to-all-done.mine), channel_id=1, source_target_pairs={{0,8},{8,0},{1,9},{9,1},{2,10},{10,2},{3,11},{11,3},{4,12},{12,4},... | collective-permute-start | bytes 2359304 | tf_op jit(solution)/shard_map/ppermute | solution.py:289
  65.4 44.5 %collective-permute-start.1 = (bf16[1024,1024]{1,0:T(8,128)(2,1)}, bf16[1024,1024]{1,0:T(8,128)(2,1)}, u32[]{:S(2)}, u32[]{:S(2)}) collective-permute-start(bf16[1024,1024]{1,0:T(8,128)(2,1)} %bitcast.6), channel_id=1, source_target_pairs={{0,8},{8,0},{1,9},{9,1},{2,10},{10,2},{3,11},{11,3},{4,12},{12,4},... | collective-permute-start | bytes 6291464 | tf_op jit(solution)/shard_map/ppermute | solution.py:288
  73.1 16.9 %all-to-all-start.1 = ((f32[64,4,128]{2,1,0:T(4,128)}), f32[64,4,128]{2,1,0:T(4,128)S(1)}, u32[]{:S(2)}, u32[]{:S(2)}) async-start(f32[64,4,128]{2,1,0:T(4,128)} %get-tuple-element.15), calls=%async_computation.1 | async-start | bytes 262144 | tf_op jit(solution)/shard_map/all_to_all | solution.py:304
  78.9 1.0 copy-start.3
  105.0 3.2 %copy-start = (bf16[32,32,1024]{2,1,0:T(8,128)(2,1)S(1)}, bf16[32,32,1024]{2,1,0:T(8,128)(2,1)}, u32[]{:S(2)}) copy-start(bf16[32,32,1024]{2,1,0:T(8,128)(2,1)} %get-tuple-element.21) | copy-start | bytes 6291460
  105.7 4.2 %collective-permute-start.2 = (bf16[1024,384]{1,0:T(8,128)(2,1)S(1)}, bf16[1024,384]{1,0:T(8,128)(2,1)S(1)}, u32[]{:S(2)}, u32[]{:S(2)}) collective-permute-start(bf16[1024,384]{1,0:T(8,128)(2,1)S(1)} %shard_map.56.dproj), channel_id=1, source_target_pairs={{0,8},{8,0},{1,9},{9,1},{2,10},{10,2},{3,11},{11,3},{4,12},{12,4},... | collective-permute-start | bytes 2359304 | tf_op jit(solution)/shard_map/ppermute | solution.py:328
  109.5 8.1 %copy-start.4 = (f32[1024,128]{1,0:T(8,128)S(1)}, f32[1024,128]{1,0:T(8,128)}, u32[]{:S(2)}) copy-start(f32[1024,128]{1,0:T(8,128)} %get-tuple-element.16.query) | copy-start | bytes 1572868
  113.7 25.5 %all-to-all-start.3 = ((bf16[32,32,384]{2,1,0:T(8,128)(2,1)}), bf16[32,32,384]{2,1,0:T(8,128)(2,1)S(1)}, u32[]{:S(2)}, u32[]{:S(2)}) async-start(bf16[32,32,384]{2,1,0:T(8,128)(2,1)} %bitcast.5), calls=%async_computation.3 | async-start | bytes 1572864 | tf_op jit(solution)/shard_map/all_to_all | solution.py:346

commit v5 on v4

--- a/solution.py
+++ b/solution.py
@@ -115,18 +115,13 @@
     return at >= lax.broadcasted_iota(jnp.int32, (BLOCK, BLOCK), 1)
 
 
-def spread_kernel(weight, copies, sems):
-    copying = [
-        pltpu.make_async_copy(weight, copies.at[chip], sems.at[chip])
-        for chip in range(copies.shape[0])
-    ]
-    for each in copying:
-        each.start()
-    for each in copying:
-        each.wait()
-
-
-def turn_kernel(core, hidden, keep, give):
+def spread_kernel(weight, copies):
+    for chip in range(copies.shape[0]):
+        copies[chip] = weight[...]
+
+
+def turn_kernel(core, hidden, keep, give, head):
+    head[...] = hidden[: head.shape[0], :]
     first = core[0] == 0
     group = keep.shape[1]
     for column in range(hidden.shape[1] // HD):
@@ -140,8 +135,12 @@
             give[chip] = jnp.where(first, odd, even)
 
 
-def project_kernel(core, hidden, mine, other, cotangent, query, kv, parts, rows_in, weight, sems):
-    loads = fetched(hidden, rows_in, sems)
+def project_kernel(core, hidden, head, mine, other, cotangent, query, kv, parts,
+                   tail, weight, proj, load_sem, sems):
+    ahead = head.shape[0]
+    load = pltpu.make_async_copy(hidden.at[ahead:, :], tail, load_sem)
+    load.start()
+    stores = []
     place = core[0]
     chips, group, columns = mine.shape
     for chip in range(chips):
@@ -150,17 +149,28 @@
     whole = weight[...].reshape(chips * CORES * group, columns)
     kv_state = jnp.zeros((HD, HD), F32)
     qg_state = jnp.zeros((HD, HD), F32)
-    for load, rows in zip(loads, chunks(hidden.shape[0])):
-        load.wait()
-        part = mxu(rows_in[rows, :], whole)
-        query[rows, :] = part[:, :HD]
-        kv[rows, :] = part[:, HD:]
-        kv_state += gram(beside(part[:, HD : 2 * HD]), beside(part[:, 2 * HD :]))
-        qg_state += gram(beside(part[:, :HD]), beside(cotangent[rows, :]))
+    for base, held in ((0, head), (ahead, tail)):
+        if base:
+            load.wait()
+        for rows in chunks(held.shape[0]):
+            part = mxu(held[rows, :], whole)
+            to = slice(base + rows.start, base + rows.stop)
+            proj[to, :] = part
+            for which, target, columns in ((0, query, pl.ds(0, HD)), (1, kv, pl.ds(HD, 2 * HD))):
+                stores.append(
+                    pltpu.make_async_copy(
+                        proj.at[to, columns], target.at[to, :], sems.at[len(stores) // 2, which]
+                    )
+                )
+                stores[-1].start()
+            kv_state += gram(beside(part[:, HD : 2 * HD]), beside(part[:, 2 * HD :]))
+            qg_state += gram(beside(part[:, :HD]), beside(cotangent[to, :]))
     piece = HD // chips
     for chip in range(chips):
         parts[2 * chip] = kv_state[chip * piece : (chip + 1) * piece]
         parts[2 * chip + 1] = qg_state[chip * piece : (chip + 1) * piece]
+    for store in stores:
+        store.wait()
 
 
 def local_kernel(query, kv, cotangent, dlocal):
@@ -232,16 +242,22 @@
         state += gram(beside(keys), beside(values))
 
 
-def own_kernel(turned, dproj, product):
+def own_kernel(turned, dproj, taken, product, held, sems):
+    loads = fetched(taken, held, sems)
     for rows in chunks(turned.shape[0]):
         product[rows, :] = mxu(turned[rows, :], dproj[...])
-
-
-def total_kernel(turned, dproj, product, total, rows_in, sems):
-    loads = fetched(turned, rows_in, sems)
-    for load, rows in zip(loads, chunks(turned.shape[0])):
+    for load in loads:
         load.wait()
-        total[rows, :] = (product[rows, :] + mxu(rows_in[rows, :], dproj[...])).astype(BF16)
+
+
+def total_kernel(turned, dproj, product, total, rows_out, sems):
+    stores = []
+    for index, rows in enumerate(chunks(turned.shape[0])):
+        rows_out[rows, :] = (product[rows, :] + mxu(turned[rows, :], dproj[...])).astype(BF16)
+        stores.append(pltpu.make_async_copy(rows_out.at[rows, :], total.at[rows, :], sems.at[index]))
+        stores[-1].start()
+    for store in stores:
+        store.wait()
 
 
 def sum_kernel(scale, landed, grad):
@@ -266,39 +282,35 @@
     states = [pltpu.VMEM((2, HD, HD), F32)]
 
     (copies,) = call(
-        spread_kernel,
-        [direct((chips, group, columns), BF16)],
-        [qkv_weight],
-        1024,
-        8,
-        [HBM],
-        [pltpu.SemaphoreType.DMA((chips,))],
+        spread_kernel, [vmem((chips, group, columns), BF16)], [qkv_weight], 1024, 8, [VMEM]
     )
     mine = lax.all_to_all(copies, "chip", 0, 0, tiled=True)
-    keep, give = call(
+    keep, give, head = call(
         turn_kernel,
-        [hbm((chips, group, tokens), BF16)] * 2,
+        [hbm((chips, group, tokens), BF16)] * 2 + [vmem((tokens // 2, width), BF16)],
         [core, hidden],
         tokens * width * 1024,
         24,
         [SMEM, VMEM],
     )
-    mine, keep, give = lax.optimization_barrier((mine, keep, give))
+    mine, keep, give, head = lax.optimization_barrier((mine, keep, give, head))
     keep, give = keep.reshape(half, tokens), give.reshape(half, tokens)
     taken = lax.ppermute(give, "core", SWAP)
     other = lax.ppermute(mine, "core", SWAP)
 
     query, kv, parts = call(
         project_kernel,
-        [hbm((tokens, HD)), vmem((tokens, 2 * HD)), vmem((devices, piece, HD))],
-        [core, hidden, mine, other, out_grad],
+        [direct((tokens, HD)), direct((tokens, 2 * HD)), vmem((devices, piece, HD))],
+        [core, hidden, head, mine, other, out_grad],
         2 * tokens * width * columns + 16 * square,
         32,
-        [SMEM, HBM, VMEM, VMEM, VMEM],
+        [SMEM, HBM, VMEM, VMEM, VMEM, VMEM],
         [
-            pltpu.VMEM((tokens, width), BF16),
+            pltpu.VMEM((tokens // 2, width), BF16),
             pltpu.VMEM((devices, group, columns), BF16),
-            pltpu.SemaphoreType.DMA((tokens // BLOCK,)),
+            pltpu.VMEM((tokens, columns), F32),
+            pltpu.SemaphoreType.DMA(()),
+            pltpu.SemaphoreType.DMA((tokens // BLOCK, 2)),
         ],
     )
     pieces = lax.all_to_all(parts, CTX, 0, 0, tiled=True)
@@ -326,22 +338,23 @@
         states,
     )
     theirs = lax.ppermute(dproj, "core", SWAP)
-    (product,) = call(
+    product, held = call(
         own_kernel,
-        [vmem((half, columns))],
-        [keep, dproj],
+        [vmem((half, columns)), (pltpu.VMEM((half, tokens), BF16), VMEM)],
+        [keep, dproj, taken],
         2 * half * tokens * columns,
         24,
-        [VMEM] * 2,
+        [VMEM, VMEM, HBM],
+        [pltpu.SemaphoreType.DMA((half // BLOCK,))],
     )
     (total,) = call(
         total_kernel,
-        [hbm((half, columns), BF16)],
-        [taken, theirs, product],
+        [direct((half, columns), BF16)],
+        [held, theirs, product],
         2 * half * tokens * columns,
         24,
-        [HBM, VMEM, VMEM],
-        [pltpu.VMEM((half, tokens), BF16), pltpu.SemaphoreType.DMA((half // BLOCK,))],
+        [VMEM] * 3,
+        [pltpu.VMEM((half, columns), BF16), pltpu.SemaphoreType.DMA((half // BLOCK,))],
     )
     landed = lax.all_to_all(total.reshape(chips, group, columns), "chip", 0, 0, tiled=True)
     (attended,) = call(

time: 141 us -> 117 us (0.83)
  Pallas kernels: 46.1 us -> 20.4 us
  local copies, waits for them, and re-layouts: 3.23 us -> 5.19 us
    pallas_call x10, Pallas kernels: 46.1 us -> 20.4 us  [call(): pl.pallas_call(body, out_shape=[kind for kind, _ in outs], in_specs=specs...]
    unnamed x10 -> x14, local copies, waits for them, and re-layouts: 3.23 us -> 5.19 us
  transfers between devices with their start and end apart: 6 -> 6, of which waited for: 4 -> 3; matrix products, arithmetic and copies ran while one was open for 0% -> 0% of each run, Pallas kernels for 12% -> 14%
where the time goes in v5:
time: 117 us; the launch traced here: 116 us
  waiting for transfers between devices  41.5 us (35%)
  starting transfers between devices  32.5 us (28%)
  Pallas kernels  20.4 us (17%)
  blocking collectives  15.6 us (13%)
  local copies, waits for them, and re-layouts  5.19 us (4%)
    pallas_call x10, Pallas kernels, call(): pl.pallas_call(body, out_shape=[kind for kind, _ in outs], in_specs=specs...  20.4 us
    all_to_all x1, waiting for transfers between devices, local(): lax.all_to_all(total.reshape(chips, group, columns), 'chip', 0, 0, tiled=...  20.2 us
    all_to_all x1, waiting for transfers between devices, local(): mine = lax.all_to_all(copies, 'chip', 0, 0, tiled=True)  15.7 us
    all_to_all x1, blocking collectives, local(): back = lax.all_to_all(sums, CTX, 0, 0, tiled=True)  15.6 us
    all_to_all x1, starting transfers between devices, local(): mine = lax.all_to_all(copies, 'chip', 0, 0, tiled=True)  13.7 us
    all_to_all x1, starting transfers between devices, local(): pieces = lax.all_to_all(parts, CTX, 0, 0, tiled=True)  5.76 us
    all_to_all x1, waiting for transfers between devices, local(): pieces = lax.all_to_all(parts, CTX, 0, 0, tiled=True)  5.64 us
    unnamed x14, local copies, waits for them, and re-layouts  5.19 us
  transfers between devices with their start and end apart: 6, of which 3 were waited for; matrix products, arithmetic and copies ran while one was open for 0% of the time, Pallas kernels for 14%

profile of v5, /device:TPU:1, one launch (start us, length us, event | category | flops | bytes accessed | tf_op | source)
XLA Modules:
  0.0 116.1 jit_solution(6725715731382316016)
XLA Ops:
  0.6 0.0 copy-start.4
  0.6 0.7 copy-done.4
  1.4 1.0 shard_map.50
  2.3 13.7 %all-to-all-start = ((bf16[32,32,384]{2,1,0:T(8,128)(2,1)}), bf16[32,32,384]{2,1,0:T(8,128)(2,1)S(1)}, u32[]{:S(2)}, u32[]{:S(2)}) async-start(bf16[32,32,384]{2,1,0:T(8,128)(2,1)} %shard_map.50), calls=%async_computation | async-start | bytes 1572864 | tf_op jit(solution)/shard_map/all_to_all | solution.py:287
  16.1 0.0 copy-start
  16.1 2.2 %copy-done = bf16[1024,2048]{1,0:T(8,128)(2,1)S(1)} copy-done((bf16[1024,2048]{1,0:T(8,128)(2,1)S(1)}, bf16[1024,2048]{1,0:T(8,128)(2,1)}, u32[]{:S(2)}) %copy-start) | copy-done | bytes 4194328
  18.3 3.2 %shard_map.51 = (bf16[32,32,1024]{2,1,0:T(8,128)(2,1)}, bf16[32,32,1024]{2,1,0:T(8,128)(2,1)}, bf16[512,2048]{1,0:T(8,128)(2,1)S(1)}) custom-call(s32[1]{0:T(128)} %bitcast.core, bf16[1024,2048]{1,0:T(8,128)(2,1)S(1)} %copy-done), custom_call_target="tpu_custom_call" | custom-call | flops 2147483648 | bytes 4194308 | tf_op jit(solution)/shard_map/pallas_call | solution.py:88
  21.5 15.7 %all-to-all-done.mine = bf16[32,32,384]{2,1,0:T(8,128)(2,1)S(1)} async-done(((bf16[32,32,384]{2,1,0:T(8,128)(2,1)}), bf16[32,32,384]{2,1,0:T(8,128)(2,1)S(1)}, u32[]{:S(2)}, u32[]{:S(2)}) %all-to-all-start) | async-done | bytes 786464 | tf_op jit(solution)/shard_map/all_to_all | solution.py:287
  37.1 4.7 %collective-permute-start = (bf16[32,32,384]{2,1,0:T(8,128)(2,1)S(1)}, bf16[32,32,384]{2,1,0:T(8,128)(2,1)S(1)}, u32[]{:S(2)}, u32[]{:S(2)}) collective-permute-start(bf16[32,32,384]{2,1,0:T(8,128)(2,1)S(1)} %all-to-all-done.mine), channel_id=1, source_target_pairs={{0,8},{8,0},{1,9},{9,1},{2,10},{10,2},{3,11},{11,3},{4,12},{12,4},... | collective-permute-start | bytes 2359304 | tf_op jit(solution)/shard_map/ppermute | solution.py:299
  41.9 1.9 %collective-permute-start.1 = (bf16[1024,1024]{1,0:T(8,128)(2,1)}, bf16[1024,1024]{1,0:T(8,128)(2,1)}, u32[]{:S(2)}, u32[]{:S(2)}) collective-permute-start(bf16[1024,1024]{1,0:T(8,128)(2,1)} %bitcast.6), channel_id=1, source_target_pairs={{0,8},{8,0},{1,9},{9,1},{2,10},{10,2},{3,11},{11,3},{4,12},{12,4},... | collective-permute-start | bytes 6291464 | tf_op jit(solution)/shard_map/ppermute | solution.py:298
  43.8 0.0 collective-permute-done.other
  43.8 0.0 copy-done.2
  43.8 5.0 %shard_map.52 = (f32[1024,128]{1,0:T(8,128)}, f32[1024,256]{1,0:T(8,128)}, f32[64,4,128]{2,1,0:T(4,128)}) custom-call(s32[1]{0:T(128)} %bitcast.core, bf16[1024,2048]{1,0:T(8,128)(2,1)} %hidden.3, bf16[512,2048]{1,0:T(8,128)(2,1)S(1)} %get-tuple-element.19.head, bf16[32,32,384]{2,1,0:T(8,128)(2,1)S(1)} %all-to-all-done.mine, ...), custom_call_target="tpu_custom_call" | custom-call | flops 1879048192 | bytes 8388612 | tf_op jit(solution)/shard_map/pallas_call | solution.py:88
  48.8 5.8 %all-to-all-start.1 = ((f32[64,4,128]{2,1,0:T(4,128)}), f32[64,4,128]{2,1,0:T(4,128)S(1)}, u32[]{:S(2)}, u32[]{:S(2)}) async-start(f32[64,4,128]{2,1,0:T(4,128)} %get-tuple-element.21), calls=%async_computation.1 | async-start | bytes 262144 | tf_op jit(solution)/shard_map/all_to_all | solution.py:316
  54.6 0.0 copy-start.3
  54.6 1.2 %copy-done.3 = f32[1024,256]{1,0:T(8,128)S(1)} copy-done((f32[1024,256]{1,0:T(8,128)S(1)}, f32[1024,256]{1,0:T(8,128)}, u32[]{:S(2)}) %copy-start.3) | copy-done | bytes 1048600
  55.8 1.0 copy-done.5
  56.9 3.2 %shard_map.53.dlocal = f32[1024,384]{1,0:T(8,128)S(1)} custom-call(f32[1024,128]{1,0:T(8,128)S(1)} %copy-done.5, f32[1024,256]{1,0:T(8,128)S(1)} %copy-done.3, f32[1024,128]{1,0:T(8,128)S(1)} %copy-done.2), custom_call_target="tpu_custom_call" | custom-call | flops 1509949440 | bytes 2097152 | tf_op jit(solution)/shard_map/pallas_call | solution.py:88
  60.1 5.6 %all-to-all-done.1.pieces = f32[64,4,128]{2,1,0:T(4,128)S(1)} async-done(((f32[64,4,128]{2,1,0:T(4,128)}), f32[64,4,128]{2,1,0:T(4,128)S(1)}, u32[]{:S(2)}, u32[]{:S(2)}) %all-to-all-start.1) | async-done | bytes 131104 | tf_op jit(solution)/shard_map/all_to_all | solution.py:316
  65.7 0.1 shard_map.54
  65.8 15.6 %all_to_all.20.back = f32[64,4,128]{2,1,0:T(4,128)S(1)} all-to-all(f32[64,4,128]{2,1,0:T(4,128)S(1)} %shard_map.54), channel_id=1, replica_groups=mesh['chip'=32,'core'=2,'head'=8] {'chip','core'}, dimensions={0} | all-to-all | bytes 262144 | tf_op jit(solution)/shard_map/all_to_all | solution.py:329
  81.4 0.7 shard_map.56.dproj
  82.1 2.5 %collective-permute-start.2 = (bf16[1024,384]{1,0:T(8,128)(2,1)S(1)}, bf16[1024,384]{1,0:T(8,128)(2,1)S(1)}, u32[]{:S(2)}, u32[]{:S(2)}) collective-permute-start(bf16[1024,384]{1,0:T(8,128)(2,1)S(1)} %shard_map.56.dproj), channel_id=1, source_target_pairs={{0,8},{8,0},{1,9},{9,1},{2,10},{10,2},{3,11},{11,3},{4,12},{12,4},... | collective-permute-start | bytes 2359304 | tf_op jit(solution)/shard_map/ppermute | solution.py:340
  84.6 0.0 collective-permute-done.1.taken
  84.6 2.2 %shard_map.57 = (f32[1024,384]{1,0:T(8,128)S(1)}, bf16[1024,1024]{1,0:T(8,128)(2,1)S(1)}) custom-call(bf16[1024,1024]{1,0:T(8,128)(2,1)S(1)} %bitcast.4, bf16[1024,384]{1,0:T(8,128)(2,1)S(1)} %shard_map.56.dproj, bf16[1024,1024]{1,0:T(8,128)(2,1)} %collective-permute-done.1.taken), custom_call_target="tpu_custom_call" | custom-call | flops 805306368 | bytes 4980736 | tf_op jit(solution)/shard_map/pallas_call | solution.py:88
  86.8 0.0 collective-permute-done.2.dproj
  86.9 0.0 copy-start.6
  86.9 2.0 %shard_map.58 = bf16[1024,384]{1,0:T(8,128)(2,1)} custom-call(bf16[1024,1024]{1,0:T(8,128)(2,1)S(1)} %get-tuple-element.28.turned, bf16[1024,384]{1,0:T(8,128)(2,1)S(1)} %collective-permute-done.2.dproj, f32[1024,384]{1,0:T(8,128)S(1)} %get-tuple-element.29.product), custom_call_target="tpu_custom_call" | custom-call | flops 805306368 | bytes 4456448 | tf_op jit(solution)/shard_map/pallas_call | solution.py:88
  88.8 3.9 %all-to-all-start.3 = ((bf16[32,32,384]{2,1,0:T(8,128)(2,1)}), bf16[32,32,384]{2,1,0:T(8,128)(2,1)S(1)}, u32[]{:S(2)}, u32[]{:S(2)}) async-start(bf16[32,32,384]{2,1,0:T(8,128)(2,1)} %bitcast.5), calls=%async_computation.3 | async-start | bytes 1572864 | tf_op jit(solution)/shard_map/all_to_all | solution.py:359
  92.8 2.3 %shard_map.55 = f32[1024,128]{1,0:T(8,128)} custom-call(f32[64,4,128]{2,1,0:T(4,128)S(1)} %all_to_all.20.back, f32[1024,128]{1,0:T(8,128)S(1)} %copy-done.6, f32[1024,256]{1,0:T(8,128)S(1)} %copy-done.3), custom_call_target="tpu_custom_call" | custom-call | flops 603979776 | bytes 1703936 | tf_op jit(solution)/shard_map/pallas_call | solution.py:88
  95.1 20.2 %all-to-all-done.3.landed = bf16[32,32,384]{2,1,0:T(8,128)(2,1)S(1)} async-done(((bf16[32,32,384]{2,1,0:T(8,128)(2,1)}), bf16[32,32,384]{2,1,0:T(8,128)(2,1)S(1)}, u32[]{:S(2)}, u32[]{:S(2)}) %all-to-all-start.3) | async-done | bytes 786464 | tf_op jit(solution)/shard_map/all_to_all | solution.py:359
  115.3 0.7 shard_map.59
  (5 shorter events, 0.0 us)
Async XLA Ops:
  0.6 0.7 copy-start.4
  2.3 34.8 %all-to-all-start = ((bf16[32,32,384]{2,1,0:T(8,128)(2,1)}), bf16[32,32,384]{2,1,0:T(8,128)(2,1)S(1)}, u32[]{:S(2)}, u32[]{:S(2)}) async-start(bf16[32,32,384]{2,1,0:T(8,128)(2,1)} %shard_map.50), calls=%async_computation | async-start | bytes 1572864 | tf_op jit(solution)/shard_map/all_to_all | solution.py:287
  16.1 2.2 %copy-start = (bf16[1024,2048]{1,0:T(8,128)(2,1)S(1)}, bf16[1024,2048]{1,0:T(8,128)(2,1)}, u32[]{:S(2)}) copy-start(bf16[1024,2048]{1,0:T(8,128)(2,1)} %hidden.3) | copy-start | bytes 12582916
  18.3 25.5 %copy-start.2 = (f32[1024,128]{1,0:T(8,128)S(1)}, f32[1024,128]{1,0:T(8,128)}, u32[]{:S(2)}) copy-start(f32[1024,128]{1,0:T(8,128)} %cotangent.5) | copy-start | bytes 1572868
  37.1 6.7 %collective-permute-start = (bf16[32,32,384]{2,1,0:T(8,128)(2,1)S(1)}, bf16[32,32,384]{2,1,0:T(8,128)(2,1)S(1)}, u32[]{:S(2)}, u32[]{:S(2)}) collective-permute-start(bf16[32,32,384]{2,1,0:T(8,128)(2,1)S(1)} %all-to-all-done.mine), channel_id=1, source_target_pairs={{0,8},{8,0},{1,9},{9,1},{2,10},{10,2},{3,11},{11,3},{4,12},{12,4},... | collective-permute-start | bytes 2359304 | tf_op jit(solution)/shard_map/ppermute | solution.py:299
  41.9 42.7 %collective-permute-start.1 = (bf16[1024,1024]{1,0:T(8,128)(2,1)}, bf16[1024,1024]{1,0:T(8,128)(2,1)}, u32[]{:S(2)}, u32[]{:S(2)}) collective-permute-start(bf16[1024,1024]{1,0:T(8,128)(2,1)} %bitcast.6), channel_id=1, source_target_pairs={{0,8},{8,0},{1,9},{9,1},{2,10},{10,2},{3,11},{11,3},{4,12},{12,4},... | collective-permute-start | bytes 6291464 | tf_op jit(solution)/shard_map/ppermute | solution.py:298
  48.8 16.9 %all-to-all-start.1 = ((f32[64,4,128]{2,1,0:T(4,128)}), f32[64,4,128]{2,1,0:T(4,128)S(1)}, u32[]{:S(2)}, u32[]{:S(2)}) async-start(f32[64,4,128]{2,1,0:T(4,128)} %get-tuple-element.21), calls=%async_computation.1 | async-start | bytes 262144 | tf_op jit(solution)/shard_map/all_to_all | solution.py:316
  54.6 1.2 %copy-start.3 = (f32[1024,256]{1,0:T(8,128)S(1)}, f32[1024,256]{1,0:T(8,128)}, u32[]{:S(2)}) copy-start(f32[1024,256]{1,0:T(8,128)} %get-tuple-element.23.kv) | copy-start | bytes 3145732
  55.8 1.0 copy-start.5
  81.4 3.2 %copy-start.1 = (bf16[32,32,1024]{2,1,0:T(8,128)(2,1)S(1)}, bf16[32,32,1024]{2,1,0:T(8,128)(2,1)}, u32[]{:S(2)}) copy-start(bf16[32,32,1024]{2,1,0:T(8,128)(2,1)} %get-tuple-element.25) | copy-start | bytes 6291460
  82.1 4.7 %collective-permute-start.2 = (bf16[1024,384]{1,0:T(8,128)(2,1)S(1)}, bf16[1024,384]{1,0:T(8,128)(2,1)S(1)}, u32[]{:S(2)}, u32[]{:S(2)}) collective-permute-start(bf16[1024,384]{1,0:T(8,128)(2,1)S(1)} %shard_map.56.dproj), channel_id=1, source_target_pairs={{0,8},{8,0},{1,9},{9,1},{2,10},{10,2},{3,11},{11,3},{4,12},{12,4},... | collective-permute-start | bytes 2359304 | tf_op jit(solution)/shard_map/ppermute | solution.py:340
  86.9 5.9 %copy-start.6 = (f32[1024,128]{1,0:T(8,128)S(1)}, f32[1024,128]{1,0:T(8,128)}, u32[]{:S(2)}) copy-start(f32[1024,128]{1,0:T(8,128)} %get-tuple-element.22.query) | copy-start | bytes 1572868
  88.8 26.5 %all-to-all-start.3 = ((bf16[32,32,384]{2,1,0:T(8,128)(2,1)}), bf16[32,32,384]{2,1,0:T(8,128)(2,1)S(1)}, u32[]{:S(2)}, u32[]{:S(2)}) async-start(bf16[32,32,384]{2,1,0:T(8,128)(2,1)} %bitcast.5), calls=%async_computation.3 | async-start | bytes 1572864 | tf_op jit(solution)/shard_map/all_to_all | solution.py:359

commit v6 on v5

--- a/solution.py
+++ b/solution.py
@@ -14,6 +14,7 @@
 
 SWAP = [(0, 1), (1, 0)]
 CTX = ("chip", "core")
+RANKS = ("core", "chip")
 F32 = jnp.float32
 BF16 = jnp.bfloat16
 
@@ -144,31 +145,32 @@
     place = core[0]
     chips, group, columns = mine.shape
     for chip in range(chips):
-        weight[2 * chip + place] = mine[chip]
-        weight[2 * chip + 1 - place] = other[chip]
-    whole = weight[...].reshape(chips * CORES * group, columns)
-    kv_state = jnp.zeros((HD, HD), F32)
-    qg_state = jnp.zeros((HD, HD), F32)
+        for member, held in ((place, mine), (1 - place, other)):
+            at = pl.multiple_of((CORES * chip + member) * group, group)
+            weight[pl.ds(at, group), :] = held[chip]
     for base, held in ((0, head), (ahead, tail)):
         if base:
             load.wait()
-        for rows in chunks(held.shape[0]):
-            part = mxu(held[rows, :], whole)
-            to = slice(base + rows.start, base + rows.stop)
-            proj[to, :] = part
-            for which, target, columns in ((0, query, pl.ds(0, HD)), (1, kv, pl.ds(HD, 2 * HD))):
-                stores.append(
-                    pltpu.make_async_copy(
-                        proj.at[to, columns], target.at[to, :], sems.at[len(stores) // 2, which]
-                    )
+        for rows in chunks(ahead):
+            proj[base + rows.start : base + rows.stop, :] = mxu(held[rows, :], weight[...])
+        to = pl.ds(base, ahead)
+        for which, target, columns_of in ((0, query, pl.ds(0, HD)), (1, kv, pl.ds(HD, 2 * HD))):
+            stores.append(
+                pltpu.make_async_copy(
+                    proj.at[to, columns_of], target.at[to, :], sems.at[len(stores) // 2, which]
                 )
-                stores[-1].start()
-            kv_state += gram(beside(part[:, HD : 2 * HD]), beside(part[:, 2 * HD :]))
-            qg_state += gram(beside(part[:, :HD]), beside(cotangent[to, :]))
+            )
+            stores[-1].start()
+    kv_state = jnp.zeros((HD, HD), F32)
+    qg_state = jnp.zeros((HD, HD), F32)
+    for rows in chunks(proj.shape[0]):
+        part = proj[rows, :]
+        kv_state += gram(beside(part[:, HD : 2 * HD]), beside(part[:, 2 * HD :]))
+        qg_state += gram(beside(part[:, :HD]), beside(cotangent[rows, :]))
     piece = HD // chips
     for chip in range(chips):
-        parts[2 * chip] = kv_state[chip * piece : (chip + 1) * piece]
-        parts[2 * chip + 1] = qg_state[chip * piece : (chip + 1) * piece]
+        parts[chip] = kv_state[chip * piece : (chip + 1) * piece]
+        parts[chips + chip] = qg_state[chip * piece : (chip + 1) * piece]
     for store in stores:
         store.wait()
 
@@ -201,8 +203,9 @@
     devices = pieces.shape[0]
     flip = core[0] == 1
     total = jnp.zeros(pieces.shape[1:], F32)
+    rank = [(slab % CORES) * (devices // CORES) + slab // CORES for slab in range(devices)]
     for step in range(devices):
-        source = jnp.where(flip, devices - 1 - step, step)
+        source = jnp.where(flip, rank[devices - 1 - step], rank[step])
         sums[source] = total
         total += pieces[source]
 
@@ -210,7 +213,7 @@
 def joined(back, which, states):
     chips, piece = back.shape[0] // CORES, back.shape[1]
     for chip in range(chips):
-        states[which, chip * piece : (chip + 1) * piece, :] = back[CORES * chip + which]
+        states[which, chip * piece : (chip + 1) * piece, :] = back[which * chips + chip]
     return states[which]
 
 
@@ -307,13 +310,13 @@
         [SMEM, HBM, VMEM, VMEM, VMEM, VMEM],
         [
             pltpu.VMEM((tokens // 2, width), BF16),
-            pltpu.VMEM((devices, group, columns), BF16),
+            pltpu.VMEM((width, columns), BF16),
             pltpu.VMEM((tokens, columns), F32),
             pltpu.SemaphoreType.DMA(()),
-            pltpu.SemaphoreType.DMA((tokens // BLOCK, 2)),
+            pltpu.SemaphoreType.DMA((2, 2)),
         ],
     )
-    pieces = lax.all_to_all(parts, CTX, 0, 0, tiled=True)
+    pieces = lax.all_to_all(parts, RANKS, 0, 0, tiled=True)
     (dlocal,) = call(
         local_kernel,
         [vmem((tokens, columns))],
@@ -326,7 +329,7 @@
     (sums,) = call(
         scan_kernel, [vmem(parts.shape)], [core, pieces], devices * HD * HD, 8, [SMEM, VMEM]
     )
-    back = lax.all_to_all(sums, CTX, 0, 0, tiled=True)
+    back = lax.all_to_all(sums, RANKS, 0, 0, tiled=True)
 
     (dproj,) = call(
         functools.partial(dproj_kernel, scale),

time: 117 us -> 115 us (0.983)
  waiting for transfers between devices: 41.5 us -> 40.1 us
where the time goes in v6:
time: 115 us; the launch traced here: 114 us
  waiting for transfers between devices  40.1 us (35%)
  starting transfers between devices  32.4 us (28%)
  Pallas kernels  20 us (17%)
  blocking collectives  15.5 us (13%)
  local copies, waits for them, and re-layouts  5.19 us (5%)
    pallas_call x10, Pallas kernels, call(): pl.pallas_call(body, out_shape=[kind for kind, _ in outs], in_specs=specs...  20 us
    all_to_all x1, waiting for transfers between devices, local(): lax.all_to_all(total.reshape(chips, group, columns), 'chip', 0, 0, tiled=...  19.4 us
    all_to_all x1, waiting for transfers between devices, local(): mine = lax.all_to_all(copies, 'chip', 0, 0, tiled=True)  15.7 us
    all_to_all x1, blocking collectives, local(): back = lax.all_to_all(sums, RANKS, 0, 0, tiled=True)  15.5 us
    all_to_all x1, starting transfers between devices, local(): mine = lax.all_to_all(copies, 'chip', 0, 0, tiled=True)  13.7 us
    all_to_all x1, starting transfers between devices, local(): pieces = lax.all_to_all(parts, RANKS, 0, 0, tiled=True)  5.86 us
    unnamed x14, local copies, waits for them, and re-layouts  5.19 us
    all_to_all x1, waiting for transfers between devices, local(): pieces = lax.all_to_all(parts, RANKS, 0, 0, tiled=True)  5.01 us
  transfers between devices with their start and end apart: 6, of which 3 were waited for; matrix products, arithmetic and copies ran while one was open for 0% of the time, Pallas kernels for 14%

profile of v6, /device:TPU:1, one launch (start us, length us, event | category | flops | bytes accessed | tf_op | source)
XLA Modules:
  0.0 114.0 jit_solution(2959767529083560468)
XLA Ops:
  0.6 0.0 copy-start.4
  0.6 0.7 copy-done.4
  1.4 1.0 shard_map.50
  2.3 13.7 %all-to-all-start = ((bf16[32,32,384]{2,1,0:T(8,128)(2,1)}), bf16[32,32,384]{2,1,0:T(8,128)(2,1)S(1)}, u32[]{:S(2)}, u32[]{:S(2)}) async-start(bf16[32,32,384]{2,1,0:T(8,128)(2,1)} %shard_map.50), calls=%async_computation | async-start | bytes 1572864 | tf_op jit(solution)/shard_map/all_to_all | solution.py:290
  16.1 0.0 copy-start
  16.1 2.2 %copy-done = bf16[1024,2048]{1,0:T(8,128)(2,1)S(1)} copy-done((bf16[1024,2048]{1,0:T(8,128)(2,1)S(1)}, bf16[1024,2048]{1,0:T(8,128)(2,1)}, u32[]{:S(2)}) %copy-start) | copy-done | bytes 4194328
  18.3 3.2 %shard_map.51 = (bf16[32,32,1024]{2,1,0:T(8,128)(2,1)}, bf16[32,32,1024]{2,1,0:T(8,128)(2,1)}, bf16[512,2048]{1,0:T(8,128)(2,1)S(1)}) custom-call(s32[1]{0:T(128)} %bitcast.core, bf16[1024,2048]{1,0:T(8,128)(2,1)S(1)} %copy-done), custom_call_target="tpu_custom_call" | custom-call | flops 2147483648 | bytes 4194308 | tf_op jit(solution)/shard_map/pallas_call | solution.py:89
  21.5 15.7 %all-to-all-done.mine = bf16[32,32,384]{2,1,0:T(8,128)(2,1)S(1)} async-done(((bf16[32,32,384]{2,1,0:T(8,128)(2,1)}), bf16[32,32,384]{2,1,0:T(8,128)(2,1)S(1)}, u32[]{:S(2)}, u32[]{:S(2)}) %all-to-all-start) | async-done | bytes 786464 | tf_op jit(solution)/shard_map/all_to_all | solution.py:290
  37.1 4.7 %collective-permute-start = (bf16[32,32,384]{2,1,0:T(8,128)(2,1)S(1)}, bf16[32,32,384]{2,1,0:T(8,128)(2,1)S(1)}, u32[]{:S(2)}, u32[]{:S(2)}) collective-permute-start(bf16[32,32,384]{2,1,0:T(8,128)(2,1)S(1)} %all-to-all-done.mine), channel_id=1, source_target_pairs={{0,8},{8,0},{1,9},{9,1},{2,10},{10,2},{3,11},{11,3},{4,12},{12,4},... | collective-permute-start | bytes 2359304 | tf_op jit(solution)/shard_map/ppermute | solution.py:302
  41.9 1.9 %collective-permute-start.1 = (bf16[1024,1024]{1,0:T(8,128)(2,1)}, bf16[1024,1024]{1,0:T(8,128)(2,1)}, u32[]{:S(2)}, u32[]{:S(2)}) collective-permute-start(bf16[1024,1024]{1,0:T(8,128)(2,1)} %bitcast.6), channel_id=1, source_target_pairs={{0,8},{8,0},{1,9},{9,1},{2,10},{10,2},{3,11},{11,3},{4,12},{12,4},... | collective-permute-start | bytes 6291464 | tf_op jit(solution)/shard_map/ppermute | solution.py:301
  43.8 0.0 collective-permute-done.other
  43.8 0.0 copy-done.2
  43.8 4.6 %shard_map.52 = (f32[1024,128]{1,0:T(8,128)}, f32[1024,256]{1,0:T(8,128)}, f32[64,4,128]{2,1,0:T(4,128)}) custom-call(s32[1]{0:T(128)} %bitcast.core, bf16[1024,2048]{1,0:T(8,128)(2,1)} %hidden.3, bf16[512,2048]{1,0:T(8,128)(2,1)S(1)} %get-tuple-element.19.head, bf16[32,32,384]{2,1,0:T(8,128)(2,1)S(1)} %all-to-all-done.mine, ...), custom_call_target="tpu_custom_call" | custom-call | flops 1879048192 | bytes 8388612 | tf_op jit(solution)/shard_map/pallas_call | solution.py:89
  48.4 5.9 %all-to-all-start.1 = ((f32[64,4,128]{2,1,0:T(4,128)}), f32[64,4,128]{2,1,0:T(4,128)S(1)}, u32[]{:S(2)}, u32[]{:S(2)}) async-start(f32[64,4,128]{2,1,0:T(4,128)} %get-tuple-element.21), calls=%async_computation.1 | async-start | bytes 262144 | tf_op jit(solution)/shard_map/all_to_all | solution.py:319
  54.2 0.0 copy-start.3
  54.3 1.2 %copy-done.3 = f32[1024,256]{1,0:T(8,128)S(1)} copy-done((f32[1024,256]{1,0:T(8,128)S(1)}, f32[1024,256]{1,0:T(8,128)}, u32[]{:S(2)}) %copy-start.3) | copy-done | bytes 1048600
  55.5 1.0 copy-done.5
  56.5 3.2 %shard_map.53.dlocal = f32[1024,384]{1,0:T(8,128)S(1)} custom-call(f32[1024,128]{1,0:T(8,128)S(1)} %copy-done.5, f32[1024,256]{1,0:T(8,128)S(1)} %copy-done.3, f32[1024,128]{1,0:T(8,128)S(1)} %copy-done.2), custom_call_target="tpu_custom_call" | custom-call | flops 1509949440 | bytes 2097152 | tf_op jit(solution)/shard_map/pallas_call | solution.py:89
  59.7 5.0 %all-to-all-done.1.pieces = f32[64,4,128]{2,1,0:T(4,128)S(1)} async-done(((f32[64,4,128]{2,1,0:T(4,128)}), f32[64,4,128]{2,1,0:T(4,128)S(1)}, u32[]{:S(2)}, u32[]{:S(2)}) %all-to-all-start.1) | async-done | bytes 131104 | tf_op jit(solution)/shard_map/all_to_all | solution.py:319
  64.7 0.1 shard_map.54
  64.8 15.5 %all_to_all.20.back = f32[64,4,128]{2,1,0:T(4,128)S(1)} all-to-all(f32[64,4,128]{2,1,0:T(4,128)S(1)} %shard_map.54), channel_id=1, replica_groups=mesh['chip'=32,'core'=2,'head'=8] {'core','chip'}, dimensions={0} | all-to-all | bytes 262144 | tf_op jit(solution)/shard_map/all_to_all | solution.py:332
  80.3 0.7 shard_map.56.dproj
  81.0 2.1 %collective-permute-start.2 = (bf16[1024,384]{1,0:T(8,128)(2,1)S(1)}, bf16[1024,384]{1,0:T(8,128)(2,1)S(1)}, u32[]{:S(2)}, u32[]{:S(2)}) collective-permute-start(bf16[1024,384]{1,0:T(8,128)(2,1)S(1)} %shard_map.56.dproj), channel_id=1, source_target_pairs={{0,8},{8,0},{1,9},{9,1},{2,10},{10,2},{3,11},{11,3},{4,12},{12,4},... | collective-permute-start | bytes 2359304 | tf_op jit(solution)/shard_map/ppermute | solution.py:343
  83.1 0.0 collective-permute-done.1.taken
  83.1 2.2 %shard_map.57 = (f32[1024,384]{1,0:T(8,128)S(1)}, bf16[1024,1024]{1,0:T(8,128)(2,1)S(1)}) custom-call(bf16[1024,1024]{1,0:T(8,128)(2,1)S(1)} %bitcast.4, bf16[1024,384]{1,0:T(8,128)(2,1)S(1)} %shard_map.56.dproj, bf16[1024,1024]{1,0:T(8,128)(2,1)} %collective-permute-done.1.taken), custom_call_target="tpu_custom_call" | custom-call | flops 805306368 | bytes 4980736 | tf_op jit(solution)/shard_map/pallas_call | solution.py:89
  85.4 0.0 collective-permute-done.2.dproj
  85.4 0.0 copy-start.6
  85.4 2.0 %shard_map.58 = bf16[1024,384]{1,0:T(8,128)(2,1)} custom-call(bf16[1024,1024]{1,0:T(8,128)(2,1)S(1)} %get-tuple-element.28.turned, bf16[1024,384]{1,0:T(8,128)(2,1)S(1)} %collective-permute-done.2.dproj, f32[1024,384]{1,0:T(8,128)S(1)} %get-tuple-element.29.product), custom_call_target="tpu_custom_call" | custom-call | flops 805306368 | bytes 4456448 | tf_op jit(solution)/shard_map/pallas_call | solution.py:89
  87.4 4.1 %all-to-all-start.3 = ((bf16[32,32,384]{2,1,0:T(8,128)(2,1)}), bf16[32,32,384]{2,1,0:T(8,128)(2,1)S(1)}, u32[]{:S(2)}, u32[]{:S(2)}) async-start(bf16[32,32,384]{2,1,0:T(8,128)(2,1)} %bitcast.5), calls=%async_computation.3 | async-start | bytes 1572864 | tf_op jit(solution)/shard_map/all_to_all | solution.py:362
  91.5 2.3 %shard_map.55 = f32[1024,128]{1,0:T(8,128)} custom-call(f32[64,4,128]{2,1,0:T(4,128)S(1)} %all_to_all.20.back, f32[1024,128]{1,0:T(8,128)S(1)} %copy-done.6, f32[1024,256]{1,0:T(8,128)S(1)} %copy-done.3), custom_call_target="tpu_custom_call" | custom-call | flops 603979776 | bytes 1703936 | tf_op jit(solution)/shard_map/pallas_call | solution.py:89
  93.8 19.4 %all-to-all-done.3.landed = bf16[32,32,384]{2,1,0:T(8,128)(2,1)S(1)} async-done(((bf16[32,32,384]{2,1,0:T(8,128)(2,1)}), bf16[32,32,384]{2,1,0:T(8,128)(2,1)S(1)}, u32[]{:S(2)}, u32[]{:S(2)}) %all-to-all-start.3) | async-done | bytes 786464 | tf_op jit(solution)/shard_map/all_to_all | solution.py:362
  113.2 0.7 shard_map.59
  (5 shorter events, 0.0 us)
Async XLA Ops:
  0.6 0.7 copy-start.4
  2.3 34.8 %all-to-all-start = ((bf16[32,32,384]{2,1,0:T(8,128)(2,1)}), bf16[32,32,384]{2,1,0:T(8,128)(2,1)S(1)}, u32[]{:S(2)}, u32[]{:S(2)}) async-start(bf16[32,32,384]{2,1,0:T(8,128)(2,1)} %shard_map.50), calls=%async_computation | async-start | bytes 1572864 | tf_op jit(solution)/shard_map/all_to_all | solution.py:290
  16.1 2.2 %copy-start = (bf16[1024,2048]{1,0:T(8,128)(2,1)S(1)}, bf16[1024,2048]{1,0:T(8,128)(2,1)}, u32[]{:S(2)}) copy-start(bf16[1024,2048]{1,0:T(8,128)(2,1)} %hidden.3) | copy-start | bytes 12582916
  18.3 25.5 %copy-start.2 = (f32[1024,128]{1,0:T(8,128)S(1)}, f32[1024,128]{1,0:T(8,128)}, u32[]{:S(2)}) copy-start(f32[1024,128]{1,0:T(8,128)} %cotangent.5) | copy-start | bytes 1572868
  37.1 6.7 %collective-permute-start = (bf16[32,32,384]{2,1,0:T(8,128)(2,1)S(1)}, bf16[32,32,384]{2,1,0:T(8,128)(2,1)S(1)}, u32[]{:S(2)}, u32[]{:S(2)}) collective-permute-start(bf16[32,32,384]{2,1,0:T(8,128)(2,1)S(1)} %all-to-all-done.mine), channel_id=1, source_target_pairs={{0,8},{8,0},{1,9},{9,1},{2,10},{10,2},{3,11},{11,3},{4,12},{12,4},... | collective-permute-start | bytes 2359304 | tf_op jit(solution)/shard_map/ppermute | solution.py:302
  41.9 41.2 %collective-permute-start.1 = (bf16[1024,1024]{1,0:T(8,128)(2,1)}, bf16[1024,1024]{1,0:T(8,128)(2,1)}, u32[]{:S(2)}, u32[]{:S(2)}) collective-permute-start(bf16[1024,1024]{1,0:T(8,128)(2,1)} %bitcast.6), channel_id=1, source_target_pairs={{0,8},{8,0},{1,9},{9,1},{2,10},{10,2},{3,11},{11,3},{4,12},{12,4},... | collective-permute-start | bytes 6291464 | tf_op jit(solution)/shard_map/ppermute | solution.py:301
  48.4 16.3 %all-to-all-start.1 = ((f32[64,4,128]{2,1,0:T(4,128)}), f32[64,4,128]{2,1,0:T(4,128)S(1)}, u32[]{:S(2)}, u32[]{:S(2)}) async-start(f32[64,4,128]{2,1,0:T(4,128)} %get-tuple-element.21), calls=%async_computation.1 | async-start | bytes 262144 | tf_op jit(solution)/shard_map/all_to_all | solution.py:319
  54.2 1.2 %copy-start.3 = (f32[1024,256]{1,0:T(8,128)S(1)}, f32[1024,256]{1,0:T(8,128)}, u32[]{:S(2)}) copy-start(f32[1024,256]{1,0:T(8,128)} %get-tuple-element.23.kv) | copy-start | bytes 3145732
  55.5 1.0 copy-start.5
  80.3 2.8 %copy-start.1 = (bf16[32,32,1024]{2,1,0:T(8,128)(2,1)S(1)}, bf16[32,32,1024]{2,1,0:T(8,128)(2,1)}, u32[]{:S(2)}) copy-start(bf16[32,32,1024]{2,1,0:T(8,128)(2,1)} %get-tuple-element.25) | copy-start | bytes 6291460
  81.0 4.4 %collective-permute-start.2 = (bf16[1024,384]{1,0:T(8,128)(2,1)S(1)}, bf16[1024,384]{1,0:T(8,128)(2,1)S(1)}, u32[]{:S(2)}, u32[]{:S(2)}) collective-permute-start(bf16[1024,384]{1,0:T(8,128)(2,1)S(1)} %shard_map.56.dproj), channel_id=1, source_target_pairs={{0,8},{8,0},{1,9},{9,1},{2,10},{10,2},{3,11},{11,3},{4,12},{12,4},... | collective-permute-start | bytes 2359304 | tf_op jit(solution)/shard_map/ppermute | solution.py:343
  85.4 6.1 %copy-start.6 = (f32[1024,128]{1,0:T(8,128)S(1)}, f32[1024,128]{1,0:T(8,128)}, u32[]{:S(2)}) copy-start(f32[1024,128]{1,0:T(8,128)} %get-tuple-element.22.query) | copy-start | bytes 1572868
  87.4 25.9 %all-to-all-start.3 = ((bf16[32,32,384]{2,1,0:T(8,128)(2,1)}), bf16[32,32,384]{2,1,0:T(8,128)(2,1)S(1)}, u32[]{:S(2)}, u32[]{:S(2)}) async-start(bf16[32,32,384]{2,1,0:T(8,128)(2,1)} %bitcast.5), calls=%async_computation.3 | async-start | bytes 1572864 | tf_op jit(solution)/shard_map/all_to_all | solution.py:362

commit v7 on v6

--- a/solution.py
+++ b/solution.py
@@ -9,6 +9,7 @@
 
 HD = 128
 BLOCK = 256
+PARTS = 4
 CORES = 2
 MIB = 1 << 20
 
@@ -101,16 +102,6 @@
     return [slice(start, start + BLOCK) for start in range(0, total, BLOCK)]
 
 
-def fetched(source, target, sems):
-    loads = [
-        pltpu.make_async_copy(source.at[rows, :], target.at[rows, :], sems.at[index])
-        for index, rows in enumerate(chunks(source.shape[0]))
-    ]
-    for load in loads:
-        load.start()
-    return loads
-
-
 def causal():
     at = lax.broadcasted_iota(jnp.int32, (BLOCK, BLOCK), 0)
     return at >= lax.broadcasted_iota(jnp.int32, (BLOCK, BLOCK), 1)
@@ -121,43 +112,40 @@
         copies[chip] = weight[...]
 
 
-def turn_kernel(core, hidden, keep, give, head):
-    head[...] = hidden[: head.shape[0], :]
-    first = core[0] == 0
-    group = keep.shape[1]
-    for column in range(hidden.shape[1] // HD):
-        turned = hidden[:, column * HD : (column + 1) * HD].T
-        for pair in range(HD // (CORES * group)):
-            at = pair * CORES * group
-            even = turned[at : at + group]
-            odd = turned[at + group : at + CORES * group]
-            chip = column * (HD // (CORES * group)) + pair
-            keep[chip] = jnp.where(first, even, odd)
-            give[chip] = jnp.where(first, odd, even)
-
-
-def project_kernel(core, hidden, head, mine, other, cotangent, query, kv, parts,
-                   tail, weight, proj, load_sem, sems):
-    ahead = head.shape[0]
-    load = pltpu.make_async_copy(hidden.at[ahead:, :], tail, load_sem)
-    load.start()
+def prepare_kernel(group, core, hidden, near, far, keep, *give):
+    wide = 2 * HD
+    at = lax.broadcasted_iota(jnp.int32, (wide, wide), 0)
+    to = lax.broadcasted_iota(jnp.int32, (wide, wide), 1)
+    parity = jnp.where(to < HD, core[0], 1 - core[0])
+    slot = lax.rem(to, HD)
+    source = (lax.div(slot, group) * CORES + parity) * group + lax.rem(slot, group)
+    order = jnp.where(at == source, 1.0, 0.0).astype(BF16)
+    for step in range(hidden.shape[1] // wide):
+        columns = mxu(hidden[:, step * wide : (step + 1) * wide], order).astype(BF16)
+        span = slice(step * HD, (step + 1) * HD)
+        near[:, span] = columns[:, :HD]
+        far[:, span] = columns[:, HD:]
+        keep[span, :] = columns[:, :HD].T
+        which, first = divmod(step * HD, give[0].shape[0])
+        give[which][first : first + HD, :] = columns[:, HD:].T
+
+
+def half_kernel(near, mine, partial):
+    chips, group, columns = mine.shape
+    for rows in chunks(near.shape[0]):
+        partial[rows, :] = mxu(near[rows, :], mine[...].reshape(chips * group, columns))
+
+
+def project_kernel(far, other, partial, cotangent, query, kv, parts, proj, sems):
+    chips, group, columns = other.shape
     stores = []
-    place = core[0]
-    chips, group, columns = mine.shape
-    for chip in range(chips):
-        for member, held in ((place, mine), (1 - place, other)):
-            at = pl.multiple_of((CORES * chip + member) * group, group)
-            weight[pl.ds(at, group), :] = held[chip]
-    for base, held in ((0, head), (ahead, tail)):
-        if base:
-            load.wait()
-        for rows in chunks(ahead):
-            proj[base + rows.start : base + rows.stop, :] = mxu(held[rows, :], weight[...])
-        to = pl.ds(base, ahead)
-        for which, target, columns_of in ((0, query, pl.ds(0, HD)), (1, kv, pl.ds(HD, 2 * HD))):
+    for rows in chunks(far.shape[0]):
+        weight = other[...].reshape(chips * group, columns)
+        proj[rows, :] = partial[rows, :] + mxu(far[rows, :], weight)
+        for which, target, span in ((0, query, pl.ds(0, HD)), (1, kv, pl.ds(HD, 2 * HD))):
             stores.append(
                 pltpu.make_async_copy(
-                    proj.at[to, columns_of], target.at[to, :], sems.at[len(stores) // 2, which]
+                    proj.at[rows, span], target.at[rows, :], sems.at[len(stores) // 2, which]
                 )
             )
             stores[-1].start()
@@ -245,8 +233,15 @@
         state += gram(beside(keys), beside(values))
 
 
-def own_kernel(turned, dproj, taken, product, held, sems):
-    loads = fetched(taken, held, sems)
+def own_kernel(turned, dproj, *refs):
+    taken, (product, held, sems) = refs[:PARTS], refs[PARTS:]
+    size = taken[0].shape[0]
+    loads = [
+        pltpu.make_async_copy(part, held.at[index * size : (index + 1) * size, :], sems.at[index])
+        for index, part in enumerate(taken)
+    ]
+    for load in loads:
+        load.start()
     for rows in chunks(turned.shape[0]):
         product[rows, :] = mxu(turned[rows, :], dproj[...])
     for load in loads:
@@ -288,32 +283,40 @@
         spread_kernel, [vmem((chips, group, columns), BF16)], [qkv_weight], 1024, 8, [VMEM]
     )
     mine = lax.all_to_all(copies, "chip", 0, 0, tiled=True)
-    keep, give, head = call(
-        turn_kernel,
-        [hbm((chips, group, tokens), BF16)] * 2 + [vmem((tokens // 2, width), BF16)],
+    near, far, keep, *give = call(
+        functools.partial(prepare_kernel, group),
+        [
+            vmem((tokens, half), BF16),
+            hbm((tokens, half), BF16),
+            hbm((half, tokens), BF16),
+        ]
+        + [hbm((half // PARTS, tokens), BF16)] * PARTS,
         [core, hidden],
         tokens * width * 1024,
         24,
         [SMEM, VMEM],
     )
-    mine, keep, give, head = lax.optimization_barrier((mine, keep, give, head))
-    keep, give = keep.reshape(half, tokens), give.reshape(half, tokens)
-    taken = lax.ppermute(give, "core", SWAP)
+    taken = [lax.ppermute(part, "core", SWAP) for part in give]
+    mine, near, far, keep, taken = lax.optimization_barrier((mine, near, far, keep, taken))
     other = lax.ppermute(mine, "core", SWAP)
-
+    (partial,) = call(
+        half_kernel,
+        [vmem((tokens, columns))],
+        [near, mine],
+        2 * tokens * half * columns,
+        16,
+        [VMEM, VMEM],
+    )
     query, kv, parts = call(
         project_kernel,
         [direct((tokens, HD)), direct((tokens, 2 * HD)), vmem((devices, piece, HD))],
-        [core, hidden, head, mine, other, out_grad],
-        2 * tokens * width * columns + 16 * square,
-        32,
-        [SMEM, HBM, VMEM, VMEM, VMEM, VMEM],
+        [far, other, partial, out_grad],
+        2 * tokens * half * columns + 16 * square,
+        24,
+        [VMEM] * 4,
         [
-            pltpu.VMEM((tokens // 2, width), BF16),
-            pltpu.VMEM((width, columns), BF16),
             pltpu.VMEM((tokens, columns), F32),
-            pltpu.SemaphoreType.DMA(()),
-            pltpu.SemaphoreType.DMA((2, 2)),
+            pltpu.SemaphoreType.DMA((tokens // BLOCK, 2)),
         ],
     )
     pieces = lax.all_to_all(parts, RANKS, 0, 0, tiled=True)
@@ -344,11 +347,11 @@
     product, held = call(
         own_kernel,
         [vmem((half, columns)), (pltpu.VMEM((half, tokens), BF16), VMEM)],
-        [keep, dproj, taken],
+        [keep, dproj, *taken],
         2 * half * tokens * columns,
         24,
-        [VMEM, VMEM, HBM],
-        [pltpu.SemaphoreType.DMA((half // BLOCK,))],
+        [VMEM, VMEM] + [HBM] * PARTS,
+        [pltpu.SemaphoreType.DMA((PARTS,))],
     )
     (total,) = call(
         total_kernel,

time: 115 us -> 113 us (0.983)
  waiting for transfers between devices: 40.1 us -> 29.2 us
  starting transfers between devices: 32.4 us -> 39.5 us
  local copies, waits for them, and re-layouts: 5.19 us -> 6.83 us
    all_to_all x1, waiting for transfers between devices: 15.7 us -> 3.47 us  [local(): mine = lax.all_to_all(copies, 'chip', 0, 0, tiled=True)]
    ppermute x1 -> x4, starting transfers between devices: 1.92 us -> 9.1 us  [local(): taken = [lax.ppermute(part, 'core', SWAP) for part in give]]
    unnamed x14 -> x22, local copies, waits for them, and re-layouts: 5.19 us -> 6.83 us
    pallas_call x10 -> x11, Pallas kernels: 20 us -> 19.5 us  [call(): pl.pallas_call(body, out_shape=[kind for kind, _ in outs], in_specs=specs...]
  transfers between devices with their start and end apart: 6 -> 9, of which waited for: 3 -> 6; matrix products, arithmetic and copies ran while one was open for 0% -> 0% of each run, Pallas kernels for 14% -> 11%
where the time goes in v7:
time: 113 us; the launch traced here: 111 us
  starting transfers between devices  39.5 us (35%)
  waiting for transfers between devices  29.2 us (26%)
  Pallas kernels  19.5 us (17%)
  blocking collectives  15.5 us (14%)
  local copies, waits for them, and re-layouts  6.83 us (6%)
    pallas_call x11, Pallas kernels, call(): pl.pallas_call(body, out_shape=[kind for kind, _ in outs], in_specs=specs...  19.5 us
    all_to_all x1, waiting for transfers between devices, local(): lax.all_to_all(total.reshape(chips, group, columns), 'chip', 0, 0, tiled=...  19.1 us
    all_to_all x1, blocking collectives, local(): back = lax.all_to_all(sums, RANKS, 0, 0, tiled=True)  15.5 us
    all_to_all x1, starting transfers between devices, local(): mine = lax.all_to_all(copies, 'chip', 0, 0, tiled=True)  13.7 us
    ppermute x4, starting transfers between devices, local(): taken = [lax.ppermute(part, 'core', SWAP) for part in give]  9.1 us
    unnamed x22, local copies, waits for them, and re-layouts  6.83 us
    all_to_all x1, starting transfers between devices, local(): pieces = lax.all_to_all(parts, RANKS, 0, 0, tiled=True)  5.73 us
    all_to_all x1, waiting for transfers between devices, local(): pieces = lax.all_to_all(parts, RANKS, 0, 0, tiled=True)  5.01 us
  transfers between devices with their start and end apart: 9, of which 6 were waited for; matrix products, arithmetic and copies ran while one was open for 0% of the time, Pallas kernels for 11%

profile of v7, /device:TPU:1, one launch (start us, length us, event | category | flops | bytes accessed | tf_op | source)
XLA Modules:
  0.0 111.5 jit_solution(9431867029584159595)
XLA Ops:
  0.6 0.7 copy-done.4
  1.4 1.0 shard_map.50
  2.3 13.7 %all-to-all-start = ((bf16[32,32,384]{2,1,0:T(8,128)(2,1)}), bf16[32,32,384]{2,1,0:T(8,128)(2,1)S(1)}, u32[]{:S(2)}, u32[]{:S(2)}) async-start(bf16[32,32,384]{2,1,0:T(8,128)(2,1)} %shard_map.50), calls=%async_computation | async-start | bytes 1572864 | tf_op jit(solution)/shard_map/all_to_all | solution.py:285
  16.1 2.2 %copy-done.5 = bf16[1024,2048]{1,0:T(8,128)(2,1)S(1)} copy-done((bf16[1024,2048]{1,0:T(8,128)(2,1)S(1)}, bf16[1024,2048]{1,0:T(8,128)(2,1)}, u32[]{:S(2)}) %copy-start.5) | copy-done | bytes 4194328
  18.2 4.1 %shard_map.51 = (bf16[1024,1024]{1,0:T(8,128)(2,1)S(1)}, bf16[1024,1024]{1,0:T(8,128)(2,1)}, bf16[1024,1024]{1,0:T(8,128)(2,1)}, bf16[256,1024]{1,0:T(8,128)(2,1...) custom-call(s32[1]{0:T(128)} %bitcast.core, bf16[1024,2048]{1,0:T(8,128)(2,1)S(1)} %copy-done.5), custom_call_target="tpu_custom_call" | custom-call | flops 2147483648 | bytes 4194308 | tf_op jit(solution)/shard_map/pallas_call | solution.py:90
  22.3 2.8 %collective-permute-start = (bf16[256,1024]{1,0:T(8,128)(2,1)}, bf16[256,1024]{1,0:T(8,128)(2,1)S(1)}, u32[]{:S(2)}, u32[]{:S(2)}) collective-permute-start(bf16[256,1024]{1,0:T(8,128)(2,1)} %get-tuple-element.27), channel_id=1, source_target_pairs={{0,8},{8,0},{1,9},{9,1},{2,10},{10,2},{3,11},{11,3},{4,12},{12,4},... | collective-permute-start | bytes 1572872 | tf_op jit(solution)/shard_map/ppermute | solution.py:299
  25.2 1.9 %collective-permute-start.1 = (bf16[256,1024]{1,0:T(8,128)(2,1)}, bf16[256,1024]{1,0:T(8,128)(2,1)S(1)}, u32[]{:S(2)}, u32[]{:S(2)}) collective-permute-start(bf16[256,1024]{1,0:T(8,128)(2,1)} %get-tuple-element.28), channel_id=1, source_target_pairs={{0,8},{8,0},{1,9},{9,1},{2,10},{10,2},{3,11},{11,3},{4,12},{12,4},... | collective-permute-start | bytes 1572872 | tf_op jit(solution)/shard_map/ppermute | solution.py:299
  27.1 2.4 %collective-permute-start.2 = (bf16[256,1024]{1,0:T(8,128)(2,1)}, bf16[256,1024]{1,0:T(8,128)(2,1)S(1)}, u32[]{:S(2)}, u32[]{:S(2)}) collective-permute-start(bf16[256,1024]{1,0:T(8,128)(2,1)} %get-tuple-element.29), channel_id=1, source_target_pairs={{0,8},{8,0},{1,9},{9,1},{2,10},{10,2},{3,11},{11,3},{4,12},{12,4},... | collective-permute-start | bytes 1572872 | tf_op jit(solution)/shard_map/ppermute | solution.py:299
  29.5 1.9 %collective-permute-start.3 = (bf16[256,1024]{1,0:T(8,128)(2,1)}, bf16[256,1024]{1,0:T(8,128)(2,1)}, u32[]{:S(2)}, u32[]{:S(2)}) collective-permute-start(bf16[256,1024]{1,0:T(8,128)(2,1)} %get-tuple-element.30), channel_id=1, source_target_pairs={{0,8},{8,0},{1,9},{9,1},{2,10},{10,2},{3,11},{11,3},{4,12},{12,4},... | collective-permute-start | bytes 1572872 | tf_op jit(solution)/shard_map/ppermute | solution.py:299
  31.5 0.8 copy-done.9
  32.3 0.8 copy-done.10
  33.1 0.5 collective-permute-done.3.refs_3_
  33.6 3.5 %all-to-all-done.mine = bf16[32,32,384]{2,1,0:T(8,128)(2,1)S(1)} async-done(((bf16[32,32,384]{2,1,0:T(8,128)(2,1)}), bf16[32,32,384]{2,1,0:T(8,128)(2,1)S(1)}, u32[]{:S(2)}, u32[]{:S(2)}) %all-to-all-start) | async-done | bytes 786464 | tf_op jit(solution)/shard_map/all_to_all | solution.py:285
  37.1 5.0 %collective-permute-start.4 = (bf16[32,32,384]{2,1,0:T(8,128)(2,1)S(1)}, bf16[32,32,384]{2,1,0:T(8,128)(2,1)S(1)}, u32[]{:S(2)}, u32[]{:S(2)}) collective-permute-start(bf16[32,32,384]{2,1,0:T(8,128)(2,1)S(1)} %all-to-all-done.mine), channel_id=1, source_target_pairs={{0,8},{8,0},{1,9},{9,1},{2,10},{10,2},{3,11},{11,3},{4,12},{12,4},... | collective-permute-start | bytes 2359304 | tf_op jit(solution)/shard_map/ppermute | solution.py:301
  42.1 1.2 %shard_map.52.partial = f32[1024,384]{1,0:T(8,128)S(1)} custom-call(bf16[1024,1024]{1,0:T(8,128)(2,1)S(1)} %get-tuple-element.33.near, bf16[32,32,384]{2,1,0:T(8,128)(2,1)S(1)} %all-to-all-done.mine), custom_call_target="tpu_custom_call" | custom-call | flops 805306368 | bytes 2883584 | tf_op jit(solution)/shard_map/pallas_call | solution.py:90
  43.4 0.6 collective-permute-done.4.other
  44.0 2.7 %shard_map.53 = (f32[1024,128]{1,0:T(8,128)}, f32[1024,256]{1,0:T(8,128)}, f32[64,4,128]{2,1,0:T(4,128)}) custom-call(bf16[1024,1024]{1,0:T(8,128)(2,1)S(1)} %copy-done.1, bf16[32,32,384]{2,1,0:T(8,128)(2,1)S(1)} %collective-permute-done.4.other, f32[1024,384]{1,0:T(8,128)S(1)} %shard_map.52.partial, f32[1024,128]{1,0:T(8,128)S(1)} %copy-done.2), custom_call_target="tpu_custom_call" | custom-call | flops 1073741824 | bytes 4980736 | tf_op jit(solution)/shard_map/pallas_call | solution.py:90
  46.7 5.7 %all-to-all-start.1 = ((f32[64,4,128]{2,1,0:T(4,128)}), f32[64,4,128]{2,1,0:T(4,128)S(1)}, u32[]{:S(2)}, u32[]{:S(2)}) async-start(f32[64,4,128]{2,1,0:T(4,128)} %get-tuple-element.34), calls=%async_computation.1 | async-start | bytes 262144 | tf_op jit(solution)/shard_map/all_to_all | solution.py:322
  52.5 1.2 %copy-done.3 = f32[1024,256]{1,0:T(8,128)S(1)} copy-done((f32[1024,256]{1,0:T(8,128)S(1)}, f32[1024,256]{1,0:T(8,128)}, u32[]{:S(2)}) %copy-start.3) | copy-done | bytes 1048600
  53.7 1.0 copy-done.6
  54.7 3.2 %shard_map.54.dlocal = f32[1024,384]{1,0:T(8,128)S(1)} custom-call(f32[1024,128]{1,0:T(8,128)S(1)} %copy-done.6, f32[1024,256]{1,0:T(8,128)S(1)} %copy-done.3, f32[1024,128]{1,0:T(8,128)S(1)} %copy-done.2), custom_call_target="tpu_custom_call" | custom-call | flops 1509949440 | bytes 2097152 | tf_op jit(solution)/shard_map/pallas_call | solution.py:90
  57.9 5.0 %all-to-all-done.1.pieces = f32[64,4,128]{2,1,0:T(4,128)S(1)} async-done(((f32[64,4,128]{2,1,0:T(4,128)}), f32[64,4,128]{2,1,0:T(4,128)S(1)}, u32[]{:S(2)}, u32[]{:S(2)}) %all-to-all-start.1) | async-done | bytes 131104 | tf_op jit(solution)/shard_map/all_to_all | solution.py:322
  63.1 15.5 %all_to_all.20.back = f32[64,4,128]{2,1,0:T(4,128)S(1)} all-to-all(f32[64,4,128]{2,1,0:T(4,128)S(1)} %shard_map.55), channel_id=1, replica_groups=mesh['chip'=32,'core'=2,'head'=8] {'core','chip'}, dimensions={0} | all-to-all | bytes 262144 | tf_op jit(solution)/shard_map/all_to_all | solution.py:335
  78.5 0.7 shard_map.57.dproj
  79.2 2.1 %collective-permute-start.5 = (bf16[1024,384]{1,0:T(8,128)(2,1)S(1)}, bf16[1024,384]{1,0:T(8,128)(2,1)S(1)}, u32[]{:S(2)}, u32[]{:S(2)}) collective-permute-start(bf16[1024,384]{1,0:T(8,128)(2,1)S(1)} %shard_map.57.dproj), channel_id=1, source_target_pairs={{0,8},{8,0},{1,9},{9,1},{2,10},{10,2},{3,11},{11,3},{4,12},{12,4},... | collective-permute-start | bytes 2359304 | tf_op jit(solution)/shard_map/ppermute | solution.py:346
  81.3 1.6 %shard_map.58 = (f32[1024,384]{1,0:T(8,128)S(1)}, bf16[1024,1024]{1,0:T(8,128)(2,1)S(1)}) custom-call(bf16[1024,1024]{1,0:T(8,128)(2,1)S(1)} %copy-done, bf16[1024,384]{1,0:T(8,128)(2,1)S(1)} %shard_map.57.dproj, bf16[256,1024]{1,0:T(8,128)(2,1)} %copy-done.8, bf16[256,1024]{1,0:T(8,128)(2,1)} %copy-done.9, bf16[256,1024]{1,0:T(8,128)(2,1)} %copy-done.10, ...), custom_call_target="tpu_custom_call" | custom-call | flops 805306368 | bytes 4980736 | tf_op jit(solution)/shard_map/pallas_call | solution.py:90
  82.9 0.5 collective-permute-done.5.dproj
  83.4 2.0 %shard_map.59 = bf16[1024,384]{1,0:T(8,128)(2,1)} custom-call(bf16[1024,1024]{1,0:T(8,128)(2,1)S(1)} %get-tuple-element.44.turned, bf16[1024,384]{1,0:T(8,128)(2,1)S(1)} %collective-permute-done.5.dproj, f32[1024,384]{1,0:T(8,128)S(1)} %get-tuple-element.45.product), custom_call_target="tpu_custom_call" | custom-call | flops 805306368 | bytes 4456448 | tf_op jit(solution)/shard_map/pallas_call | solution.py:90
  85.4 3.9 %all-to-all-start.3 = ((bf16[32,32,384]{2,1,0:T(8,128)(2,1)}), bf16[32,32,384]{2,1,0:T(8,128)(2,1)S(1)}, u32[]{:S(2)}, u32[]{:S(2)}) async-start(bf16[32,32,384]{2,1,0:T(8,128)(2,1)} %bitcast.2), calls=%async_computation.3 | async-start | bytes 1572864 | tf_op jit(solution)/shard_map/all_to_all | solution.py:365
  89.3 2.3 %shard_map.56 = f32[1024,128]{1,0:T(8,128)} custom-call(f32[64,4,128]{2,1,0:T(4,128)S(1)} %all_to_all.20.back, f32[1024,128]{1,0:T(8,128)S(1)} %copy-done.7, f32[1024,256]{1,0:T(8,128)S(1)} %copy-done.3), custom_call_target="tpu_custom_call" | custom-call | flops 603979776 | bytes 1703936 | tf_op jit(solution)/shard_map/pallas_call | solution.py:90
  91.6 19.1 %all-to-all-done.3.landed = bf16[32,32,384]{2,1,0:T(8,128)(2,1)S(1)} async-done(((bf16[32,32,384]{2,1,0:T(8,128)(2,1)}), bf16[32,32,384]{2,1,0:T(8,128)(2,1)S(1)}, u32[]{:S(2)}, u32[]{:S(2)}) %all-to-all-start.3) | async-done | bytes 786464 | tf_op jit(solution)/shard_map/all_to_all | solution.py:365
  110.7 0.7 shard_map.60
  (20 shorter events, 0.1 us)
Async XLA Ops:
  0.6 0.7 copy-start.4
  2.3 34.8 %all-to-all-start = ((bf16[32,32,384]{2,1,0:T(8,128)(2,1)}), bf16[32,32,384]{2,1,0:T(8,128)(2,1)S(1)}, u32[]{:S(2)}, u32[]{:S(2)}) async-start(bf16[32,32,384]{2,1,0:T(8,128)(2,1)} %shard_map.50), calls=%async_computation | async-start | bytes 1572864 | tf_op jit(solution)/shard_map/all_to_all | solution.py:285
  16.0 2.2 %copy-start.5 = (bf16[1024,2048]{1,0:T(8,128)(2,1)S(1)}, bf16[1024,2048]{1,0:T(8,128)(2,1)}, u32[]{:S(2)}) copy-start(bf16[1024,2048]{1,0:T(8,128)(2,1)} %hidden.1) | copy-start | bytes 12582916
  22.3 9.1 %collective-permute-start = (bf16[256,1024]{1,0:T(8,128)(2,1)}, bf16[256,1024]{1,0:T(8,128)(2,1)S(1)}, u32[]{:S(2)}, u32[]{:S(2)}) collective-permute-start(bf16[256,1024]{1,0:T(8,128)(2,1)} %get-tuple-element.27), channel_id=1, source_target_pairs={{0,8},{8,0},{1,9},{9,1},{2,10},{10,2},{3,11},{11,3},{4,12},{12,4},... | collective-permute-start | bytes 1572872 | tf_op jit(solution)/shard_map/ppermute | solution.py:299
  25.2 6.3 %collective-permute-start.1 = (bf16[256,1024]{1,0:T(8,128)(2,1)}, bf16[256,1024]{1,0:T(8,128)(2,1)S(1)}, u32[]{:S(2)}, u32[]{:S(2)}) collective-permute-start(bf16[256,1024]{1,0:T(8,128)(2,1)} %get-tuple-element.28), channel_id=1, source_target_pairs={{0,8},{8,0},{1,9},{9,1},{2,10},{10,2},{3,11},{11,3},{4,12},{12,4},... | collective-permute-start | bytes 1572872 | tf_op jit(solution)/shard_map/ppermute | solution.py:299
  27.1 4.4 %collective-permute-start.2 = (bf16[256,1024]{1,0:T(8,128)(2,1)}, bf16[256,1024]{1,0:T(8,128)(2,1)S(1)}, u32[]{:S(2)}, u32[]{:S(2)}) collective-permute-start(bf16[256,1024]{1,0:T(8,128)(2,1)} %get-tuple-element.29), channel_id=1, source_target_pairs={{0,8},{8,0},{1,9},{9,1},{2,10},{10,2},{3,11},{11,3},{4,12},{12,4},... | collective-permute-start | bytes 1572872 | tf_op jit(solution)/shard_map/ppermute | solution.py:299
  29.5 4.1 %collective-permute-start.3 = (bf16[256,1024]{1,0:T(8,128)(2,1)}, bf16[256,1024]{1,0:T(8,128)(2,1)}, u32[]{:S(2)}, u32[]{:S(2)}) collective-permute-start(bf16[256,1024]{1,0:T(8,128)(2,1)} %get-tuple-element.30), channel_id=1, source_target_pairs={{0,8},{8,0},{1,9},{9,1},{2,10},{10,2},{3,11},{11,3},{4,12},{12,4},... | collective-permute-start | bytes 1572872 | tf_op jit(solution)/shard_map/ppermute | solution.py:299
  31.4 5.7 %copy-start.8 = (bf16[256,1024]{1,0:T(8,128)(2,1)}, bf16[256,1024]{1,0:T(8,128)(2,1)S(1)}, u32[]{:S(2)}) copy-start(bf16[256,1024]{1,0:T(8,128)(2,1)S(1)} %collective-permute-done.refs_0_) | copy-start | bytes 1572868
  31.5 0.9 copy-start.9
  32.3 0.8 copy-start.10
  37.1 6.9 %copy-start.1 = (bf16[1024,1024]{1,0:T(8,128)(2,1)S(1)}, bf16[1024,1024]{1,0:T(8,128)(2,1)}, u32[]{:S(2)}) copy-start(bf16[1024,1024]{1,0:T(8,128)(2,1)} %get-tuple-element.31.far) | copy-start | bytes 6291460
  37.1 6.9 %copy-start.2 = (f32[1024,128]{1,0:T(8,128)S(1)}, f32[1024,128]{1,0:T(8,128)}, u32[]{:S(2)}) copy-start(f32[1024,128]{1,0:T(8,128)} %cotangent.5) | copy-start | bytes 1572868
  37.1 6.9 %collective-permute-start.4 = (bf16[32,32,384]{2,1,0:T(8,128)(2,1)S(1)}, bf16[32,32,384]{2,1,0:T(8,128)(2,1)S(1)}, u32[]{:S(2)}, u32[]{:S(2)}) collective-permute-start(bf16[32,32,384]{2,1,0:T(8,128)(2,1)S(1)} %all-to-all-done.mine), channel_id=1, source_target_pairs={{0,8},{8,0},{1,9},{9,1},{2,10},{10,2},{3,11},{11,3},{4,12},{12,4},... | collective-permute-start | bytes 2359304 | tf_op jit(solution)/shard_map/ppermute | solution.py:301
  46.7 16.2 %all-to-all-start.1 = ((f32[64,4,128]{2,1,0:T(4,128)}), f32[64,4,128]{2,1,0:T(4,128)S(1)}, u32[]{:S(2)}, u32[]{:S(2)}) async-start(f32[64,4,128]{2,1,0:T(4,128)} %get-tuple-element.34), calls=%async_computation.1 | async-start | bytes 262144 | tf_op jit(solution)/shard_map/all_to_all | solution.py:322
  52.5 1.2 %copy-start.3 = (f32[1024,256]{1,0:T(8,128)S(1)}, f32[1024,256]{1,0:T(8,128)}, u32[]{:S(2)}) copy-start(f32[1024,256]{1,0:T(8,128)} %get-tuple-element.36.kv) | copy-start | bytes 3145732
  53.7 1.0 copy-start.6
  78.5 2.8 %copy-start = (bf16[1024,1024]{1,0:T(8,128)(2,1)S(1)}, bf16[1024,1024]{1,0:T(8,128)(2,1)}, u32[]{:S(2)}) copy-start(bf16[1024,1024]{1,0:T(8,128)(2,1)} %get-tuple-element.38.turned) | copy-start | bytes 6291460
  79.2 4.2 %collective-permute-start.5 = (bf16[1024,384]{1,0:T(8,128)(2,1)S(1)}, bf16[1024,384]{1,0:T(8,128)(2,1)S(1)}, u32[]{:S(2)}, u32[]{:S(2)}) collective-permute-start(bf16[1024,384]{1,0:T(8,128)(2,1)S(1)} %shard_map.57.dproj), channel_id=1, source_target_pairs={{0,8},{8,0},{1,9},{9,1},{2,10},{10,2},{3,11},{11,3},{4,12},{12,4},... | collective-permute-start | bytes 2359304 | tf_op jit(solution)/shard_map/ppermute | solution.py:346
  83.4 5.9 %copy-start.7 = (f32[1024,128]{1,0:T(8,128)S(1)}, f32[1024,128]{1,0:T(8,128)}, u32[]{:S(2)}) copy-start(f32[1024,128]{1,0:T(8,128)} %get-tuple-element.35.query) | copy-start | bytes 1572868
  85.4 25.3 %all-to-all-start.3 = ((bf16[32,32,384]{2,1,0:T(8,128)(2,1)}), bf16[32,32,384]{2,1,0:T(8,128)(2,1)S(1)}, u32[]{:S(2)}, u32[]{:S(2)}) async-start(bf16[32,32,384]{2,1,0:T(8,128)(2,1)} %bitcast.2), calls=%async_computation.3 | async-start | bytes 1572864 | tf_op jit(solution)/shard_map/all_to_all | solution.py:365

commit v8 on v7

--- a/solution.py
+++ b/solution.py
@@ -136,25 +136,23 @@
         partial[rows, :] = mxu(near[rows, :], mine[...].reshape(chips * group, columns))
 
 
-def project_kernel(far, other, partial, cotangent, query, kv, parts, proj, sems):
+def project_kernel(far, other, partial, cotangent, query, kv, parts, held, sems):
     chips, group, columns = other.shape
     stores = []
     for rows in chunks(far.shape[0]):
         weight = other[...].reshape(chips * group, columns)
-        proj[rows, :] = partial[rows, :] + mxu(far[rows, :], weight)
-        for which, target, span in ((0, query, pl.ds(0, HD)), (1, kv, pl.ds(HD, 2 * HD))):
-            stores.append(
-                pltpu.make_async_copy(
-                    proj.at[rows, span], target.at[rows, :], sems.at[len(stores) // 2, which]
-                )
-            )
-            stores[-1].start()
+        part = partial[rows, :] + mxu(far[rows, :], weight)
+        held[rows, :] = part[:, :HD]
+        kv[rows, :] = part[:, HD:]
+        stores.append(
+            pltpu.make_async_copy(held.at[rows, :], query.at[rows, :], sems.at[len(stores)])
+        )
+        stores[-1].start()
     kv_state = jnp.zeros((HD, HD), F32)
     qg_state = jnp.zeros((HD, HD), F32)
-    for rows in chunks(proj.shape[0]):
-        part = proj[rows, :]
-        kv_state += gram(beside(part[:, HD : 2 * HD]), beside(part[:, 2 * HD :]))
-        qg_state += gram(beside(part[:, :HD]), beside(cotangent[rows, :]))
+    for rows in chunks(far.shape[0]):
+        kv_state += gram(beside(kv[rows, :HD]), beside(kv[rows, HD:]))
+        qg_state += gram(beside(held[rows, :]), beside(cotangent[rows, :]))
     piece = HD // chips
     for chip in range(chips):
         parts[chip] = kv_state[chip * piece : (chip + 1) * piece]
@@ -309,15 +307,12 @@
     )
     query, kv, parts = call(
         project_kernel,
-        [direct((tokens, HD)), direct((tokens, 2 * HD)), vmem((devices, piece, HD))],
+        [direct((tokens, HD)), vmem((tokens, 2 * HD)), vmem((devices, piece, HD))],
         [far, other, partial, out_grad],
         2 * tokens * half * columns + 16 * square,
         24,
         [VMEM] * 4,
-        [
-            pltpu.VMEM((tokens, columns), F32),
-            pltpu.SemaphoreType.DMA((tokens // BLOCK, 2)),
-        ],
+        [pltpu.VMEM((tokens, HD), F32), pltpu.SemaphoreType.DMA((tokens // BLOCK,))],
     )
     pieces = lax.all_to_all(parts, RANKS, 0, 0, tiled=True)
     (dlocal,) = call(

time: 113 us -> 112 us (level)
  waiting for transfers between devices: 29.2 us -> 30.5 us
  local copies, waits for them, and re-layouts: 6.83 us -> 5.61 us
    unnamed x22 -> x20, local copies, waits for them, and re-layouts: 6.83 us -> 5.61 us
    all_to_all x1, waiting for transfers between devices: 5.01 us -> 6.23 us  [local(): pieces = lax.all_to_all(parts, RANKS, 0, 0, tiled=True)]
where the time goes in v8:
time: 112 us; the launch traced here: 111 us
  starting transfers between devices  39.6 us (35%)
  waiting for transfers between devices  30.5 us (27%)
  Pallas kernels  19.4 us (17%)
  blocking collectives  14.9 us (13%)
  local copies, waits for them, and re-layouts  5.61 us (5%)
    pallas_call x11, Pallas kernels, call(): pl.pallas_call(body, out_shape=[kind for kind, _ in outs], in_specs=specs...  19.4 us
    all_to_all x1, waiting for transfers between devices, local(): lax.all_to_all(total.reshape(chips, group, columns), 'chip', 0, 0, tiled=...  19.1 us
    all_to_all x1, blocking collectives, local(): back = lax.all_to_all(sums, RANKS, 0, 0, tiled=True)  14.9 us
    all_to_all x1, starting transfers between devices, local(): mine = lax.all_to_all(copies, 'chip', 0, 0, tiled=True)  13.7 us
    ppermute x4, starting transfers between devices, local(): taken = [lax.ppermute(part, 'core', SWAP) for part in give]  9.1 us
    all_to_all x1, waiting for transfers between devices, local(): pieces = lax.all_to_all(parts, RANKS, 0, 0, tiled=True)  6.23 us
    all_to_all x1, starting transfers between devices, local(): pieces = lax.all_to_all(parts, RANKS, 0, 0, tiled=True)  5.73 us
    unnamed x20, local copies, waits for them, and re-layouts  5.61 us
  transfers between devices with their start and end apart: 9, of which 6 were waited for; matrix products, arithmetic and copies ran while one was open for 0% of the time, Pallas kernels for 11%

profile of v8, /device:TPU:1, one launch (start us, length us, event | category | flops | bytes accessed | tf_op | source)
XLA Modules:
  0.0 110.8 jit_solution(11293900482694305996)
XLA Ops:
  0.6 0.7 copy-done.3
  1.4 0.9 shard_map.50
  2.3 13.7 %all-to-all-start = ((bf16[32,32,384]{2,1,0:T(8,128)(2,1)}), bf16[32,32,384]{2,1,0:T(8,128)(2,1)S(1)}, u32[]{:S(2)}, u32[]{:S(2)}) async-start(bf16[32,32,384]{2,1,0:T(8,128)(2,1)} %shard_map.50), calls=%async_computation | async-start | bytes 1572864 | tf_op jit(solution)/shard_map/all_to_all | solution.py:283
  16.0 2.2 %copy-done.4 = bf16[1024,2048]{1,0:T(8,128)(2,1)S(1)} copy-done((bf16[1024,2048]{1,0:T(8,128)(2,1)S(1)}, bf16[1024,2048]{1,0:T(8,128)(2,1)}, u32[]{:S(2)}) %copy-start.4) | copy-done | bytes 4194328
  18.2 4.0 %shard_map.51 = (bf16[1024,1024]{1,0:T(8,128)(2,1)S(1)}, bf16[1024,1024]{1,0:T(8,128)(2,1)}, bf16[1024,1024]{1,0:T(8,128)(2,1)}, bf16[256,1024]{1,0:T(8,128)(2,1...) custom-call(s32[1]{0:T(128)} %bitcast.core, bf16[1024,2048]{1,0:T(8,128)(2,1)S(1)} %copy-done.4), custom_call_target="tpu_custom_call" | custom-call | flops 2147483648 | bytes 4194308 | tf_op jit(solution)/shard_map/pallas_call | solution.py:90
  22.3 2.9 %collective-permute-start = (bf16[256,1024]{1,0:T(8,128)(2,1)}, bf16[256,1024]{1,0:T(8,128)(2,1)S(1)}, u32[]{:S(2)}, u32[]{:S(2)}) collective-permute-start(bf16[256,1024]{1,0:T(8,128)(2,1)} %get-tuple-element.27), channel_id=1, source_target_pairs={{0,8},{8,0},{1,9},{9,1},{2,10},{10,2},{3,11},{11,3},{4,12},{12,4},... | collective-permute-start | bytes 1572872 | tf_op jit(solution)/shard_map/ppermute | solution.py:297
  25.1 1.9 %collective-permute-start.1 = (bf16[256,1024]{1,0:T(8,128)(2,1)}, bf16[256,1024]{1,0:T(8,128)(2,1)S(1)}, u32[]{:S(2)}, u32[]{:S(2)}) collective-permute-start(bf16[256,1024]{1,0:T(8,128)(2,1)} %get-tuple-element.28), channel_id=1, source_target_pairs={{0,8},{8,0},{1,9},{9,1},{2,10},{10,2},{3,11},{11,3},{4,12},{12,4},... | collective-permute-start | bytes 1572872 | tf_op jit(solution)/shard_map/ppermute | solution.py:297
  27.1 2.4 %collective-permute-start.2 = (bf16[256,1024]{1,0:T(8,128)(2,1)}, bf16[256,1024]{1,0:T(8,128)(2,1)S(1)}, u32[]{:S(2)}, u32[]{:S(2)}) collective-permute-start(bf16[256,1024]{1,0:T(8,128)(2,1)} %get-tuple-element.29), channel_id=1, source_target_pairs={{0,8},{8,0},{1,9},{9,1},{2,10},{10,2},{3,11},{11,3},{4,12},{12,4},... | collective-permute-start | bytes 1572872 | tf_op jit(solution)/shard_map/ppermute | solution.py:297
  29.5 1.9 %collective-permute-start.3 = (bf16[256,1024]{1,0:T(8,128)(2,1)}, bf16[256,1024]{1,0:T(8,128)(2,1)}, u32[]{:S(2)}, u32[]{:S(2)}) collective-permute-start(bf16[256,1024]{1,0:T(8,128)(2,1)} %get-tuple-element.30), channel_id=1, source_target_pairs={{0,8},{8,0},{1,9},{9,1},{2,10},{10,2},{3,11},{11,3},{4,12},{12,4},... | collective-permute-start | bytes 1572872 | tf_op jit(solution)/shard_map/ppermute | solution.py:297
  31.5 0.8 copy-done.8
  32.3 0.8 copy-done.9
  33.1 0.5 collective-permute-done.3.refs_3_
  33.6 3.5 %all-to-all-done.mine = bf16[32,32,384]{2,1,0:T(8,128)(2,1)S(1)} async-done(((bf16[32,32,384]{2,1,0:T(8,128)(2,1)}), bf16[32,32,384]{2,1,0:T(8,128)(2,1)S(1)}, u32[]{:S(2)}, u32[]{:S(2)}) %all-to-all-start) | async-done | bytes 786464 | tf_op jit(solution)/shard_map/all_to_all | solution.py:283
  37.1 5.0 %collective-permute-start.4 = (bf16[32,32,384]{2,1,0:T(8,128)(2,1)S(1)}, bf16[32,32,384]{2,1,0:T(8,128)(2,1)S(1)}, u32[]{:S(2)}, u32[]{:S(2)}) collective-permute-start(bf16[32,32,384]{2,1,0:T(8,128)(2,1)S(1)} %all-to-all-done.mine), channel_id=1, source_target_pairs={{0,8},{8,0},{1,9},{9,1},{2,10},{10,2},{3,11},{11,3},{4,12},{12,4},... | collective-permute-start | bytes 2359304 | tf_op jit(solution)/shard_map/ppermute | solution.py:299
  42.1 1.2 %shard_map.52.partial = f32[1024,384]{1,0:T(8,128)S(1)} custom-call(bf16[1024,1024]{1,0:T(8,128)(2,1)S(1)} %get-tuple-element.33.near, bf16[32,32,384]{2,1,0:T(8,128)(2,1)S(1)} %all-to-all-done.mine), custom_call_target="tpu_custom_call" | custom-call | flops 805306368 | bytes 2883584 | tf_op jit(solution)/shard_map/pallas_call | solution.py:90
  43.3 0.6 collective-permute-done.4.other
  44.0 2.6 %shard_map.53 = (f32[1024,128]{1,0:T(8,128)}, f32[1024,256]{1,0:T(8,128)S(1)}, f32[64,4,128]{2,1,0:T(4,128)}) custom-call(bf16[1024,1024]{1,0:T(8,128)(2,1)S(1)} %copy-done.1, bf16[32,32,384]{2,1,0:T(8,128)(2,1)S(1)} %collective-permute-done.4.other, f32[1024,384]{1,0:T(8,128)S(1)} %shard_map.52.partial, f32[1024,128]{1,0:T(8,128)S(1)} %copy-done.2), custom_call_target="tpu_custom_call" | custom-call | flops 1073741824 | bytes 4980736 | tf_op jit(solution)/shard_map/pallas_call | solution.py:90
  46.6 5.7 %all-to-all-start.1 = ((f32[64,4,128]{2,1,0:T(4,128)}), f32[64,4,128]{2,1,0:T(4,128)S(1)}, u32[]{:S(2)}, u32[]{:S(2)}) async-start(f32[64,4,128]{2,1,0:T(4,128)} %get-tuple-element.34), calls=%async_computation.1 | async-start | bytes 262144 | tf_op jit(solution)/shard_map/all_to_all | solution.py:317
  52.4 1.0 copy-done.5
  53.4 3.2 %shard_map.54.dlocal = f32[1024,384]{1,0:T(8,128)S(1)} custom-call(f32[1024,128]{1,0:T(8,128)S(1)} %copy-done.5, f32[1024,256]{1,0:T(8,128)S(1)} %get-tuple-element.36.kv, f32[1024,128]{1,0:T(8,128)S(1)} %copy-done.2), custom_call_target="tpu_custom_call" | custom-call | flops 1509949440 | bytes 2097152 | tf_op jit(solution)/shard_map/pallas_call | solution.py:90
  56.6 6.2 %all-to-all-done.1.pieces = f32[64,4,128]{2,1,0:T(4,128)S(1)} async-done(((f32[64,4,128]{2,1,0:T(4,128)}), f32[64,4,128]{2,1,0:T(4,128)S(1)}, u32[]{:S(2)}, u32[]{:S(2)}) %all-to-all-start.1) | async-done | bytes 131104 | tf_op jit(solution)/shard_map/all_to_all | solution.py:317
  62.8 0.1 shard_map.55
  62.9 14.9 %all_to_all.20.back = f32[64,4,128]{2,1,0:T(4,128)S(1)} all-to-all(f32[64,4,128]{2,1,0:T(4,128)S(1)} %shard_map.55), channel_id=1, replica_groups=mesh['chip'=32,'core'=2,'head'=8] {'core','chip'}, dimensions={0} | all-to-all | bytes 262144 | tf_op jit(solution)/shard_map/all_to_all | solution.py:330
  77.9 0.7 shard_map.57.dproj
  78.5 2.1 %collective-permute-start.5 = (bf16[1024,384]{1,0:T(8,128)(2,1)S(1)}, bf16[1024,384]{1,0:T(8,128)(2,1)S(1)}, u32[]{:S(2)}, u32[]{:S(2)}) collective-permute-start(bf16[1024,384]{1,0:T(8,128)(2,1)S(1)} %shard_map.57.dproj), channel_id=1, source_target_pairs={{0,8},{8,0},{1,9},{9,1},{2,10},{10,2},{3,11},{11,3},{4,12},{12,4},... | collective-permute-start | bytes 2359304 | tf_op jit(solution)/shard_map/ppermute | solution.py:341
  80.7 1.6 %shard_map.58 = (f32[1024,384]{1,0:T(8,128)S(1)}, bf16[1024,1024]{1,0:T(8,128)(2,1)S(1)}) custom-call(bf16[1024,1024]{1,0:T(8,128)(2,1)S(1)} %copy-done, bf16[1024,384]{1,0:T(8,128)(2,1)S(1)} %shard_map.57.dproj, bf16[256,1024]{1,0:T(8,128)(2,1)} %copy-done.7, bf16[256,1024]{1,0:T(8,128)(2,1)} %copy-done.8, bf16[256,1024]{1,0:T(8,128)(2,1)} %copy-done.9, ...), custom_call_target="tpu_custom_call" | custom-call | flops 805306368 | bytes 4980736 | tf_op jit(solution)/shard_map/pallas_call | solution.py:90
  82.2 0.5 collective-permute-done.5.dproj
  82.7 2.0 %shard_map.59 = bf16[1024,384]{1,0:T(8,128)(2,1)} custom-call(bf16[1024,1024]{1,0:T(8,128)(2,1)S(1)} %get-tuple-element.44.turned, bf16[1024,384]{1,0:T(8,128)(2,1)S(1)} %collective-permute-done.5.dproj, f32[1024,384]{1,0:T(8,128)S(1)} %get-tuple-element.45.product), custom_call_target="tpu_custom_call" | custom-call | flops 805306368 | bytes 4456448 | tf_op jit(solution)/shard_map/pallas_call | solution.py:90
  84.7 3.9 %all-to-all-start.3 = ((bf16[32,32,384]{2,1,0:T(8,128)(2,1)}), bf16[32,32,384]{2,1,0:T(8,128)(2,1)S(1)}, u32[]{:S(2)}, u32[]{:S(2)}) async-start(bf16[32,32,384]{2,1,0:T(8,128)(2,1)} %bitcast.2), calls=%async_computation.3 | async-start | bytes 1572864 | tf_op jit(solution)/shard_map/all_to_all | solution.py:360
  88.6 2.3 %shard_map.56 = f32[1024,128]{1,0:T(8,128)} custom-call(f32[64,4,128]{2,1,0:T(4,128)S(1)} %all_to_all.20.back, f32[1024,128]{1,0:T(8,128)S(1)} %copy-done.6, f32[1024,256]{1,0:T(8,128)S(1)} %get-tuple-element.36.kv), custom_call_target="tpu_custom_call" | custom-call | flops 603979776 | bytes 1703936 | tf_op jit(solution)/shard_map/pallas_call | solution.py:90
  90.9 19.1 %all-to-all-done.3.landed = bf16[32,32,384]{2,1,0:T(8,128)(2,1)S(1)} async-done(((bf16[32,32,384]{2,1,0:T(8,128)(2,1)}), bf16[32,32,384]{2,1,0:T(8,128)(2,1)S(1)}, u32[]{:S(2)}, u32[]{:S(2)}) %all-to-all-start.3) | async-done | bytes 786464 | tf_op jit(solution)/shard_map/all_to_all | solution.py:360
  110.0 0.7 shard_map.60
  (18 shorter events, 0.0 us)
Async XLA Ops:
  0.6 0.7 copy-start.3
  2.3 34.8 %all-to-all-start = ((bf16[32,32,384]{2,1,0:T(8,128)(2,1)}), bf16[32,32,384]{2,1,0:T(8,128)(2,1)S(1)}, u32[]{:S(2)}, u32[]{:S(2)}) async-start(bf16[32,32,384]{2,1,0:T(8,128)(2,1)} %shard_map.50), calls=%async_computation | async-start | bytes 1572864 | tf_op jit(solution)/shard_map/all_to_all | solution.py:283
  16.0 2.2 %copy-start.4 = (bf16[1024,2048]{1,0:T(8,128)(2,1)S(1)}, bf16[1024,2048]{1,0:T(8,128)(2,1)}, u32[]{:S(2)}) copy-start(bf16[1024,2048]{1,0:T(8,128)(2,1)} %hidden.1) | copy-start | bytes 12582916
  22.3 9.1 %collective-permute-start = (bf16[256,1024]{1,0:T(8,128)(2,1)}, bf16[256,1024]{1,0:T(8,128)(2,1)S(1)}, u32[]{:S(2)}, u32[]{:S(2)}) collective-permute-start(bf16[256,1024]{1,0:T(8,128)(2,1)} %get-tuple-element.27), channel_id=1, source_target_pairs={{0,8},{8,0},{1,9},{9,1},{2,10},{10,2},{3,11},{11,3},{4,12},{12,4},... | collective-permute-start | bytes 1572872 | tf_op jit(solution)/shard_map/ppermute | solution.py:297
  25.1 6.3 %collective-permute-start.1 = (bf16[256,1024]{1,0:T(8,128)(2,1)}, bf16[256,1024]{1,0:T(8,128)(2,1)S(1)}, u32[]{:S(2)}, u32[]{:S(2)}) collective-permute-start(bf16[256,1024]{1,0:T(8,128)(2,1)} %get-tuple-element.28), channel_id=1, source_target_pairs={{0,8},{8,0},{1,9},{9,1},{2,10},{10,2},{3,11},{11,3},{4,12},{12,4},... | collective-permute-start | bytes 1572872 | tf_op jit(solution)/shard_map/ppermute | solution.py:297
  27.1 4.4 %collective-permute-start.2 = (bf16[256,1024]{1,0:T(8,128)(2,1)}, bf16[256,1024]{1,0:T(8,128)(2,1)S(1)}, u32[]{:S(2)}, u32[]{:S(2)}) collective-permute-start(bf16[256,1024]{1,0:T(8,128)(2,1)} %get-tuple-element.29), channel_id=1, source_target_pairs={{0,8},{8,0},{1,9},{9,1},{2,10},{10,2},{3,11},{11,3},{4,12},{12,4},... | collective-permute-start | bytes 1572872 | tf_op jit(solution)/shard_map/ppermute | solution.py:297
  29.5 4.1 %collective-permute-start.3 = (bf16[256,1024]{1,0:T(8,128)(2,1)}, bf16[256,1024]{1,0:T(8,128)(2,1)}, u32[]{:S(2)}, u32[]{:S(2)}) collective-permute-start(bf16[256,1024]{1,0:T(8,128)(2,1)} %get-tuple-element.30), channel_id=1, source_target_pairs={{0,8},{8,0},{1,9},{9,1},{2,10},{10,2},{3,11},{11,3},{4,12},{12,4},... | collective-permute-start | bytes 1572872 | tf_op jit(solution)/shard_map/ppermute | solution.py:297
  31.4 5.7 %copy-start.7 = (bf16[256,1024]{1,0:T(8,128)(2,1)}, bf16[256,1024]{1,0:T(8,128)(2,1)S(1)}, u32[]{:S(2)}) copy-start(bf16[256,1024]{1,0:T(8,128)(2,1)S(1)} %collective-permute-done.refs_0_) | copy-start | bytes 1572868
  31.4 0.9 copy-start.8
  32.3 0.8 copy-start.9
  37.1 6.9 %copy-start.1 = (bf16[1024,1024]{1,0:T(8,128)(2,1)S(1)}, bf16[1024,1024]{1,0:T(8,128)(2,1)}, u32[]{:S(2)}) copy-start(bf16[1024,1024]{1,0:T(8,128)(2,1)} %get-tuple-element.31.far) | copy-start | bytes 6291460
  37.1 6.9 %copy-start.2 = (f32[1024,128]{1,0:T(8,128)S(1)}, f32[1024,128]{1,0:T(8,128)}, u32[]{:S(2)}) copy-start(f32[1024,128]{1,0:T(8,128)} %cotangent.5) | copy-start | bytes 1572868
  37.1 6.9 %collective-permute-start.4 = (bf16[32,32,384]{2,1,0:T(8,128)(2,1)S(1)}, bf16[32,32,384]{2,1,0:T(8,128)(2,1)S(1)}, u32[]{:S(2)}, u32[]{:S(2)}) collective-permute-start(bf16[32,32,384]{2,1,0:T(8,128)(2,1)S(1)} %all-to-all-done.mine), channel_id=1, source_target_pairs={{0,8},{8,0},{1,9},{9,1},{2,10},{10,2},{3,11},{11,3},{4,12},{12,4},... | collective-permute-start | bytes 2359304 | tf_op jit(solution)/shard_map/ppermute | solution.py:299
  46.6 16.2 %all-to-all-start.1 = ((f32[64,4,128]{2,1,0:T(4,128)}), f32[64,4,128]{2,1,0:T(4,128)S(1)}, u32[]{:S(2)}, u32[]{:S(2)}) async-start(f32[64,4,128]{2,1,0:T(4,128)} %get-tuple-element.34), calls=%async_computation.1 | async-start | bytes 262144 | tf_op jit(solution)/shard_map/all_to_all | solution.py:317
  52.3 1.0 copy-start.5
  77.9 2.8 %copy-start = (bf16[1024,1024]{1,0:T(8,128)(2,1)S(1)}, bf16[1024,1024]{1,0:T(8,128)(2,1)}, u32[]{:S(2)}) copy-start(bf16[1024,1024]{1,0:T(8,128)(2,1)} %get-tuple-element.38.turned) | copy-start | bytes 6291460
  78.5 4.2 %collective-permute-start.5 = (bf16[1024,384]{1,0:T(8,128)(2,1)S(1)}, bf16[1024,384]{1,0:T(8,128)(2,1)S(1)}, u32[]{:S(2)}, u32[]{:S(2)}) collective-permute-start(bf16[1024,384]{1,0:T(8,128)(2,1)S(1)} %shard_map.57.dproj), channel_id=1, source_target_pairs={{0,8},{8,0},{1,9},{9,1},{2,10},{10,2},{3,11},{11,3},{4,12},{12,4},... | collective-permute-start | bytes 2359304 | tf_op jit(solution)/shard_map/ppermute | solution.py:341
  82.7 5.9 %copy-start.6 = (f32[1024,128]{1,0:T(8,128)S(1)}, f32[1024,128]{1,0:T(8,128)}, u32[]{:S(2)}) copy-start(f32[1024,128]{1,0:T(8,128)} %get-tuple-element.35.query) | copy-start | bytes 1572868
  84.7 25.4 %all-to-all-start.3 = ((bf16[32,32,384]{2,1,0:T(8,128)(2,1)}), bf16[32,32,384]{2,1,0:T(8,128)(2,1)S(1)}, u32[]{:S(2)}, u32[]{:S(2)}) async-start(bf16[32,32,384]{2,1,0:T(8,128)(2,1)} %bitcast.2), calls=%async_computation.3 | async-start | bytes 1572864 | tf_op jit(solution)/shard_map/all_to_all | solution.py:360

commit v9 on v8

--- a/solution.py
+++ b/solution.py
@@ -161,7 +161,7 @@
         store.wait()
 
 
-def local_kernel(query, kv, cotangent, dlocal):
+def local_kernel(query, kv, cotangent, dlocal, inner):
     mask = causal()
     order = chunks(query.shape[0])
     state = jnp.zeros((HD, HD), F32)
@@ -171,8 +171,11 @@
         scores = jnp.where(mask, cross(queries, keys), 0.0)
         dmat = jnp.where(mask, cross(cot, values), 0.0)
         dquery = times(beside(dmat), doubled(keys))
+        out = times(beside(scores), doubled(values))
         if rows is not order[0]:
             dquery += times(cot, doubled(state.T))
+            out += times(queries, doubled(state))
+        inner[rows, :] = out
         dlocal[rows, 0:HD] = dquery
         dlocal[rows, HD : 2 * HD] = gram(beside(dmat), queries)
         dlocal[rows, 2 * HD :] = gram(beside(scores), cot)
@@ -218,17 +221,10 @@
             dproj[rows, columns] = (scale * (dlocal[rows, columns] + term)).astype(BF16)
 
 
-def attended_kernel(scale, back, query, kv, attended, states):
-    state = joined(back, 0, states)
-    mask = causal()
+def attended_kernel(scale, back, query, inner, attended, states):
+    prefix = doubled(joined(back, 0, states))
     for rows in chunks(query.shape[0]):
-        keys, values = kv[rows, :HD], kv[rows, HD:]
-        queries = beside(query[rows, :])
-        scores = jnp.where(mask, cross(queries, keys), 0.0)
-        attended[rows, :] = scale * (
-            times(beside(scores), doubled(values)) + times(queries, doubled(state))
-        )
-        state += gram(beside(keys), beside(values))
+        attended[rows, :] = scale * (inner[rows, :] + times(beside(query[rows, :]), prefix))
 
 
 def own_kernel(turned, dproj, *refs):
@@ -246,14 +242,9 @@
         load.wait()
 
 
-def total_kernel(turned, dproj, product, total, rows_out, sems):
-    stores = []
-    for index, rows in enumerate(chunks(turned.shape[0])):
-        rows_out[rows, :] = (product[rows, :] + mxu(turned[rows, :], dproj[...])).astype(BF16)
-        stores.append(pltpu.make_async_copy(rows_out.at[rows, :], total.at[rows, :], sems.at[index]))
-        stores[-1].start()
-    for store in stores:
-        store.wait()
+def total_kernel(turned, dproj, product, total):
+    for rows in chunks(turned.shape[0]):
+        total[rows, :] = (product[rows, :] + mxu(turned[rows, :], dproj[...])).astype(BF16)
 
 
 def sum_kernel(scale, landed, grad):
@@ -315,9 +306,9 @@
         [pltpu.VMEM((tokens, HD), F32), pltpu.SemaphoreType.DMA((tokens // BLOCK,))],
     )
     pieces = lax.all_to_all(parts, RANKS, 0, 0, tiled=True)
-    (dlocal,) = call(
+    dlocal, inner = call(
         local_kernel,
-        [vmem((tokens, columns))],
+        [vmem((tokens, columns)), hbm((tokens, HD))],
         [query, kv, out_grad],
         15 * 6 * square,
         24,
@@ -348,25 +339,25 @@
         [VMEM, VMEM] + [HBM] * PARTS,
         [pltpu.SemaphoreType.DMA((PARTS,))],
     )
-    (total,) = call(
-        total_kernel,
-        [direct((half, columns), BF16)],
-        [held, theirs, product],
-        2 * half * tokens * columns,
-        24,
-        [VMEM] * 3,
-        [pltpu.VMEM((half, columns), BF16), pltpu.SemaphoreType.DMA((half // BLOCK,))],
-    )
-    landed = lax.all_to_all(total.reshape(chips, group, columns), "chip", 0, 0, tiled=True)
     (attended,) = call(
         functools.partial(attended_kernel, scale),
         [hbm((tokens, HD))],
-        [back, query, kv],
-        6 * 6 * square,
+        [back, query, inner],
+        4 * square,
         24,
         [VMEM] * 3,
         states,
     )
+    product, held, attended = lax.optimization_barrier((product, held, attended))
+    (total,) = call(
+        total_kernel,
+        [vmem((half, columns), BF16)],
+        [held, theirs, product],
+        2 * half * tokens * columns,
+        24,
+        [VMEM] * 3,
+    )
+    landed = lax.all_to_all(total.reshape(chips, group, columns), "chip", 0, 0, tiled=True)
     (grad,) = call(
         functools.partial(sum_kernel, grad_scale),
         [hbm((group, columns))],

time: 112 us -> 112 us (level)
  blocking collectives: 14.9 us -> 40.6 us
  waiting for transfers between devices: 30.5 us -> 10.4 us
  starting transfers between devices: 39.6 us -> 35.8 us
  Pallas kernels: 19.4 us -> 17.8 us
    all_to_all x0 -> x1, blocking collectives: none -> 25.6 us  [local(): lax.all_to_all(total.reshape(chips, group, columns), 'chip', 0, 0, tiled=...]
    all_to_all x1 -> x0, waiting for transfers between devices: 19.1 us -> none  [local(): lax.all_to_all(total.reshape(chips, group, columns), 'chip', 0, 0, tiled=...]
    all_to_all x1 -> x0, starting transfers between devices: 3.92 us -> none  [local(): lax.all_to_all(total.reshape(chips, group, columns), 'chip', 0, 0, tiled=...]
    pallas_call x11, Pallas kernels: 19.4 us -> 17.8 us  [call(): pl.pallas_call(body, out_shape=[kind for kind, _ in outs], in_specs=specs...]
    unnamed x20 -> x22, local copies, waits for them, and re-layouts: 5.61 us -> 5.77 us
  transfers between devices with their start and end apart: 9 -> 8, of which waited for: 6 -> 4; matrix products, arithmetic and copies ran while one was open for 0% -> 0% of each run, Pallas kernels for 11% -> 10%
where the time goes in v9:
time: 112 us; the launch traced here: 111 us
  blocking collectives  40.6 us (36%)
  starting transfers between devices  35.8 us (32%)
  Pallas kernels  17.8 us (16%)
  waiting for transfers between devices  10.4 us (9%)
  local copies, waits for them, and re-layouts  5.77 us (5%)
    all_to_all x1, blocking collectives, local(): lax.all_to_all(total.reshape(chips, group, columns), 'chip', 0, 0, tiled=...  25.6 us
    pallas_call x11, Pallas kernels, call(): pl.pallas_call(body, out_shape=[kind for kind, _ in outs], in_specs=specs...  17.8 us
    all_to_all x1, blocking collectives, local(): back = lax.all_to_all(sums, RANKS, 0, 0, tiled=True)  14.9 us
    all_to_all x1, starting transfers between devices, local(): mine = lax.all_to_all(copies, 'chip', 0, 0, tiled=True)  13.7 us
    ppermute x4, starting transfers between devices, local(): taken = [lax.ppermute(part, 'core', SWAP) for part in give]  9.1 us
    all_to_all x1, waiting for transfers between devices, local(): pieces = lax.all_to_all(parts, RANKS, 0, 0, tiled=True)  5.89 us
    unnamed x22, local copies, waits for them, and re-layouts  5.77 us
    all_to_all x1, starting transfers between devices, local(): pieces = lax.all_to_all(parts, RANKS, 0, 0, tiled=True)  5.73 us
  transfers between devices with their start and end apart: 8, of which 4 were waited for; matrix products, arithmetic and copies ran while one was open for 0% of the time, Pallas kernels for 10%

profile of v9, /device:TPU:1, one launch (start us, length us, event | category | flops | bytes accessed | tf_op | source)
XLA Modules:
  0.0 111.1 jit_solution(12499673984528751309)
XLA Ops:
  0.6 0.7 copy-done.6
  1.4 0.9 shard_map.50
  2.3 13.7 %all-to-all-start = ((bf16[32,32,384]{2,1,0:T(8,128)(2,1)}), bf16[32,32,384]{2,1,0:T(8,128)(2,1)S(1)}, u32[]{:S(2)}, u32[]{:S(2)}) async-start(bf16[32,32,384]{2,1,0:T(8,128)(2,1)} %shard_map.50), calls=%async_computation | async-start | bytes 1572864 | tf_op jit(solution)/shard_map/all_to_all | solution.py:274
  16.0 0.0 copy-start.7
  16.0 2.2 %copy-done.7 = bf16[1024,2048]{1,0:T(8,128)(2,1)S(1)} copy-done((bf16[1024,2048]{1,0:T(8,128)(2,1)S(1)}, bf16[1024,2048]{1,0:T(8,128)(2,1)}, u32[]{:S(2)}) %copy-start.7) | copy-done | bytes 4194328
  18.2 4.1 %shard_map.51 = (bf16[1024,1024]{1,0:T(8,128)(2,1)S(1)}, bf16[1024,1024]{1,0:T(8,128)(2,1)}, bf16[1024,1024]{1,0:T(8,128)(2,1)}, bf16[256,1024]{1,0:T(8,128)(2,1...) custom-call(s32[1]{0:T(128)} %bitcast.core, bf16[1024,2048]{1,0:T(8,128)(2,1)S(1)} %copy-done.7), custom_call_target="tpu_custom_call" | custom-call | flops 2147483648 | bytes 4194308 | tf_op jit(solution)/shard_map/pallas_call | solution.py:90
  22.3 2.9 %collective-permute-start = (bf16[256,1024]{1,0:T(8,128)(2,1)}, bf16[256,1024]{1,0:T(8,128)(2,1)S(1)}, u32[]{:S(2)}, u32[]{:S(2)}) collective-permute-start(bf16[256,1024]{1,0:T(8,128)(2,1)} %get-tuple-element.32), channel_id=1, source_target_pairs={{0,8},{8,0},{1,9},{9,1},{2,10},{10,2},{3,11},{11,3},{4,12},{12,4},... | collective-permute-start | bytes 1572872 | tf_op jit(solution)/shard_map/ppermute | solution.py:288
  25.2 1.9 %collective-permute-start.1 = (bf16[256,1024]{1,0:T(8,128)(2,1)}, bf16[256,1024]{1,0:T(8,128)(2,1)S(1)}, u32[]{:S(2)}, u32[]{:S(2)}) collective-permute-start(bf16[256,1024]{1,0:T(8,128)(2,1)} %get-tuple-element.33), channel_id=1, source_target_pairs={{0,8},{8,0},{1,9},{9,1},{2,10},{10,2},{3,11},{11,3},{4,12},{12,4},... | collective-permute-start | bytes 1572872 | tf_op jit(solution)/shard_map/ppermute | solution.py:288
  27.1 2.4 %collective-permute-start.2 = (bf16[256,1024]{1,0:T(8,128)(2,1)}, bf16[256,1024]{1,0:T(8,128)(2,1)S(1)}, u32[]{:S(2)}, u32[]{:S(2)}) collective-permute-start(bf16[256,1024]{1,0:T(8,128)(2,1)} %get-tuple-element.34), channel_id=1, source_target_pairs={{0,8},{8,0},{1,9},{9,1},{2,10},{10,2},{3,11},{11,3},{4,12},{12,4},... | collective-permute-start | bytes 1572872 | tf_op jit(solution)/shard_map/ppermute | solution.py:288
  29.5 1.9 %collective-permute-start.3 = (bf16[256,1024]{1,0:T(8,128)(2,1)}, bf16[256,1024]{1,0:T(8,128)(2,1)}, u32[]{:S(2)}, u32[]{:S(2)}) collective-permute-start(bf16[256,1024]{1,0:T(8,128)(2,1)} %get-tuple-element.35), channel_id=1, source_target_pairs={{0,8},{8,0},{1,9},{9,1},{2,10},{10,2},{3,11},{11,3},{4,12},{12,4},... | collective-permute-start | bytes 1572872 | tf_op jit(solution)/shard_map/ppermute | solution.py:288
  31.5 0.8 copy-done.8
  32.3 0.2 copy-done.9
  32.5 0.8 copy-done.10
  33.3 0.4 collective-permute-done.3.refs_3_
  33.7 3.4 %all-to-all-done.mine = bf16[32,32,384]{2,1,0:T(8,128)(2,1)S(1)} async-done(((bf16[32,32,384]{2,1,0:T(8,128)(2,1)}), bf16[32,32,384]{2,1,0:T(8,128)(2,1)S(1)}, u32[]{:S(2)}, u32[]{:S(2)}) %all-to-all-start) | async-done | bytes 786464 | tf_op jit(solution)/shard_map/all_to_all | solution.py:274
  37.1 5.0 %collective-permute-start.4 = (bf16[32,32,384]{2,1,0:T(8,128)(2,1)S(1)}, bf16[32,32,384]{2,1,0:T(8,128)(2,1)S(1)}, u32[]{:S(2)}, u32[]{:S(2)}) collective-permute-start(bf16[32,32,384]{2,1,0:T(8,128)(2,1)S(1)} %all-to-all-done.mine), channel_id=1, source_target_pairs={{0,8},{8,0},{1,9},{9,1},{2,10},{10,2},{3,11},{11,3},{4,12},{12,4},... | collective-permute-start | bytes 2359304 | tf_op jit(solution)/shard_map/ppermute | solution.py:290
  42.1 1.2 %shard_map.52.partial = f32[1024,384]{1,0:T(8,128)S(1)} custom-call(bf16[1024,1024]{1,0:T(8,128)(2,1)S(1)} %get-tuple-element.39.near, bf16[32,32,384]{2,1,0:T(8,128)(2,1)S(1)} %all-to-all-done.mine), custom_call_target="tpu_custom_call" | custom-call | flops 805306368 | bytes 2883584 | tf_op jit(solution)/shard_map/pallas_call | solution.py:90
  43.3 0.6 collective-permute-done.4.other
  44.0 2.6 %shard_map.53 = (f32[1024,128]{1,0:T(8,128)}, f32[1024,256]{1,0:T(8,128)S(1)}, f32[64,4,128]{2,1,0:T(4,128)}) custom-call(bf16[1024,1024]{1,0:T(8,128)(2,1)S(1)} %copy-done.1, bf16[32,32,384]{2,1,0:T(8,128)(2,1)S(1)} %collective-permute-done.4.other, f32[1024,384]{1,0:T(8,128)S(1)} %shard_map.52.partial, f32[1024,128]{1,0:T(8,128)S(1)} %copy-done.2), custom_call_target="tpu_custom_call" | custom-call | flops 1073741824 | bytes 4980736 | tf_op jit(solution)/shard_map/pallas_call | solution.py:90
  46.6 5.7 %all-to-all-start.1 = ((f32[64,4,128]{2,1,0:T(4,128)}), f32[64,4,128]{2,1,0:T(4,128)S(1)}, u32[]{:S(2)}, u32[]{:S(2)}) async-start(f32[64,4,128]{2,1,0:T(4,128)} %get-tuple-element.40), calls=%async_computation.1 | async-start | bytes 262144 | tf_op jit(solution)/shard_map/all_to_all | solution.py:308
  52.4 1.0 copy-done.3
  53.4 3.5 %shard_map.54 = (f32[1024,384]{1,0:T(8,128)S(1)}, f32[1024,128]{1,0:T(8,128)}) custom-call(f32[1024,128]{1,0:T(8,128)S(1)} %copy-done.3, f32[1024,256]{1,0:T(8,128)S(1)} %get-tuple-element.42.kv, f32[1024,128]{1,0:T(8,128)S(1)} %copy-done.2), custom_call_target="tpu_custom_call" | custom-call | flops 1509949440 | bytes 2097152 | tf_op jit(solution)/shard_map/pallas_call | solution.py:90
  56.9 5.9 %all-to-all-done.1.pieces = f32[64,4,128]{2,1,0:T(4,128)S(1)} async-done(((f32[64,4,128]{2,1,0:T(4,128)}), f32[64,4,128]{2,1,0:T(4,128)S(1)}, u32[]{:S(2)}, u32[]{:S(2)}) %all-to-all-start.1) | async-done | bytes 131104 | tf_op jit(solution)/shard_map/all_to_all | solution.py:308
  62.8 0.1 shard_map.55
  62.9 14.9 %all_to_all.20.back = f32[64,4,128]{2,1,0:T(4,128)S(1)} all-to-all(f32[64,4,128]{2,1,0:T(4,128)S(1)} %shard_map.55), channel_id=1, replica_groups=mesh['chip'=32,'core'=2,'head'=8] {'core','chip'}, dimensions={0} | all-to-all | bytes 262144 | tf_op jit(solution)/shard_map/all_to_all | solution.py:321
  77.9 0.7 shard_map.56.dproj
  78.5 2.2 %collective-permute-start.5 = (bf16[1024,384]{1,0:T(8,128)(2,1)S(1)}, bf16[1024,384]{1,0:T(8,128)(2,1)S(1)}, u32[]{:S(2)}, u32[]{:S(2)}) collective-permute-start(bf16[1024,384]{1,0:T(8,128)(2,1)S(1)} %shard_map.56.dproj), channel_id=1, source_target_pairs={{0,8},{8,0},{1,9},{9,1},{2,10},{10,2},{3,11},{11,3},{4,12},{12,4},... | collective-permute-start | bytes 2359304 | tf_op jit(solution)/shard_map/ppermute | solution.py:332
  80.8 1.1 %shard_map.58 = f32[1024,128]{1,0:T(8,128)} custom-call(f32[64,4,128]{2,1,0:T(4,128)S(1)} %all_to_all.20.back, f32[1024,128]{1,0:T(8,128)S(1)} %copy-done.4, f32[1024,128]{1,0:T(8,128)S(1)} %copy-done.5), custom_call_target="tpu_custom_call" | custom-call | flops 67108864 | bytes 1179648 | tf_op jit(solution)/shard_map/pallas_call | solution.py:90
  81.9 1.6 %shard_map.57 = (f32[1024,384]{1,0:T(8,128)S(1)}, bf16[1024,1024]{1,0:T(8,128)(2,1)S(1)}) custom-call(bf16[1024,1024]{1,0:T(8,128)(2,1)S(1)} %copy-done, bf16[1024,384]{1,0:T(8,128)(2,1)S(1)} %shard_map.56.dproj, bf16[256,1024]{1,0:T(8,128)(2,1)} %copy-done.8, bf16[256,1024]{1,0:T(8,128)(2,1)} %copy-done.9, bf16[256,1024]{1,0:T(8,128)(2,1)} %copy-done.10, ...), custom_call_target="tpu_custom_call" | custom-call | flops 805306368 | bytes 4980736 | tf_op jit(solution)/shard_map/pallas_call | solution.py:90
  83.5 1.3 %shard_map.59 = bf16[1024,384]{1,0:T(8,128)(2,1)S(1)} custom-call(bf16[1024,1024]{1,0:T(8,128)(2,1)S(1)} %get-tuple-element.54.turned, bf16[1024,384]{1,0:T(8,128)(2,1)S(1)} %collective-permute-done.5.dproj, f32[1024,384]{1,0:T(8,128)S(1)} %get-tuple-element.55.product), custom_call_target="tpu_custom_call" | custom-call | flops 805306368 | bytes 4456448 | tf_op jit(solution)/shard_map/pallas_call | solution.py:90
  84.8 25.6 %all_to_all.21.landed = bf16[32,32,384]{2,1,0:T(8,128)(2,1)S(1)} all-to-all(bf16[32,32,384]{2,1,0:T(8,128)(2,1)S(1)} %bitcast.2), channel_id=1, replica_groups=mesh['chip'=32,'core'=2,'head'=8] {'chip'}, dimensions={0} | all-to-all | bytes 1572864 | tf_op jit(solution)/shard_map/all_to_all | solution.py:360
  110.4 0.7 shard_map.60
  (19 shorter events, 0.0 us)
Async XLA Ops:
  0.6 0.7 copy-start.6
  2.3 34.8 %all-to-all-start = ((bf16[32,32,384]{2,1,0:T(8,128)(2,1)}), bf16[32,32,384]{2,1,0:T(8,128)(2,1)S(1)}, u32[]{:S(2)}, u32[]{:S(2)}) async-start(bf16[32,32,384]{2,1,0:T(8,128)(2,1)} %shard_map.50), calls=%async_computation | async-start | bytes 1572864 | tf_op jit(solution)/shard_map/all_to_all | solution.py:274
  16.0 2.2 %copy-start.7 = (bf16[1024,2048]{1,0:T(8,128)(2,1)S(1)}, bf16[1024,2048]{1,0:T(8,128)(2,1)}, u32[]{:S(2)}) copy-start(bf16[1024,2048]{1,0:T(8,128)(2,1)} %hidden.1) | copy-start | bytes 12582916
  22.3 9.1 %collective-permute-start = (bf16[256,1024]{1,0:T(8,128)(2,1)}, bf16[256,1024]{1,0:T(8,128)(2,1)S(1)}, u32[]{:S(2)}, u32[]{:S(2)}) collective-permute-start(bf16[256,1024]{1,0:T(8,128)(2,1)} %get-tuple-element.32), channel_id=1, source_target_pairs={{0,8},{8,0},{1,9},{9,1},{2,10},{10,2},{3,11},{11,3},{4,12},{12,4},... | collective-permute-start | bytes 1572872 | tf_op jit(solution)/shard_map/ppermute | solution.py:288
  25.2 6.3 %collective-permute-start.1 = (bf16[256,1024]{1,0:T(8,128)(2,1)}, bf16[256,1024]{1,0:T(8,128)(2,1)S(1)}, u32[]{:S(2)}, u32[]{:S(2)}) collective-permute-start(bf16[256,1024]{1,0:T(8,128)(2,1)} %get-tuple-element.33), channel_id=1, source_target_pairs={{0,8},{8,0},{1,9},{9,1},{2,10},{10,2},{3,11},{11,3},{4,12},{12,4},... | collective-permute-start | bytes 1572872 | tf_op jit(solution)/shard_map/ppermute | solution.py:288
  27.1 4.4 %collective-permute-start.2 = (bf16[256,1024]{1,0:T(8,128)(2,1)}, bf16[256,1024]{1,0:T(8,128)(2,1)S(1)}, u32[]{:S(2)}, u32[]{:S(2)}) collective-permute-start(bf16[256,1024]{1,0:T(8,128)(2,1)} %get-tuple-element.34), channel_id=1, source_target_pairs={{0,8},{8,0},{1,9},{9,1},{2,10},{10,2},{3,11},{11,3},{4,12},{12,4},... | collective-permute-start | bytes 1572872 | tf_op jit(solution)/shard_map/ppermute | solution.py:288
  29.5 4.1 %collective-permute-start.3 = (bf16[256,1024]{1,0:T(8,128)(2,1)}, bf16[256,1024]{1,0:T(8,128)(2,1)}, u32[]{:S(2)}, u32[]{:S(2)}) collective-permute-start(bf16[256,1024]{1,0:T(8,128)(2,1)} %get-tuple-element.35), channel_id=1, source_target_pairs={{0,8},{8,0},{1,9},{9,1},{2,10},{10,2},{3,11},{11,3},{4,12},{12,4},... | collective-permute-start | bytes 1572872 | tf_op jit(solution)/shard_map/ppermute | solution.py:288
  31.4 0.8 copy-start.8
  31.5 1.0 copy-start.9
  32.5 0.8 copy-start.10
  37.1 6.9 %copy-start.1 = (bf16[1024,1024]{1,0:T(8,128)(2,1)S(1)}, bf16[1024,1024]{1,0:T(8,128)(2,1)}, u32[]{:S(2)}) copy-start(bf16[1024,1024]{1,0:T(8,128)(2,1)} %get-tuple-element.37.far) | copy-start | bytes 6291460
  37.1 6.9 %copy-start.2 = (f32[1024,128]{1,0:T(8,128)S(1)}, f32[1024,128]{1,0:T(8,128)}, u32[]{:S(2)}) copy-start(f32[1024,128]{1,0:T(8,128)} %cotangent.5) | copy-start | bytes 1572868
  37.1 6.9 %collective-permute-start.4 = (bf16[32,32,384]{2,1,0:T(8,128)(2,1)S(1)}, bf16[32,32,384]{2,1,0:T(8,128)(2,1)S(1)}, u32[]{:S(2)}, u32[]{:S(2)}) collective-permute-start(bf16[32,32,384]{2,1,0:T(8,128)(2,1)S(1)} %all-to-all-done.mine), channel_id=1, source_target_pairs={{0,8},{8,0},{1,9},{9,1},{2,10},{10,2},{3,11},{11,3},{4,12},{12,4},... | collective-permute-start | bytes 2359304 | tf_op jit(solution)/shard_map/ppermute | solution.py:290
  46.6 16.2 %all-to-all-start.1 = ((f32[64,4,128]{2,1,0:T(4,128)}), f32[64,4,128]{2,1,0:T(4,128)S(1)}, u32[]{:S(2)}, u32[]{:S(2)}) async-start(f32[64,4,128]{2,1,0:T(4,128)} %get-tuple-element.40), calls=%async_computation.1 | async-start | bytes 262144 | tf_op jit(solution)/shard_map/all_to_all | solution.py:308
  52.3 1.0 copy-start.3
  77.9 2.9 %copy-start.4 = (f32[1024,128]{1,0:T(8,128)S(1)}, f32[1024,128]{1,0:T(8,128)}, u32[]{:S(2)}) copy-start(f32[1024,128]{1,0:T(8,128)} %get-tuple-element.41.query) | copy-start | bytes 1572868
  77.9 2.9 %copy-start.5 = (f32[1024,128]{1,0:T(8,128)S(1)}, f32[1024,128]{1,0:T(8,128)}, u32[]{:S(2)}) copy-start(f32[1024,128]{1,0:T(8,128)} %get-tuple-element.52.inner) | copy-start | bytes 1572868
  77.9 4.1 %copy-start = (bf16[1024,1024]{1,0:T(8,128)(2,1)S(1)}, bf16[1024,1024]{1,0:T(8,128)(2,1)}, u32[]{:S(2)}) copy-start(bf16[1024,1024]{1,0:T(8,128)(2,1)} %get-tuple-element.36.turned) | copy-start | bytes 6291460
  78.5 5.0 %collective-permute-start.5 = (bf16[1024,384]{1,0:T(8,128)(2,1)S(1)}, bf16[1024,384]{1,0:T(8,128)(2,1)S(1)}, u32[]{:S(2)}, u32[]{:S(2)}) collective-permute-start(bf16[1024,384]{1,0:T(8,128)(2,1)S(1)} %shard_map.56.dproj), channel_id=1, source_target_pairs={{0,8},{8,0},{1,9},{9,1},{2,10},{10,2},{3,11},{11,3},{4,12},{12,4},... | collective-permute-start | bytes 2359304 | tf_op jit(solution)/shard_map/ppermute | solution.py:332

commit v10 on v9

--- a/solution.py
+++ b/solution.py
@@ -221,14 +221,8 @@
             dproj[rows, columns] = (scale * (dlocal[rows, columns] + term)).astype(BF16)
 
 
-def attended_kernel(scale, back, query, inner, attended, states):
-    prefix = doubled(joined(back, 0, states))
-    for rows in chunks(query.shape[0]):
-        attended[rows, :] = scale * (inner[rows, :] + times(beside(query[rows, :]), prefix))
-
-
-def own_kernel(turned, dproj, *refs):
-    taken, (product, held, sems) = refs[:PARTS], refs[PARTS:]
+def own_kernel(scale, turned, dproj, back, query, inner, *refs):
+    taken, (product, held, attended, rows_out, states, sems, out_sems) = refs[:PARTS], refs[PARTS:]
     size = taken[0].shape[0]
     loads = [
         pltpu.make_async_copy(part, held.at[index * size : (index + 1) * size, :], sems.at[index])
@@ -236,10 +230,18 @@
     ]
     for load in loads:
         load.start()
+    prefix = doubled(joined(back, 0, states))
+    stores = []
+    for index, rows in enumerate(chunks(query.shape[0])):
+        rows_out[rows, :] = scale * (inner[rows, :] + times(beside(query[rows, :]), prefix))
+        stores.append(
+            pltpu.make_async_copy(rows_out.at[rows, :], attended.at[rows, :], out_sems.at[index])
+        )
+        stores[-1].start()
     for rows in chunks(turned.shape[0]):
         product[rows, :] = mxu(turned[rows, :], dproj[...])
-    for load in loads:
-        load.wait()
+    for copy in loads + stores:
+        copy.wait()
 
 
 def total_kernel(turned, dproj, product, total):
@@ -330,25 +332,24 @@
         states,
     )
     theirs = lax.ppermute(dproj, "core", SWAP)
-    product, held = call(
-        own_kernel,
-        [vmem((half, columns)), (pltpu.VMEM((half, tokens), BF16), VMEM)],
-        [keep, dproj, *taken],
+    product, held, attended = call(
+        functools.partial(own_kernel, scale),
+        [
+            vmem((half, columns)),
+            (pltpu.VMEM((half, tokens), BF16), VMEM),
+            direct((tokens, HD)),
+        ],
+        [keep, dproj, back, query, inner, *taken],
         2 * half * tokens * columns,
         24,
-        [VMEM, VMEM] + [HBM] * PARTS,
-        [pltpu.SemaphoreType.DMA((PARTS,))],
-    )
-    (attended,) = call(
-        functools.partial(attended_kernel, scale),
-        [hbm((tokens, HD))],
-        [back, query, inner],
-        4 * square,
-        24,
-        [VMEM] * 3,
-        states,
-    )
-    product, held, attended = lax.optimization_barrier((product, held, attended))
+        [VMEM] * 5 + [HBM] * PARTS,
+        [
+            pltpu.VMEM((tokens, HD), F32),
+            *states,
+            pltpu.SemaphoreType.DMA((PARTS,)),
+            pltpu.SemaphoreType.DMA((tokens // BLOCK,)),
+        ],
+    )
     (total,) = call(
         total_kernel,
         [vmem((half, columns), BF16)],

time: 112 us -> 112 us (level)
    pallas_call x11 -> x10, Pallas kernels: 17.8 us -> 17.2 us  [call(): pl.pallas_call(body, out_shape=[kind for kind, _ in outs], in_specs=specs...]
where the time goes in v10:
time: 112 us; the launch traced here: 111 us
  blocking collectives  40.6 us (36%)
  starting transfers between devices  35.8 us (32%)
  Pallas kernels  17.2 us (15%)
  waiting for transfers between devices  10.4 us (9%)
  local copies, waits for them, and re-layouts  5.77 us (5%)
    all_to_all x1, blocking collectives, local(): lax.all_to_all(total.reshape(chips, group, columns), 'chip', 0, 0, tiled=...  25.7 us
    pallas_call x10, Pallas kernels, call(): pl.pallas_call(body, out_shape=[kind for kind, _ in outs], in_specs=specs...  17.2 us
    all_to_all x1, blocking collectives, local(): back = lax.all_to_all(sums, RANKS, 0, 0, tiled=True)  14.9 us
    all_to_all x1, starting transfers between devices, local(): mine = lax.all_to_all(copies, 'chip', 0, 0, tiled=True)  13.7 us
    ppermute x4, starting transfers between devices, local(): taken = [lax.ppermute(part, 'core', SWAP) for part in give]  9.1 us
    all_to_all x1, waiting for transfers between devices, local(): pieces = lax.all_to_all(parts, RANKS, 0, 0, tiled=True)  5.89 us
    unnamed x22, local copies, waits for them, and re-layouts  5.77 us
    all_to_all x1, starting transfers between devices, local(): pieces = lax.all_to_all(parts, RANKS, 0, 0, tiled=True)  5.73 us
  transfers between devices with their start and end apart: 8, of which 4 were waited for; matrix products, arithmetic and copies ran while one was open for 0% of the time, Pallas kernels for 10%

profile of v10, /device:TPU:1, one launch (start us, length us, event | category | flops | bytes accessed | tf_op | source)
XLA Modules:
  0.0 110.5 jit_solution(13896047598729714733)
XLA Ops:
  0.6 0.7 copy-done.6
  1.4 0.9 shard_map.50
  2.3 13.7 %all-to-all-start = ((bf16[32,32,384]{2,1,0:T(8,128)(2,1)}), bf16[32,32,384]{2,1,0:T(8,128)(2,1)S(1)}, u32[]{:S(2)}, u32[]{:S(2)}) async-start(bf16[32,32,384]{2,1,0:T(8,128)(2,1)} %shard_map.50), calls=%async_computation | async-start | bytes 1572864 | tf_op jit(solution)/shard_map/all_to_all | solution.py:276
  16.0 0.0 copy-start.7
  16.0 2.2 %copy-done.7 = bf16[1024,2048]{1,0:T(8,128)(2,1)S(1)} copy-done((bf16[1024,2048]{1,0:T(8,128)(2,1)S(1)}, bf16[1024,2048]{1,0:T(8,128)(2,1)}, u32[]{:S(2)}) %copy-start.7) | copy-done | bytes 4194328
  18.2 4.1 %shard_map.51 = (bf16[1024,1024]{1,0:T(8,128)(2,1)S(1)}, bf16[1024,1024]{1,0:T(8,128)(2,1)}, bf16[1024,1024]{1,0:T(8,128)(2,1)}, bf16[256,1024]{1,0:T(8,128)(2,1...) custom-call(s32[1]{0:T(128)} %bitcast.core, bf16[1024,2048]{1,0:T(8,128)(2,1)S(1)} %copy-done.7), custom_call_target="tpu_custom_call" | custom-call | flops 2147483648 | bytes 4194308 | tf_op jit(solution)/shard_map/pallas_call | solution.py:90
  22.3 2.9 %collective-permute-start = (bf16[256,1024]{1,0:T(8,128)(2,1)}, bf16[256,1024]{1,0:T(8,128)(2,1)S(1)}, u32[]{:S(2)}, u32[]{:S(2)}) collective-permute-start(bf16[256,1024]{1,0:T(8,128)(2,1)} %get-tuple-element.30), channel_id=1, source_target_pairs={{0,8},{8,0},{1,9},{9,1},{2,10},{10,2},{3,11},{11,3},{4,12},{12,4},... | collective-permute-start | bytes 1572872 | tf_op jit(solution)/shard_map/ppermute | solution.py:290
  25.2 1.9 %collective-permute-start.1 = (bf16[256,1024]{1,0:T(8,128)(2,1)}, bf16[256,1024]{1,0:T(8,128)(2,1)S(1)}, u32[]{:S(2)}, u32[]{:S(2)}) collective-permute-start(bf16[256,1024]{1,0:T(8,128)(2,1)} %get-tuple-element.31), channel_id=1, source_target_pairs={{0,8},{8,0},{1,9},{9,1},{2,10},{10,2},{3,11},{11,3},{4,12},{12,4},... | collective-permute-start | bytes 1572872 | tf_op jit(solution)/shard_map/ppermute | solution.py:290
  27.1 2.4 %collective-permute-start.2 = (bf16[256,1024]{1,0:T(8,128)(2,1)}, bf16[256,1024]{1,0:T(8,128)(2,1)S(1)}, u32[]{:S(2)}, u32[]{:S(2)}) collective-permute-start(bf16[256,1024]{1,0:T(8,128)(2,1)} %get-tuple-element.32), channel_id=1, source_target_pairs={{0,8},{8,0},{1,9},{9,1},{2,10},{10,2},{3,11},{11,3},{4,12},{12,4},... | collective-permute-start | bytes 1572872 | tf_op jit(solution)/shard_map/ppermute | solution.py:290
  29.5 1.9 %collective-permute-start.3 = (bf16[256,1024]{1,0:T(8,128)(2,1)}, bf16[256,1024]{1,0:T(8,128)(2,1)}, u32[]{:S(2)}, u32[]{:S(2)}) collective-permute-start(bf16[256,1024]{1,0:T(8,128)(2,1)} %get-tuple-element.33), channel_id=1, source_target_pairs={{0,8},{8,0},{1,9},{9,1},{2,10},{10,2},{3,11},{11,3},{4,12},{12,4},... | collective-permute-start | bytes 1572872 | tf_op jit(solution)/shard_map/ppermute | solution.py:290
  31.5 0.8 copy-done.8
  32.3 0.2 copy-done.9
  32.5 0.8 copy-done.10
  33.3 0.4 collective-permute-done.3.refs_3_
  33.7 3.4 %all-to-all-done.mine = bf16[32,32,384]{2,1,0:T(8,128)(2,1)S(1)} async-done(((bf16[32,32,384]{2,1,0:T(8,128)(2,1)}), bf16[32,32,384]{2,1,0:T(8,128)(2,1)S(1)}, u32[]{:S(2)}, u32[]{:S(2)}) %all-to-all-start) | async-done | bytes 786464 | tf_op jit(solution)/shard_map/all_to_all | solution.py:276
  37.1 5.0 %collective-permute-start.4 = (bf16[32,32,384]{2,1,0:T(8,128)(2,1)S(1)}, bf16[32,32,384]{2,1,0:T(8,128)(2,1)S(1)}, u32[]{:S(2)}, u32[]{:S(2)}) collective-permute-start(bf16[32,32,384]{2,1,0:T(8,128)(2,1)S(1)} %all-to-all-done.mine), channel_id=1, source_target_pairs={{0,8},{8,0},{1,9},{9,1},{2,10},{10,2},{3,11},{11,3},{4,12},{12,4},... | collective-permute-start | bytes 2359304 | tf_op jit(solution)/shard_map/ppermute | solution.py:292
  42.1 1.2 %shard_map.52.partial = f32[1024,384]{1,0:T(8,128)S(1)} custom-call(bf16[1024,1024]{1,0:T(8,128)(2,1)S(1)} %get-tuple-element.37.near, bf16[32,32,384]{2,1,0:T(8,128)(2,1)S(1)} %all-to-all-done.mine), custom_call_target="tpu_custom_call" | custom-call | flops 805306368 | bytes 2883584 | tf_op jit(solution)/shard_map/pallas_call | solution.py:90
  43.3 0.6 collective-permute-done.4.other
  44.0 2.6 %shard_map.53 = (f32[1024,128]{1,0:T(8,128)}, f32[1024,256]{1,0:T(8,128)S(1)}, f32[64,4,128]{2,1,0:T(4,128)}) custom-call(bf16[1024,1024]{1,0:T(8,128)(2,1)S(1)} %copy-done.1, bf16[32,32,384]{2,1,0:T(8,128)(2,1)S(1)} %collective-permute-done.4.other, f32[1024,384]{1,0:T(8,128)S(1)} %shard_map.52.partial, f32[1024,128]{1,0:T(8,128)S(1)} %copy-done.2), custom_call_target="tpu_custom_call" | custom-call | flops 1073741824 | bytes 4980736 | tf_op jit(solution)/shard_map/pallas_call | solution.py:90
  46.6 5.7 %all-to-all-start.1 = ((f32[64,4,128]{2,1,0:T(4,128)}), f32[64,4,128]{2,1,0:T(4,128)S(1)}, u32[]{:S(2)}, u32[]{:S(2)}) async-start(f32[64,4,128]{2,1,0:T(4,128)} %get-tuple-element.38), calls=%async_computation.1 | async-start | bytes 262144 | tf_op jit(solution)/shard_map/all_to_all | solution.py:310
  52.3 0.0 copy-start.3
  52.4 1.0 copy-done.3
  53.4 3.5 %shard_map.54 = (f32[1024,384]{1,0:T(8,128)S(1)}, f32[1024,128]{1,0:T(8,128)}) custom-call(f32[1024,128]{1,0:T(8,128)S(1)} %copy-done.3, f32[1024,256]{1,0:T(8,128)S(1)} %get-tuple-element.40.kv, f32[1024,128]{1,0:T(8,128)S(1)} %copy-done.2), custom_call_target="tpu_custom_call" | custom-call | flops 1509949440 | bytes 2097152 | tf_op jit(solution)/shard_map/pallas_call | solution.py:90
  56.9 5.9 %all-to-all-done.1.pieces = f32[64,4,128]{2,1,0:T(4,128)S(1)} async-done(((f32[64,4,128]{2,1,0:T(4,128)}), f32[64,4,128]{2,1,0:T(4,128)S(1)}, u32[]{:S(2)}, u32[]{:S(2)}) %all-to-all-start.1) | async-done | bytes 131104 | tf_op jit(solution)/shard_map/all_to_all | solution.py:310
  62.8 0.1 shard_map.55
  62.9 14.9 %all_to_all.20.back = f32[64,4,128]{2,1,0:T(4,128)S(1)} all-to-all(f32[64,4,128]{2,1,0:T(4,128)S(1)} %shard_map.55), channel_id=1, replica_groups=mesh['chip'=32,'core'=2,'head'=8] {'core','chip'}, dimensions={0} | all-to-all | bytes 262144 | tf_op jit(solution)/shard_map/all_to_all | solution.py:323
  77.9 0.7 shard_map.56.dproj
  78.5 2.2 %collective-permute-start.5 = (bf16[1024,384]{1,0:T(8,128)(2,1)S(1)}, bf16[1024,384]{1,0:T(8,128)(2,1)S(1)}, u32[]{:S(2)}, u32[]{:S(2)}) collective-permute-start(bf16[1024,384]{1,0:T(8,128)(2,1)S(1)} %shard_map.56.dproj), channel_id=1, source_target_pairs={{0,8},{8,0},{1,9},{9,1},{2,10},{10,2},{3,11},{11,3},{4,12},{12,4},... | collective-permute-start | bytes 2359304 | tf_op jit(solution)/shard_map/ppermute | solution.py:334
  80.8 2.1 %shard_map.57 = (f32[1024,384]{1,0:T(8,128)S(1)}, bf16[1024,1024]{1,0:T(8,128)(2,1)S(1)}, f32[1024,128]{1,0:T(8,128)}) custom-call(bf16[1024,1024]{1,0:T(8,128)(2,1)S(1)} %copy-done, bf16[1024,384]{1,0:T(8,128)(2,1)S(1)} %shard_map.56.dproj, f32[64,4,128]{2,1,0:T(4,128)S(1)} %all_to_all.20.back, f32[1024,128]{1,0:T(8,128)S(1)} %copy-done.4, ...), custom_call_target="tpu_custom_call" | custom-call | flops 805306368 | bytes 6160384 | tf_op jit(solution)/shard_map/pallas_call | solution.py:90
  82.9 1.3 %shard_map.58 = bf16[1024,384]{1,0:T(8,128)(2,1)S(1)} custom-call(bf16[1024,1024]{1,0:T(8,128)(2,1)S(1)} %get-tuple-element.50.turned, bf16[1024,384]{1,0:T(8,128)(2,1)S(1)} %collective-permute-done.5.dproj, f32[1024,384]{1,0:T(8,128)S(1)} %get-tuple-element.51.product), custom_call_target="tpu_custom_call" | custom-call | flops 805306368 | bytes 4456448 | tf_op jit(solution)/shard_map/pallas_call | solution.py:90
  84.2 25.7 %all_to_all.21.landed = bf16[32,32,384]{2,1,0:T(8,128)(2,1)S(1)} all-to-all(bf16[32,32,384]{2,1,0:T(8,128)(2,1)S(1)} %bitcast.2), channel_id=1, replica_groups=mesh['chip'=32,'core'=2,'head'=8] {'chip'}, dimensions={0} | all-to-all | bytes 1572864 | tf_op jit(solution)/shard_map/all_to_all | solution.py:361
  109.8 0.7 shard_map.59
  (18 shorter events, 0.0 us)
Async XLA Ops:
  0.6 0.7 copy-start.6
  2.3 34.8 %all-to-all-start = ((bf16[32,32,384]{2,1,0:T(8,128)(2,1)}), bf16[32,32,384]{2,1,0:T(8,128)(2,1)S(1)}, u32[]{:S(2)}, u32[]{:S(2)}) async-start(bf16[32,32,384]{2,1,0:T(8,128)(2,1)} %shard_map.50), calls=%async_computation | async-start | bytes 1572864 | tf_op jit(solution)/shard_map/all_to_all | solution.py:276
  16.0 2.2 %copy-start.7 = (bf16[1024,2048]{1,0:T(8,128)(2,1)S(1)}, bf16[1024,2048]{1,0:T(8,128)(2,1)}, u32[]{:S(2)}) copy-start(bf16[1024,2048]{1,0:T(8,128)(2,1)} %hidden.1) | copy-start | bytes 12582916
  22.3 9.1 %collective-permute-start = (bf16[256,1024]{1,0:T(8,128)(2,1)}, bf16[256,1024]{1,0:T(8,128)(2,1)S(1)}, u32[]{:S(2)}, u32[]{:S(2)}) collective-permute-start(bf16[256,1024]{1,0:T(8,128)(2,1)} %get-tuple-element.30), channel_id=1, source_target_pairs={{0,8},{8,0},{1,9},{9,1},{2,10},{10,2},{3,11},{11,3},{4,12},{12,4},... | collective-permute-start | bytes 1572872 | tf_op jit(solution)/shard_map/ppermute | solution.py:290
  25.2 6.3 %collective-permute-start.1 = (bf16[256,1024]{1,0:T(8,128)(2,1)}, bf16[256,1024]{1,0:T(8,128)(2,1)S(1)}, u32[]{:S(2)}, u32[]{:S(2)}) collective-permute-start(bf16[256,1024]{1,0:T(8,128)(2,1)} %get-tuple-element.31), channel_id=1, source_target_pairs={{0,8},{8,0},{1,9},{9,1},{2,10},{10,2},{3,11},{11,3},{4,12},{12,4},... | collective-permute-start | bytes 1572872 | tf_op jit(solution)/shard_map/ppermute | solution.py:290
  27.1 4.4 %collective-permute-start.2 = (bf16[256,1024]{1,0:T(8,128)(2,1)}, bf16[256,1024]{1,0:T(8,128)(2,1)S(1)}, u32[]{:S(2)}, u32[]{:S(2)}) collective-permute-start(bf16[256,1024]{1,0:T(8,128)(2,1)} %get-tuple-element.32), channel_id=1, source_target_pairs={{0,8},{8,0},{1,9},{9,1},{2,10},{10,2},{3,11},{11,3},{4,12},{12,4},... | collective-permute-start | bytes 1572872 | tf_op jit(solution)/shard_map/ppermute | solution.py:290
  29.5 4.1 %collective-permute-start.3 = (bf16[256,1024]{1,0:T(8,128)(2,1)}, bf16[256,1024]{1,0:T(8,128)(2,1)}, u32[]{:S(2)}, u32[]{:S(2)}) collective-permute-start(bf16[256,1024]{1,0:T(8,128)(2,1)} %get-tuple-element.33), channel_id=1, source_target_pairs={{0,8},{8,0},{1,9},{9,1},{2,10},{10,2},{3,11},{11,3},{4,12},{12,4},... | collective-permute-start | bytes 1572872 | tf_op jit(solution)/shard_map/ppermute | solution.py:290
  31.4 0.8 copy-start.8
  31.5 1.0 copy-start.9
  32.5 0.8 copy-start.10
  37.1 6.9 %copy-start.1 = (bf16[1024,1024]{1,0:T(8,128)(2,1)S(1)}, bf16[1024,1024]{1,0:T(8,128)(2,1)}, u32[]{:S(2)}) copy-start(bf16[1024,1024]{1,0:T(8,128)(2,1)} %get-tuple-element.35.far) | copy-start | bytes 6291460
  37.1 6.9 %copy-start.2 = (f32[1024,128]{1,0:T(8,128)S(1)}, f32[1024,128]{1,0:T(8,128)}, u32[]{:S(2)}) copy-start(f32[1024,128]{1,0:T(8,128)} %cotangent.5) | copy-start | bytes 1572868
  37.1 6.9 %collective-permute-start.4 = (bf16[32,32,384]{2,1,0:T(8,128)(2,1)S(1)}, bf16[32,32,384]{2,1,0:T(8,128)(2,1)S(1)}, u32[]{:S(2)}, u32[]{:S(2)}) collective-permute-start(bf16[32,32,384]{2,1,0:T(8,128)(2,1)S(1)} %all-to-all-done.mine), channel_id=1, source_target_pairs={{0,8},{8,0},{1,9},{9,1},{2,10},{10,2},{3,11},{11,3},{4,12},{12,4},... | collective-permute-start | bytes 2359304 | tf_op jit(solution)/shard_map/ppermute | solution.py:292
  46.6 16.2 %all-to-all-start.1 = ((f32[64,4,128]{2,1,0:T(4,128)}), f32[64,4,128]{2,1,0:T(4,128)S(1)}, u32[]{:S(2)}, u32[]{:S(2)}) async-start(f32[64,4,128]{2,1,0:T(4,128)} %get-tuple-element.38), calls=%async_computation.1 | async-start | bytes 262144 | tf_op jit(solution)/shard_map/all_to_all | solution.py:310
  52.3 1.0 copy-start.3
  77.9 2.9 %copy-start = (bf16[1024,1024]{1,0:T(8,128)(2,1)S(1)}, bf16[1024,1024]{1,0:T(8,128)(2,1)}, u32[]{:S(2)}) copy-start(bf16[1024,1024]{1,0:T(8,128)(2,1)} %get-tuple-element.34.turned) | copy-start | bytes 6291460
  77.9 2.9 %copy-start.4 = (f32[1024,128]{1,0:T(8,128)S(1)}, f32[1024,128]{1,0:T(8,128)}, u32[]{:S(2)}) copy-start(f32[1024,128]{1,0:T(8,128)} %get-tuple-element.39.query) | copy-start | bytes 1572868
  77.9 3.0 %copy-start.5 = (f32[1024,128]{1,0:T(8,128)S(1)}, f32[1024,128]{1,0:T(8,128)}, u32[]{:S(2)}) copy-start(f32[1024,128]{1,0:T(8,128)} %get-tuple-element.44.inner) | copy-start | bytes 1572868
  78.5 4.3 %collective-permute-start.5 = (bf16[1024,384]{1,0:T(8,128)(2,1)S(1)}, bf16[1024,384]{1,0:T(8,128)(2,1)S(1)}, u32[]{:S(2)}, u32[]{:S(2)}) collective-permute-start(bf16[1024,384]{1,0:T(8,128)(2,1)S(1)} %shard_map.56.dproj), channel_id=1, source_target_pairs={{0,8},{8,0},{1,9},{9,1},{2,10},{10,2},{3,11},{11,3},{4,12},{12,4},... | collective-permute-start | bytes 2359304 | tf_op jit(solution)/shard_map/ppermute | solution.py:334
